TPU v7x, 512 devices: a whole 4x8x8 slice. The times are simulated.
512 devices in a mesh: leaf: 16 (over x_lo, z), prow: 8 (over y), pcol: 4 (over x_hi, core).
Axes of the slice: x: 4 (x_hi: 2, x_lo: 2; x = x_hi * 2 + x_lo), y: 8, z: 8, core: 2. Of those that a mesh axis runs over, the one named last changes fastest.
Arguments:
- ancestor_inverse: float32 [6144, 6144], P(('prow', 'pcol'), 'leaf'), as said below
- pattern: int32 [16, 8], P('leaf'), may hold values from 0 to 47, as said below
- child_lower: float32 [16, 1024, 896], P('leaf', ('prow', 'pcol')), may hold values from -0.1875 to 0.1875
- child_diag_inv: float32 [16, 896, 896], P('leaf', ('prow', 'pcol')), as said below
Outputs:
- cross_inverse: float32 [16, 6144, 896], P('leaf', ('prow', 'pcol'))
- diag_inverse: float32 [16, 896, 896], P('leaf', ('prow', 'pcol'))
Inputs may be any that keep to these rules, and one draw needn't show every extreme that they name: `pattern`: each row holds 8 different root block numbers in increasing order. `ancestor_inverse`: symmetric. `child_diag_inv`: symmetric in its last two dimensions.
All inputs are finite; a program needn't handle non-finite values.
Results may differ from a plain program's by a relative error of at most 0.0003.
Values sent between devices are 32-bit elements; how exact they have to be, the bound alone decides.
No kernel may reach another device: no remote copies, remote signals or barrier semaphores. Data moves between devices by JAX's collectives and lax.ppermute only.
A program may use at most 128 MiB of HBM per device.

v0:
```python
import jax
import jax.numpy as jnp
from jax import lax
from jax.sharding import PartitionSpec as P

BLK = 128


highest = lax.Precision.HIGHEST


def locate(pattern_row, first_row, row_count):
    indices = first_row + jnp.arange(row_count, dtype=jnp.int32)
    blocks = indices // BLK
    matches = pattern_row[None, :] == blocks[:, None]
    present = jnp.any(matches, axis=1)
    numbers = jnp.arange(pattern_row.shape[0], dtype=jnp.int32)
    position = jnp.sum(jnp.where(matches, numbers[None, :], 0), axis=1)
    return (position * BLK + indices % BLK, present)


def shards(ancestor_inverse, pattern, child_lower, child_diag_inv):
    pattern_row = pattern[0]
    local_rows = ancestor_inverse.shape[0]
    first_local = lax.axis_index(("prow", "pcol")) * local_rows
    own_index, own_present = locate(pattern_row, first_local, local_rows)
    root_rows = lax.all_gather(ancestor_inverse, "leaf", axis=1, tiled=True)
    lower_piece = lax.all_gather(child_lower[0], ("prow", "pcol"), axis=0, tiled=True)
    piece_rows = lower_piece.shape[0]
    packed = jnp.arange(piece_rows, dtype=jnp.int32)
    root_cols = jnp.take(pattern_row, packed // BLK) * BLK + packed % BLK
    columns = jnp.take(root_rows, root_cols, axis=1)
    partial_value = jnp.dot(
        columns, lower_piece, precision=highest, preferred_element_type=jnp.float32
    )
    inside = own_present & (own_index >= 0) & (own_index < piece_rows)
    picked = jnp.take(lower_piece, jnp.clip(own_index, 0, piece_rows - 1), axis=0)
    gathered_own = jnp.where(inside[:, None], picked, 0.0)
    update = lax.psum_scatter(
        lax.dot_general(
            gathered_own,
            partial_value,
            (((0,), (0,)), ((), ())),
            precision=highest,
            preferred_element_type=jnp.float32,
        ),
        ("prow", "pcol"),
        scatter_dimension=0,
        tiled=True,
    )
    diagonal = child_diag_inv[0] + update
    return ((-partial_value)[None], diagonal[None])


def solution(mesh):
    return jax.shard_map(
        shards,
        mesh=mesh,
        in_specs=(
            P(("prow", "pcol"), "leaf"),
            P("leaf", None),
            P("leaf", ("prow", "pcol"), None),
            P("leaf", ("prow", "pcol"), None),
        ),
        out_specs=(P("leaf", ("prow", "pcol"), None), P("leaf", ("prow", "pcol"), None)),
        check_vma=False,
    )
```

profile of v0, /device:TPU:20, one launch (start us, length us, event | category | flops | bytes accessed | tf_op | source)
XLA Modules:
  0.0 315.3 jit_solution(10489277180449407038)
XLA Ops:
  7.2 0.0 all-gather.6.cloned.1.call-start
  7.2 0.7 all-gather.6.cloned.1.call-update
  7.9 0.0 all-gather.4.cloned.1.call-start
  7.9 1.9 copy.12
  9.8 0.0 all-gather.4.cloned.1.call-update
  9.9 1.3 dynamic-slice.4
  11.8 0.7 fusion.13
  12.6 1.6 fusion.35
  14.2 4.2 %compare_select_fusion.2 = s32[1024,1]{0,1:T(1,128)S(1)} fusion(s32[]{:T(128)} %bitcast.1, s32[]{:T(128)} %bitcast.2, s32[]{:T(128)} %bitcast.3, s32[]{:T(128)} %bitcast.4, s32[]{:T(128)} %bitcast.5, s32[]{:T(128)} %bitcast.7, s32[]{:T(128)} %bitcast.6), kind=kLoop, calls=%fused_computation.19 | loop fusion | flops 23552 | bytes 4124 | tf_op jit(solution)/shard_map/jit(_take)/gather | solution.py:31
  18.4 0.7 compare_reduce_fusion.1
  19.2 0.7 compare_and_fusion
  19.9 82.3 %all-gather.6.cloned.1.call-done = f32[1,1024,896]{2,1,0:T(8,128)} async-done(((f32[1,32,896]{2,1,0:T(8,128)}), f32[1,1024,896]{2,1,0:T(8,128)}) %all-gather.6.cloned.1.call-update) | async-done | bytes 3670032 | tf_op jit(solution)/shard_map/all_gather | solution.py:28
  102.2 4.1 %gather_fusion.1 = f32[192,896]{1,0:T(8,128)} fusion(f32[1024,896]{1,0:T(8,128)} %bitcast.27, s32[1024]{0:T(1024)S(1)} %pad_clamp_fusion), kind=kCustom, calls=%fused_computation.1 | custom fusion | bytes 1377024 | tf_op jit(solution)/shard_map/jit(_take)/gather | solution.py:37
  106.3 85.4 %all-gather.4.cloned.1.call-done = f32[192,6144]{0,1:T(8,128)} async-done(((f32[192,384]{0,1:T(8,128)}), f32[192,6144]{0,1:T(8,128)}) %all-gather.4.cloned.1.call-update) | async-done | bytes 4718608 | tf_op jit(solution)/shard_map/all_gather | solution.py:27
  191.7 6.2 %gather_fusion = f32[1024,192]{1,0:T(8,128)S(1)} fusion(f32[192,6144]{0,1:T(8,128)} %all-gather.4.cloned.1.call-done, s32[1024]{0:T(1024)S(1)} %broadcast_clamp_fusion), kind=kCustom, calls=%fused_computation | custom fusion | bytes 1576960 | tf_op jit(solution)/shard_map/jit(_take)/gather | solution.py:32
  197.9 5.2 %fusion.1 = f32[192,896]{1,0:T(8,128)S(1)} fusion(f32[1024,192]{1,0:T(8,128)S(1)} %gather_fusion, pred[1024]{0:T(1024)(128)(4,1)S(1)} %get-tuple-element.12, f32[1,1024,896]{2,1,0:T(8,128)} %all-gather.6.cloned.1.call-done), kind=kOutput, calls=%fused_computation.2 | convolution fusion | flops 2114125824 | bytes 5145600 | tf_op jit(solution)/shard_map/dot_general | solution.py:33
  203.2 0.0 copy-start
  203.2 0.8 copy-done
  204.0 3.2 %fusion.3 = f32[896,896]{1,0:T(8,128)S(1)} fusion(f32[192,896]{1,0:T(8,128)S(1)} %fusion.1, f32[192,896]{1,0:T(8,128)S(1)} %copy-done.1, pred[192]{0:T(512)(128)(4,1)S(1)} %compare_and_fusion.1, pred[192]{0:T(512)(128)(4,1)S(1)} %get-tuple-element.10), kind=kOutput, calls=%fused_computation.4 | convolution fusion | flops 1850032128 | bytes 4587904 | tf_op jit(solution)/shard_map/dot_general | solution.py:40
  207.2 0.0 copy-start.2
  207.2 70.2 %fusion = f32[32,896]{1,0:T(8,128)S(1)} fusion(f32[896,896]{1,0:T(8,128)S(1)} %fusion.3), kind=kCustom, calls=%all-reduce-scatter | all-reduce-scatter fusion | flops 917505 | bytes 3328000
  277.5 1.9 collective-permute-start
  279.4 9.7 %collective-permute-start.1 = (f32[32,896]{1,0:T(8,128)S(1)}, f32[32,896]{1,0:T(8,128)S(1)}, u32[]{:S(2)}, u32[]{:S(2)}) collective-permute-start(f32[32,896]{1,0:T(8,128)S(1)} %fusion), channel_id=1, source_target_pairs={{0,2},{1,3},{2,4},{3,5},{4,6},{5,7},{6,8},{7,9},{8,10},{9,11},{10,... | collective-permute-start | bytes 344072
  289.1 11.1 %collective-permute-start.2 = (f32[32,896]{1,0:T(8,128)S(1)}, f32[32,896]{1,0:T(8,128)S(1)}, u32[]{:S(2)}, u32[]{:S(2)}) collective-permute-start(f32[32,896]{1,0:T(8,128)S(1)} %fusion), channel_id=1, source_target_pairs={{0,3},{1,4},{2,5},{3,6},{4,7},{5,8},{6,9},{7,10},{8,11},{9,12},{10... | collective-permute-start | bytes 344072
  300.3 1.9 collective-permute-start.3
  302.2 2.0 negate_bitcast_fusion
  304.2 2.8 collective-permute-done.3
  307.0 0.0 collective-permute-done
  307.0 0.0 collective-permute-done.1
  307.0 0.0 collective-permute-done.2
  307.0 0.7 concatenate
  307.7 0.7 copy.13
  (14 shorter events, 0.2 us)
Async XLA Ops:
  7.2 95.0 %all-gather.6.cloned.1.call-start = ((), (), s32[]{:S(2)}) async-start(), calls=%async_computation.1 | async-start | bytes 3784704 | tf_op jit(solution)/shard_map/all_gather | solution.py:28
  7.9 183.8 %all-gather.4.cloned.1.call-start = ((), (), s32[]{:S(2)}) async-start(), calls=%async_computation | async-start | bytes 6684672 | tf_op jit(solution)/shard_map/all_gather | solution.py:27
  197.9 6.1 %copy-start.1 = (f32[192,896]{1,0:T(8,128)S(1)}, f32[192,896]{1,0:T(8,128)}, u32[]{:S(2)}) copy-start(f32[192,896]{1,0:T(8,128)} %gather_fusion.1) | copy-start | bytes 2064388
  203.2 0.8 copy-start
  207.2 100.5 %copy-start.2 = (f32[1,28,896]{2,0,1:T(1,128)S(1)}, f32[1,28,896]{2,0,1:T(1,128)}, u32[]{:S(2)}) copy-start(f32[1,28,896]{2,0,1:T(1,128)} %param.7) | copy-start | bytes 301060
  277.5 29.5 %collective-permute-start = (f32[32,896]{1,0:T(8,128)S(1)}, f32[32,896]{1,0:T(8,128)S(1)}, u32[]{:S(2)}, u32[]{:S(2)}) collective-permute-start(f32[32,896]{1,0:T(8,128)S(1)} %fusion), channel_id=1, source_target_pairs={{0,1},{1,2},{2,3},{3,4},{4,5},{5,6},{6,7},{7,8},{8,9},{9,10},{10,1... | collective-permute-start | bytes 344072
  279.4 27.6 %collective-permute-start.1 = (f32[32,896]{1,0:T(8,128)S(1)}, f32[32,896]{1,0:T(8,128)S(1)}, u32[]{:S(2)}, u32[]{:S(2)}) collective-permute-start(f32[32,896]{1,0:T(8,128)S(1)} %fusion), channel_id=1, source_target_pairs={{0,2},{1,3},{2,4},{3,5},{4,6},{5,7},{6,8},{7,9},{8,10},{9,11},{10,... | collective-permute-start | bytes 344072
  289.1 17.8 %collective-permute-start.2 = (f32[32,896]{1,0:T(8,128)S(1)}, f32[32,896]{1,0:T(8,128)S(1)}, u32[]{:S(2)}, u32[]{:S(2)}) collective-permute-start(f32[32,896]{1,0:T(8,128)S(1)} %fusion), channel_id=1, source_target_pairs={{0,3},{1,4},{2,5},{3,6},{4,7},{5,8},{6,9},{7,10},{8,11},{9,12},{10... | collective-permute-start | bytes 344072
  300.3 6.7 %collective-permute-start.3 = (f32[28,896]{1,0:T(8,128)S(1)}, f32[28,896]{1,0:T(8,128)S(1)}, u32[]{:S(2)}, u32[]{:S(2)}) collective-permute-start(f32[28,896]{1,0:T(8,128)S(1)} %slice.22), channel_id=1, source_target_pairs={{0,4},{1,5},{2,6},{3,7},{4,8},{5,9},{6,10},{7,11},{8,12},{9,13},{1... | collective-permute-start | bytes 301064
Sparse Core Ops, SparseCore 0:
  11.3 90.8 all-gather.5
  104.9 86.7 all-gather.3
where the time goes:
time: 316 us; the launch traced here: 315 us
  waiting for transfers between devices  171 us (54%)
  blocking collectives  70.2 us (22%)
  starting transfers between devices  24.8 us (8%)
  local copies, waits for them, and re-layouts  17.4 us (6%)
  between operations  14.9 us (5%)
  other arithmetic  8.5 us (3%)
  matrix products  8.37 us (3%)
    all_gather x1, waiting for transfers between devices, shards(): root_rows = lax.all_gather(ancestor_inverse, 'leaf', axis=1, tiled=True)  85.4 us
    all_gather x1, waiting for transfers between devices, shards(): lax.all_gather(child_lower[0], ('prow', 'pcol'), axis=0, tiled=True)  82.3 us
    unnamed x1, blocking collectives  70.2 us
    unnamed x4, starting transfers between devices  24.7 us
  transfers between devices with their start and end apart: 6, of which 3 were waited for; matrix products, arithmetic and copies ran while one was open for 5% of the time, Pallas kernels for 0%

commit v1 on v0

v1 whole, which is shorter than its diff:
```python
import jax
import jax.numpy as jnp
from jax import lax
from jax.experimental import pallas as pl
from jax.experimental.pallas import tpu as pltpu
from jax.sharding import PartitionSpec as P

BLK = 128
NP = 8
N_LEAF = 16
N_GRID = 32
ROWS = 192
CHUNK = ROWS // N_LEAF
OWN_BLOCKS = 3
S1 = 896
COLS = S1 // N_GRID
LROWS = 32
PAT_ROW = OWN_BLOCKS * CHUNK
PIECE1 = 40
PIECE2 = NP * CHUNK
PIECE3 = 48
HALF_ROW = 32
VMEM_LIMIT = 48 * 1024 * 1024


def in_vmem(count):
    return [pl.BlockSpec(memory_space=pltpu.VMEM)] * count


def split(value):
    high = value.astype(jnp.bfloat16)
    low = (value - high.astype(jnp.float32)).astype(jnp.bfloat16)
    return high, low


def spread_kernel(ancestor, pattern, out):
    row = pattern[...].astype(jnp.float32)
    for leaf in range(N_LEAF):
        for block in range(OWN_BLOCKS):
            out[leaf, block * CHUNK:(block + 1) * CHUNK, :] = ancestor[
                leaf * CHUNK:(leaf + 1) * CHUNK, block * BLK:(block + 1) * BLK
            ]
        out[leaf, PAT_ROW:PIECE1, :] = jnp.zeros((PIECE1 - PAT_ROW, BLK), jnp.float32)
        out[leaf, PAT_ROW:PAT_ROW + 1, 0:NP] = row


def select_kernel(pieces, out, patterns, semaphore):
    copy = pltpu.make_async_copy(pieces.at[:, PAT_ROW:PAT_ROW + 1, :], patterns, semaphore)
    copy.start()
    copy.wait()

    def one_leaf(leaf, carry):
        for block in range(NP):
            number = patterns[leaf, 0, block].astype(jnp.int32)
            owner = number // OWN_BLOCKS
            first = (number - owner * OWN_BLOCKS) * CHUNK
            out[leaf, block * CHUNK:(block + 1) * CHUNK, :] = pieces[owner, pl.ds(first, CHUNK), :]
        return carry

    lax.fori_loop(0, N_LEAF, one_leaf, 0)


def cross_kernel(pieces, own, other, cross, out, lower_high, lower_low, panel, product):
    column = lax.axis_index("pcol")
    core = lax.rem(column, 2)
    side = column // 2
    for source, at_core in ((own, core), (other, 1 - core)):
        for block in range(NP):
            for part, at_side in ((0, side), (1, 1 - side)):
                high, low = split(source[block, part * LROWS:(part + 1) * LROWS, :])
                first = pl.multiple_of(block * BLK + at_side * 64 + at_core * LROWS, LROWS)
                lower_high[pl.ds(first, LROWS), :] = high
                lower_low[pl.ds(first, LROWS), :] = low
    for leaf in range(N_LEAF):
        for block in range(NP):
            panel[leaf * CHUNK:(leaf + 1) * CHUNK, block * BLK:(block + 1) * BLK] = pieces[
                leaf, block * CHUNK:(block + 1) * CHUNK, :
            ]
    panel_high, panel_low = split(panel[...])

    def dot(a, b):
        return jnp.dot(a, b, preferred_element_type=jnp.float32)

    value = dot(panel_high, lower_high[...]) + (
        dot(panel_low, lower_high[...]) + dot(panel_high, lower_low[...])
    )
    product[...] = value
    cross[0, :, :] = -value
    whole = product[pl.ds(pl.multiple_of(core * 64, 64), BLK), :].T
    half = product[pl.ds(pl.multiple_of((1 - core) * BLK, BLK), 64), :].T
    for device in range(N_GRID):
        at = device * COLS
        out[device, 0:COLS, :] = whole[at:at + COLS, :]
        out[device, HALF_ROW:HALF_ROW + COLS // 2, 0:64] = half[at:at + COLS // 2, :]
        out[device, HALF_ROW:HALF_ROW + COLS // 2, 64:128] = half[at + COLS // 2:at + COLS, :]


def diagonal_kernel(pattern, pieces, lower_high, lower_low, child, out, rows):
    lane = lax.broadcasted_iota(jnp.int32, (COLS // 2, BLK), 1)
    for block in range(NP):
        number = pattern[0, block]
        group = number // 3
        place = number - group * 3
        upper = 2 * group
        middle = place == 1
        whole = pieces[upper + place // 2, 0:COLS, :]
        first = pieces[upper, HALF_ROW:HALF_ROW + COLS // 2, :]
        second = pieces[upper + 1, HALF_ROW:HALF_ROW + COLS // 2, :]
        top = jnp.where(lane < 64, first, pltpu.roll(second, 64, 1))
        bottom = jnp.where(lane < 64, pltpu.roll(first, 64, 1), second)
        here = slice(block * BLK, (block + 1) * BLK)
        rows[0:COLS // 2, here] = jnp.where(middle, top, whole[0:COLS // 2, :])
        rows[COLS // 2:COLS, here] = jnp.where(middle, bottom, whole[COLS // 2:COLS, :])
    rows[COLS:, :] = jnp.zeros((32 - COLS, NP * BLK), jnp.float32)
    high, low = split(rows[...])

    def dot(a, b):
        return jnp.dot(a, b, preferred_element_type=jnp.float32)

    update = dot(high, lower_high[...]) + (dot(low, lower_high[...]) + dot(high, lower_low[...]))
    for row in range(COLS):
        out[row, 0:1, :] = child[row, 0:1, :] + update[row:row + 1, :]


def shards(ancestor_inverse, pattern, child_lower, child_diag_inv):
    params = pltpu.CompilerParams(vmem_limit_bytes=VMEM_LIMIT)
    own_rows = child_lower[0]
    pair = jnp.concatenate(
        [own_rows, lax.ppermute(own_rows, "pcol", [(0, 2), (1, 3), (2, 0), (3, 1)])], axis=0
    )
    spread = pl.pallas_call(
        spread_kernel,
        out_shape=jax.ShapeDtypeStruct((N_LEAF, PIECE1, BLK), jnp.float32),
        in_specs=in_vmem(2),
        out_specs=in_vmem(1)[0],
        compiler_params=params,
    )(ancestor_inverse, pattern)
    pair, spread = lax.optimization_barrier((pair, spread))
    lower_own = lax.all_gather(pair, "prow", axis=0, tiled=True)
    spread = lax.all_to_all(spread, "leaf", 0, 0, tiled=True)
    chosen = pl.pallas_call(
        select_kernel,
        out_shape=jax.ShapeDtypeStruct((N_LEAF, PIECE2, BLK), jnp.float32),
        in_specs=in_vmem(1),
        out_specs=in_vmem(1)[0],
        scratch_shapes=[pltpu.SMEM((N_LEAF, 1, BLK), jnp.float32), pltpu.SemaphoreType.DMA(())],
        compiler_params=params,
    )(spread)
    chosen = lax.all_to_all(chosen, "leaf", 0, 0, tiled=True)
    lower_own, chosen = lax.optimization_barrier((lower_own, chosen))
    lower_other = lax.ppermute(lower_own, "pcol", [(0, 1), (1, 0), (2, 3), (3, 2)])
    cross, pieces, lower_high, lower_low = pl.pallas_call(
        cross_kernel,
        out_shape=(
            jax.ShapeDtypeStruct((1, ROWS, S1), jnp.float32),
            jax.ShapeDtypeStruct((N_GRID, PIECE3, BLK), jnp.float32),
            jax.ShapeDtypeStruct((NP * BLK, S1), jnp.bfloat16),
            jax.ShapeDtypeStruct((NP * BLK, S1), jnp.bfloat16),
        ),
        in_specs=in_vmem(3),
        out_specs=tuple(in_vmem(4)),
        scratch_shapes=[
            pltpu.VMEM((ROWS, NP * BLK), jnp.float32),
            pltpu.VMEM((ROWS, S1), jnp.float32),
        ],
        compiler_params=params,
    )(chosen, lower_own.reshape(NP, 64, S1), lower_other.reshape(NP, 64, S1))
    pieces = lax.all_to_all(pieces, ("prow", "pcol"), 0, 0, tiled=True)
    diagonal = pl.pallas_call(
        diagonal_kernel,
        out_shape=jax.ShapeDtypeStruct((COLS, 1, S1), jnp.float32),
        in_specs=[pl.BlockSpec(memory_space=pltpu.SMEM)] + in_vmem(4),
        out_specs=in_vmem(1)[0],
        scratch_shapes=[pltpu.VMEM((32, NP * BLK), jnp.float32)],
        compiler_params=params,
    )(pattern, pieces, lower_high, lower_low, jnp.transpose(child_diag_inv, (1, 0, 2)))
    return cross, jnp.transpose(diagonal, (1, 0, 2))


def solution(mesh):
    return jax.shard_map(
        shards,
        mesh=mesh,
        in_specs=(
            P(("prow", "pcol"), "leaf"),
            P("leaf", None),
            P("leaf", ("prow", "pcol"), None),
            P("leaf", ("prow", "pcol"), None),
        ),
        out_specs=(P("leaf", ("prow", "pcol"), None), P("leaf", ("prow", "pcol"), None)),
        check_vma=False,
    )
```

time: 316 us -> 121 us (0.38)
  the two profiles are of different devices: /device:TPU:20 before, /device:TPU:6 now
where the time goes in v1:
time: 121 us; the launch traced here: 120 us
  blocking collectives  79.8 us (66%)
  between operations  14.1 us (12%)
  Pallas kernels  8.95 us (7%)
  waiting for transfers between devices  7.49 us (6%)
  starting transfers between devices  5.26 us (4%)
  local copies, waits for them, and re-layouts  2.86 us (2%)
  other arithmetic  1.6 us (1%)
    all_to_all x1, blocking collectives, shards(): pieces = lax.all_to_all(pieces, ('prow', 'pcol'), 0, 0, tiled=True)  33.3 us
    all_to_all x1, blocking collectives, shards(): chosen = lax.all_to_all(chosen, 'leaf', 0, 0, tiled=True)  25.2 us
    all_to_all x1, blocking collectives, shards(): spread = lax.all_to_all(spread, 'leaf', 0, 0, tiled=True)  21.2 us
    pallas_call x1, Pallas kernels, shards(): pl.pallas_call(cross_kernel, out_shape=(jax.ShapeDtypeStruct((1, ROWS, S1...  4.91 us
    ppermute x1, waiting for transfers between devices, shards(): lax.ppermute(lower_own, 'pcol', [(0, 1), (1, 0), (2, 3), (3, 2)])  3.96 us
    ppermute x1, waiting for transfers between devices, shards(): lax.ppermute(own_rows, 'pcol', [(0, 2), (1, 3), (2, 0), (3, 1)])  3.52 us
    ppermute x1, starting transfers between devices, shards(): lax.ppermute(own_rows, 'pcol', [(0, 2), (1, 3), (2, 0), (3, 1)])  3.32 us
    unnamed x10, local copies, waits for them, and re-layouts  2.86 us
  transfers between devices with their start and end apart: 3, of which 2 were waited for; matrix products, arithmetic and copies ran while one was open for 0% of the time, Pallas kernels for 2%

profile of v1, /device:TPU:6, one launch (start us, length us, event | category | flops | bytes accessed | tf_op | source)
XLA Modules:
  0.0 120.0 jit_solution(13106939456025520558)
XLA Ops:
  7.2 0.0 all-gather.2.cloned.1.call-start
  7.2 3.3 %collective-permute-start = (f32[32,896]{1,0:T(8,128)}, f32[32,896]{1,0:T(8,128)S(1)}, u32[]{:S(2)}, u32[]{:S(2)}) collective-permute-start(f32[32,896]{1,0:T(8,128)} %bitcast.8), channel_id=1, source_target_pairs={{0,2},{1,3},{2,0},{3,1},{4,6},{5,7},{6,4},{7,5},{8,10},{9,11},{10,... | collective-permute-start | bytes 344072 | tf_op jit(solution)/shard_map/ppermute | solution.py:129
  10.5 0.0 copy-start
  10.5 1.0 copy-done
  11.5 0.0 copy-start.2
  11.5 0.7 copy-done.2
  12.2 3.5 %collective-permute-done = f32[32,896]{1,0:T(8,128)S(1)} collective-permute-done((f32[32,896]{1,0:T(8,128)}, f32[32,896]{1,0:T(8,128)S(1)}, u32[]{:S(2)}, u32[]{:S(2)}) %collective-permute-start) | collective-permute-done | bytes 114720 | tf_op jit(solution)/shard_map/ppermute | solution.py:129
  15.7 1.6 %pad_maximum_fusion = f32[64,896]{1,0:T(8,128)} fusion(f32[32,896]{1,0:T(8,128)S(1)} %collective-permute-done, f32[32,896]{1,0:T(8,128)} %bitcast.9), kind=kLoop, calls=%fused_computation | loop fusion | flops 57344 | bytes 458752 | tf_op jit(solution)/shard_map/concatenate | solution.py:128
  17.3 0.0 all-gather.2.cloned.1.call-update
  17.3 21.2 %all_to_all.15.pieces = f32[16,40,128]{2,1,0:T(8,128)S(1)} all-to-all(f32[16,40,128]{2,1,0:T(8,128)S(1)} %shard_map.59), channel_id=1, replica_groups=mesh['leaf'=16,'prow'=8,'pcol'=4] {'leaf'}, dimensions={0} | all-to-all | bytes 655360 | tf_op jit(solution)/shard_map/all_to_all | solution.py:140
  38.5 1.8 %shard_map.60 = f32[16,96,128]{2,1,0:T(8,128)S(1)} custom-call(f32[16,40,128]{2,1,0:T(8,128)S(1)} %all_to_all.15.pieces), custom_call_target="tpu_custom_call" | custom-call | tf_op jit(solution)/shard_map/pallas_call | solution.py:141
  40.4 25.2 %all_to_all.16.pieces = f32[16,96,128]{2,1,0:T(8,128)S(1)} all-to-all(f32[16,96,128]{2,1,0:T(8,128)S(1)} %shard_map.60), channel_id=1, replica_groups=mesh['leaf'=16,'prow'=8,'pcol'=4] {'leaf'}, dimensions={0} | all-to-all | bytes 1572864 | tf_op jit(solution)/shard_map/all_to_all | solution.py:149
  65.6 0.0 all-gather.2.cloned.1.call-done
  65.6 1.9 %collective-permute-start.1 = (f32[512,896]{1,0:T(8,128)}, f32[512,896]{1,0:T(8,128)S(1)}, u32[]{:S(2)}, u32[]{:S(2)}) collective-permute-start(f32[512,896]{1,0:T(8,128)} %all-gather.2.cloned.1.call-done), channel_id=1, source_target_pairs={{0,1},{1,0},{2,3},{3,2},{4,5},{5,4},{6,7},{7,6},{8,9},{9,8},{10,11... | collective-permute-start | bytes 5505032 | tf_op jit(solution)/shard_map/ppermute | solution.py:151
  67.5 4.0 %collective-permute-done.1 = f32[512,896]{1,0:T(8,128)S(1)} collective-permute-done((f32[512,896]{1,0:T(8,128)}, f32[512,896]{1,0:T(8,128)S(1)}, u32[]{:S(2)}, u32[]{:S(2)}) %collective-permute-start.1) | collective-permute-done | bytes 1835040 | tf_op jit(solution)/shard_map/ppermute | solution.py:151
  71.5 0.0 copy-start.4
  71.5 1.2 %copy-done.4 = f32[512,896]{1,0:T(8,128)} copy-done((f32[512,896]{1,0:T(8,128)}, f32[512,896]{1,0:T(8,128)S(1)}, u32[]{:S(2)}) %copy-start.4) | copy-done | bytes 1835032
  72.7 0.0 copy-start.1
  72.7 0.0 copy-start.3
  72.7 4.9 %shard_map.61 = (f32[1,192,896]{2,1,0:T(8,128)}, f32[32,48,128]{2,1,0:T(8,128)S(1)}, bf16[1024,896]{1,0:T(8,128)(2,1)S(1)}, bf16[1024,896]{1,0:T(8,128)(2,1)S(1)}) custom-call(f32[16,96,128]{2,1,0:T(8,128)S(1)} %all_to_all.16.pieces, f32[8,64,896]{2,1,0:T(8,128)} %bitcast.6, f32[8,64,896]{2,1,0:T(8,128)} %bitcast.7), custom_call_target="tpu_custom_call" | custom-call | tf_op jit(solution)/shard_map/pallas_call | solution.py:152
  77.7 33.3 %all_to_all.17.pieces = f32[32,48,128]{2,1,0:T(8,128)S(1)} all-to-all(f32[32,48,128]{2,1,0:T(8,128)S(1)} %get-tuple-element.15), channel_id=1, replica_groups=mesh['leaf'=16,'prow'=8,'pcol'=4] {'prow','pcol'}, dimensions={0} | all-to-all | bytes 1572864 | tf_op jit(solution)/shard_map/all_to_all | solution.py:168
  111.0 0.0 copy-done.1
  111.0 0.0 copy-done.3
  111.0 2.2 %shard_map.62 = f32[28,1,896]{2,1,0:T(1,128)} custom-call(s32[1,8]{1,0:T(1,128)S(1)} %copy-done.3, f32[32,48,128]{2,1,0:T(8,128)S(1)} %all_to_all.17.pieces, bf16[1024,896]{1,0:T(8,128)(2,1)S(1)} %get-tuple-element.16.lower_high, bf16[1024,896]{1,0:T(8,128)(2,1)S(1)} %get-tuple-element.17.lower_low, f32[28,1,896]{2,1,0:T(1,128)S(1)} %bitcast.5), custom_call_target="tpu_custom_call" | custom-call | tf_op jit(solution)/shard_map/pallas_call | solution.py:169
  (1 shorter events, 0.0 us)
Async XLA Ops:
  7.2 58.5 %all-gather.2.cloned.1.call-start = ((), (), s32[]{:S(2)}) async-start(), calls=%async_computation.3 | async-start | bytes 2064384 | tf_op jit(solution)/shard_map/all_gather | solution.py:139
  7.2 8.5 %collective-permute-start = (f32[32,896]{1,0:T(8,128)}, f32[32,896]{1,0:T(8,128)S(1)}, u32[]{:S(2)}, u32[]{:S(2)}) collective-permute-start(f32[32,896]{1,0:T(8,128)} %bitcast.8), channel_id=1, source_target_pairs={{0,2},{1,3},{2,0},{3,1},{4,6},{5,7},{6,4},{7,5},{8,10},{9,11},{10,... | collective-permute-start | bytes 344072 | tf_op jit(solution)/shard_map/ppermute | solution.py:129
  10.5 1.0 copy-start
  11.5 0.7 copy-start.2
  65.6 5.9 %collective-permute-start.1 = (f32[512,896]{1,0:T(8,128)}, f32[512,896]{1,0:T(8,128)S(1)}, u32[]{:S(2)}, u32[]{:S(2)}) collective-permute-start(f32[512,896]{1,0:T(8,128)} %all-gather.2.cloned.1.call-done), channel_id=1, source_target_pairs={{0,1},{1,0},{2,3},{3,2},{4,5},{5,4},{6,7},{7,6},{8,9},{9,8},{10,11... | collective-permute-start | bytes 5505032 | tf_op jit(solution)/shard_map/ppermute | solution.py:151
  71.5 1.2 %copy-start.4 = (f32[512,896]{1,0:T(8,128)}, f32[512,896]{1,0:T(8,128)S(1)}, u32[]{:S(2)}) copy-start(f32[512,896]{1,0:T(8,128)S(1)} %collective-permute-done.1) | copy-start | bytes 5505028
  72.7 38.3 %copy-start.1 = (f32[1,28,896]{2,0,1:T(1,128)S(1)}, f32[1,28,896]{2,0,1:T(1,128)}, u32[]{:S(2)}) copy-start(f32[1,28,896]{2,0,1:T(1,128)} %param.7) | copy-start | bytes 301060
  72.7 38.3 %copy-start.3 = (s32[1,8]{1,0:T(1,128)S(1)}, s32[1,8]{1,0:T(1,128)}, u32[]{:S(2)}) copy-start(s32[1,8]{1,0:T(1,128)} %pattern.3) | copy-start | bytes 100
Sparse Core Ops, SparseCore 0:
  17.5 47.6 all-gather.1

commit v2 on v1

--- a/solution.py
+++ b/solution.py
@@ -3,6 +3,7 @@
 from jax import lax
 from jax.experimental import pallas as pl
 from jax.experimental.pallas import tpu as pltpu
+from jax.sharding import Mesh
 from jax.sharding import PartitionSpec as P
 
 BLK = 128
@@ -18,9 +19,13 @@
 PAT_ROW = OWN_BLOCKS * CHUNK
 PIECE1 = 40
 PIECE2 = NP * CHUNK
-PIECE3 = 48
-HALF_ROW = 32
-VMEM_LIMIT = 48 * 1024 * 1024
+HALF = COLS // 2
+PIECE3 = COLS + HALF
+VMEM_LIMIT = 16 * 1024 * 1024
+CROSS_LIMIT = 52 * 1024 * 1024
+
+
+GRID = ("prow", "side", "core")
 
 
 def in_vmem(count):
@@ -60,23 +65,30 @@
     lax.fori_loop(0, N_LEAF, one_leaf, 0)
 
 
-def cross_kernel(pieces, own, other, cross, out, lower_high, lower_low, panel, product):
-    column = lax.axis_index("pcol")
-    core = lax.rem(column, 2)
-    side = column // 2
-    for source, at_core in ((own, core), (other, 1 - core)):
-        for block in range(NP):
-            for part, at_side in ((0, side), (1, 1 - side)):
-                high, low = split(source[block, part * LROWS:(part + 1) * LROWS, :])
-                first = pl.multiple_of(block * BLK + at_side * 64 + at_core * LROWS, LROWS)
-                lower_high[pl.ds(first, LROWS), :] = high
-                lower_low[pl.ds(first, LROWS), :] = low
+def cross_kernel(pieces, lower, cross, out, lower_high, lower_low, panel, product, held, semaphores):
+    core = lax.axis_index("core")
+    side = lax.axis_index("side")
+    copies = [
+        pltpu.make_async_copy(lower.at[block], held.at[block], semaphores.at[block])
+        for block in range(NP)
+    ]
+    for copy in copies:
+        copy.start()
     for leaf in range(N_LEAF):
         for block in range(NP):
             panel[leaf * CHUNK:(leaf + 1) * CHUNK, block * BLK:(block + 1) * BLK] = pieces[
                 leaf, block * CHUNK:(block + 1) * CHUNK, :
             ]
     panel_high, panel_low = split(panel[...])
+    for block in range(NP):
+        copies[block].wait()
+        for at_core in range(2):
+            for part, at_side in ((0, side), (1, 1 - side)):
+                row = at_core * 64 + part * LROWS
+                high, low = split(held[block, row:row + LROWS, :])
+                first = pl.multiple_of(block * BLK + at_side * 64 + at_core * LROWS, LROWS)
+                lower_high[pl.ds(first, LROWS), :] = high
+                lower_low[pl.ds(first, LROWS), :] = low
 
     def dot(a, b):
         return jnp.dot(a, b, preferred_element_type=jnp.float32)
@@ -90,27 +102,28 @@
     half = product[pl.ds(pl.multiple_of((1 - core) * BLK, BLK), 64), :].T
     for device in range(N_GRID):
         at = device * COLS
-        out[device, 0:COLS, :] = whole[at:at + COLS, :]
-        out[device, HALF_ROW:HALF_ROW + COLS // 2, 0:64] = half[at:at + COLS // 2, :]
-        out[device, HALF_ROW:HALF_ROW + COLS // 2, 64:128] = half[at + COLS // 2:at + COLS, :]
+        first = device * PIECE3
+        out[first:first + COLS, :] = whole[at:at + COLS, :]
+        out[first + COLS:first + PIECE3, 0:64] = half[at:at + HALF, :]
+        out[first + COLS:first + PIECE3, 64:128] = half[at + HALF:at + COLS, :]
 
 
 def diagonal_kernel(pattern, pieces, lower_high, lower_low, child, out, rows):
-    lane = lax.broadcasted_iota(jnp.int32, (COLS // 2, BLK), 1)
+    lane = lax.broadcasted_iota(jnp.int32, (HALF, BLK), 1)
     for block in range(NP):
         number = pattern[0, block]
         group = number // 3
         place = number - group * 3
         upper = 2 * group
         middle = place == 1
-        whole = pieces[upper + place // 2, 0:COLS, :]
-        first = pieces[upper, HALF_ROW:HALF_ROW + COLS // 2, :]
-        second = pieces[upper + 1, HALF_ROW:HALF_ROW + COLS // 2, :]
+        whole = pieces[pl.ds((upper + place // 2) * PIECE3, COLS), :]
+        first = pieces[pl.ds(upper * PIECE3 + COLS, HALF), :]
+        second = pieces[pl.ds((upper + 1) * PIECE3 + COLS, HALF), :]
         top = jnp.where(lane < 64, first, pltpu.roll(second, 64, 1))
         bottom = jnp.where(lane < 64, pltpu.roll(first, 64, 1), second)
         here = slice(block * BLK, (block + 1) * BLK)
-        rows[0:COLS // 2, here] = jnp.where(middle, top, whole[0:COLS // 2, :])
-        rows[COLS // 2:COLS, here] = jnp.where(middle, bottom, whole[COLS // 2:COLS, :])
+        rows[0:HALF, here] = jnp.where(middle, top, whole[0:HALF, :])
+        rows[HALF:COLS, here] = jnp.where(middle, bottom, whole[HALF:COLS, :])
     rows[COLS:, :] = jnp.zeros((32 - COLS, NP * BLK), jnp.float32)
     high, low = split(rows[...])
 
@@ -126,7 +139,7 @@
     params = pltpu.CompilerParams(vmem_limit_bytes=VMEM_LIMIT)
     own_rows = child_lower[0]
     pair = jnp.concatenate(
-        [own_rows, lax.ppermute(own_rows, "pcol", [(0, 2), (1, 3), (2, 0), (3, 1)])], axis=0
+        [own_rows, lax.ppermute(own_rows, "side", [(0, 1), (1, 0)])], axis=0
     )
     spread = pl.pallas_call(
         spread_kernel,
@@ -136,7 +149,7 @@
         compiler_params=params,
     )(ancestor_inverse, pattern)
     pair, spread = lax.optimization_barrier((pair, spread))
-    lower_own = lax.all_gather(pair, "prow", axis=0, tiled=True)
+    lower = lax.all_gather(pair, ("prow", "core"), axis=0, tiled=True)
     spread = lax.all_to_all(spread, "leaf", 0, 0, tiled=True)
     chosen = pl.pallas_call(
         select_kernel,
@@ -147,25 +160,27 @@
         compiler_params=params,
     )(spread)
     chosen = lax.all_to_all(chosen, "leaf", 0, 0, tiled=True)
-    lower_own, chosen = lax.optimization_barrier((lower_own, chosen))
-    lower_other = lax.ppermute(lower_own, "pcol", [(0, 1), (1, 0), (2, 3), (3, 2)])
     cross, pieces, lower_high, lower_low = pl.pallas_call(
         cross_kernel,
         out_shape=(
             jax.ShapeDtypeStruct((1, ROWS, S1), jnp.float32),
-            jax.ShapeDtypeStruct((N_GRID, PIECE3, BLK), jnp.float32),
+            jax.ShapeDtypeStruct((N_GRID * PIECE3, BLK), jnp.float32),
             jax.ShapeDtypeStruct((NP * BLK, S1), jnp.bfloat16),
             jax.ShapeDtypeStruct((NP * BLK, S1), jnp.bfloat16),
         ),
-        in_specs=in_vmem(3),
+        in_specs=in_vmem(1) + [pl.BlockSpec(memory_space=pltpu.HBM)],
         out_specs=tuple(in_vmem(4)),
         scratch_shapes=[
             pltpu.VMEM((ROWS, NP * BLK), jnp.float32),
             pltpu.VMEM((ROWS, S1), jnp.float32),
+            pltpu.VMEM((NP, BLK, S1), jnp.float32),
+            pltpu.SemaphoreType.DMA((NP,)),
         ],
-        compiler_params=params,
-    )(chosen, lower_own.reshape(NP, 64, S1), lower_other.reshape(NP, 64, S1))
-    pieces = lax.all_to_all(pieces, ("prow", "pcol"), 0, 0, tiled=True)
+        compiler_params=pltpu.CompilerParams(vmem_limit_bytes=CROSS_LIMIT),
+    )(chosen, lower.reshape(NP, BLK, S1))
+    pieces = lax.all_to_all(
+        pieces.reshape(N_GRID, PIECE3, 1, BLK), GRID, 0, 0, tiled=True
+    ).reshape(N_GRID * PIECE3, BLK)
     diagonal = pl.pallas_call(
         diagonal_kernel,
         out_shape=jax.ShapeDtypeStruct((COLS, 1, S1), jnp.float32),
@@ -178,15 +193,19 @@
 
 
 def solution(mesh):
+    shape = mesh.shape
+    parts = Mesh(
+        mesh.devices.reshape(shape["leaf"], shape["prow"], shape["pcol"] // 2, 2), ("leaf",) + GRID
+    )
     return jax.shard_map(
         shards,
-        mesh=mesh,
+        mesh=parts,
         in_specs=(
-            P(("prow", "pcol"), "leaf"),
+            P(GRID, "leaf"),
             P("leaf", None),
-            P("leaf", ("prow", "pcol"), None),
-            P("leaf", ("prow", "pcol"), None),
+            P("leaf", GRID, None),
+            P("leaf", GRID, None),
         ),
-        out_specs=(P("leaf", ("prow", "pcol"), None), P("leaf", ("prow", "pcol"), None)),
+        out_specs=(P("leaf", GRID, None), P("leaf", GRID, None)),
         check_vma=False,
     )

time: 121 us -> 115 us (0.950)
  waiting for transfers between devices: 7.49 us -> 4.07 us
  blocking collectives: 79.8 us -> 77.2 us
  starting transfers between devices: 5.26 us -> 3.35 us
  local copies, waits for them, and re-layouts: 2.86 us -> 4.62 us
    ppermute x2 -> x1, waiting for transfers between devices: 7.48 us -> 3.52 us  [shards(): lax.ppermute(own_rows, 'side', [(0, 1), (1, 0)])]
    all_to_all x1, blocking collectives: 33.3 us -> 30.7 us  [shards(): lax.all_to_all(pieces.reshape(N_GRID, PIECE3, 1, BLK), GRID, 0, 0, tiled=...]
    ppermute x2 -> x1, starting transfers between devices: 5.22 us -> 3.32 us  [shards(): lax.ppermute(own_rows, 'side', [(0, 1), (1, 0)])]
    unnamed x10 -> x12, local copies, waits for them, and re-layouts: 2.86 us -> 4.62 us
  transfers between devices with their start and end apart: 3 -> 2, of which waited for: 2 -> 2; matrix products, arithmetic and copies ran while one was open for 0% -> 0% of each run, Pallas kernels for 2% -> 2%
where the time goes in v2:
time: 115 us; the launch traced here: 114 us
  blocking collectives  77.2 us (67%)
  between operations  14.1 us (12%)
  Pallas kernels  9.21 us (8%)
  local copies, waits for them, and re-layouts  4.62 us (4%)
  waiting for transfers between devices  4.07 us (4%)
  starting transfers between devices  3.35 us (3%)
  other arithmetic  1.6 us (1%)
    all_to_all x1, blocking collectives, shards(): lax.all_to_all(pieces.reshape(N_GRID, PIECE3, 1, BLK), GRID, 0, 0, tiled=...  30.7 us
    all_to_all x1, blocking collectives, shards(): chosen = lax.all_to_all(chosen, 'leaf', 0, 0, tiled=True)  25.2 us
    all_to_all x1, blocking collectives, shards(): spread = lax.all_to_all(spread, 'leaf', 0, 0, tiled=True)  21.2 us
    pallas_call x1, Pallas kernels, shards(): pl.pallas_call(cross_kernel, out_shape=(jax.ShapeDtypeStruct((1, ROWS, S1...  5.16 us
    unnamed x12, local copies, waits for them, and re-layouts  4.62 us
    ppermute x1, waiting for transfers between devices, shards(): lax.ppermute(own_rows, 'side', [(0, 1), (1, 0)])  3.52 us
    ppermute x1, starting transfers between devices, shards(): lax.ppermute(own_rows, 'side', [(0, 1), (1, 0)])  3.32 us
  transfers between devices with their start and end apart: 2, of which 2 were waited for; matrix products, arithmetic and copies ran while one was open for 0% of the time, Pallas kernels for 2%

profile of v2, /device:TPU:6, one launch (start us, length us, event | category | flops | bytes accessed | tf_op | source)
XLA Modules:
  0.0 114.1 jit_solution(6297675677052798747)
XLA Ops:
  7.2 0.0 all-gather.2.cloned.1.call-start
  7.2 3.3 %collective-permute-start = (f32[32,896]{1,0:T(8,128)}, f32[32,896]{1,0:T(8,128)S(1)}, u32[]{:S(2)}, u32[]{:S(2)}) collective-permute-start(f32[32,896]{1,0:T(8,128)} %bitcast.10), channel_id=1, source_target_pairs={{0,2},{2,0},{1,3},{3,1},{4,6},{6,4},{5,7},{7,5},{8,10},{10,8},{9,1... | collective-permute-start | bytes 344072 | tf_op jit(solution)/shard_map/ppermute | solution.py:142
  10.5 0.0 copy-start.2
  10.5 1.0 copy-done.2
  11.5 0.0 copy-start.4
  11.5 0.7 copy-done.4
  12.2 3.5 %collective-permute-done = f32[32,896]{1,0:T(8,128)S(1)} collective-permute-done((f32[32,896]{1,0:T(8,128)}, f32[32,896]{1,0:T(8,128)S(1)}, u32[]{:S(2)}, u32[]{:S(2)}) %collective-permute-start) | collective-permute-done | bytes 114720 | tf_op jit(solution)/shard_map/ppermute | solution.py:142
  15.7 1.6 %pad_maximum_fusion = f32[64,896]{1,0:T(8,128)} fusion(f32[32,896]{1,0:T(8,128)S(1)} %collective-permute-done, f32[32,896]{1,0:T(8,128)} %bitcast.11), kind=kLoop, calls=%fused_computation | loop fusion | flops 57344 | bytes 458752 | tf_op jit(solution)/shard_map/concatenate | solution.py:141
  17.3 0.0 all-gather.2.cloned.1.call-update
  17.3 21.2 %all_to_all.15.pieces = f32[16,40,128]{2,1,0:T(8,128)S(1)} all-to-all(f32[16,40,128]{2,1,0:T(8,128)S(1)} %shard_map.59), channel_id=1, replica_groups=mesh['leaf'=16,'prow'=8,'side'=2,'core'=2] {'leaf'}, dimensions={0} | all-to-all | bytes 655360 | tf_op jit(solution)/shard_map/all_to_all | solution.py:153
  38.5 1.8 %shard_map.60 = f32[16,96,128]{2,1,0:T(8,128)S(1)} custom-call(f32[16,40,128]{2,1,0:T(8,128)S(1)} %all_to_all.15.pieces), custom_call_target="tpu_custom_call" | custom-call | tf_op jit(solution)/shard_map/pallas_call | solution.py:154
  40.4 25.2 %all_to_all.16.pieces = f32[16,96,128]{2,1,0:T(8,128)S(1)} all-to-all(f32[16,96,128]{2,1,0:T(8,128)S(1)} %shard_map.60), channel_id=1, replica_groups=mesh['leaf'=16,'prow'=8,'side'=2,'core'=2] {'leaf'}, dimensions={0} | all-to-all | bytes 1572864 | tf_op jit(solution)/shard_map/all_to_all | solution.py:162
  65.6 0.5 all-gather.2.cloned.1.call-done
  66.2 0.0 copy-start.3
  66.2 0.0 copy-start.5
  66.2 5.2 %shard_map.61 = (f32[1,192,896]{2,1,0:T(8,128)}, f32[1344,128]{1,0:T(8,128)S(1)}, bf16[1024,896]{1,0:T(8,128)(2,1)}, bf16[1024,896]{1,0:T(8,128)(2,1)}) custom-call(f32[16,96,128]{2,1,0:T(8,128)S(1)} %all_to_all.16.pieces, f32[8,128,896]{2,1,0:T(8,128)} %bitcast.9), custom_call_target="tpu_custom_call" | custom-call | tf_op jit(solution)/shard_map/pallas_call | solution.py:163
  71.3 30.7 %all_to_all.17 = f32[32,42,1,128]{3,2,1,0:T(1,128)S(1)} all-to-all(f32[32,42,1,128]{3,2,1,0:T(1,128)S(1)} %bitcast.7), channel_id=1, replica_groups=mesh['leaf'=16,'prow'=8,'side'=2,'core'=2] {'prow','side','core'}, dimensions={0} | all-to-all | bytes 1376256 | tf_op jit(solution)/shard_map/all_to_all | solution.py:181
  102.0 0.0 copy-done.3
  102.0 0.0 copy-done.5
  102.0 0.0 copy-start
  102.0 1.5 %copy-done = bf16[1024,896]{1,0:T(8,128)(2,1)S(1)} copy-done((bf16[1024,896]{1,0:T(8,128)(2,1)S(1)}, bf16[1024,896]{1,0:T(8,128)(2,1)}, u32[]{:S(2)}) %copy-start) | copy-done | bytes 1835032
  103.5 0.0 copy-start.1
  103.5 1.5 %copy-done.1 = bf16[1024,896]{1,0:T(8,128)(2,1)S(1)} copy-done((bf16[1024,896]{1,0:T(8,128)(2,1)S(1)}, bf16[1024,896]{1,0:T(8,128)(2,1)}, u32[]{:S(2)}) %copy-start.1) | copy-done | bytes 1835032
  105.0 2.2 %shard_map.62 = f32[28,1,896]{2,1,0:T(1,128)} custom-call(s32[1,8]{1,0:T(1,128)S(1)} %copy-done.5, f32[1344,128]{1,0:T(8,128)S(1)} %bitcast.6, bf16[1024,896]{1,0:T(8,128)(2,1)S(1)} %copy-done, bf16[1024,896]{1,0:T(8,128)(2,1)S(1)} %copy-done.1, f32[28,1,896]{2,1,0:T(1,128)S(1)} %bitcast.8), custom_call_target="tpu_custom_call" | custom-call | tf_op jit(solution)/shard_map/pallas_call | solution.py:184
  (1 shorter events, 0.0 us)
Async XLA Ops:
  7.2 59.0 %all-gather.2.cloned.1.call-start = ((), (), s32[]{:S(2)}) async-start(), calls=%async_computation.3 | async-start | bytes 3899392 | tf_op jit(solution)/shard_map/all_gather | solution.py:152
  7.2 8.5 %collective-permute-start = (f32[32,896]{1,0:T(8,128)}, f32[32,896]{1,0:T(8,128)S(1)}, u32[]{:S(2)}, u32[]{:S(2)}) collective-permute-start(f32[32,896]{1,0:T(8,128)} %bitcast.10), channel_id=1, source_target_pairs={{0,2},{2,0},{1,3},{3,1},{4,6},{6,4},{5,7},{7,5},{8,10},{10,8},{9,1... | collective-permute-start | bytes 344072 | tf_op jit(solution)/shard_map/ppermute | solution.py:142
  10.5 1.0 copy-start.2
  11.5 0.7 copy-start.4
  66.2 35.9 %copy-start.3 = (f32[1,28,896]{2,0,1:T(1,128)S(1)}, f32[1,28,896]{2,0,1:T(1,128)}, u32[]{:S(2)}) copy-start(f32[1,28,896]{2,0,1:T(1,128)} %param.7) | copy-start | bytes 301060
  66.2 35.9 %copy-start.5 = (s32[1,8]{1,0:T(1,128)S(1)}, s32[1,8]{1,0:T(1,128)}, u32[]{:S(2)}) copy-start(s32[1,8]{1,0:T(1,128)} %pattern.3) | copy-start | bytes 100
  102.0 1.5 %copy-start = (bf16[1024,896]{1,0:T(8,128)(2,1)S(1)}, bf16[1024,896]{1,0:T(8,128)(2,1)}, u32[]{:S(2)}) copy-start(bf16[1024,896]{1,0:T(8,128)(2,1)} %get-tuple-element.12.lower_high) | copy-start | bytes 5505028
  103.5 1.5 %copy-start.1 = (bf16[1024,896]{1,0:T(8,128)(2,1)S(1)}, bf16[1024,896]{1,0:T(8,128)(2,1)}, u32[]{:S(2)}) copy-start(bf16[1024,896]{1,0:T(8,128)(2,1)} %get-tuple-element.13.lower_low) | copy-start | bytes 5505028
Sparse Core Ops, SparseCore 0:
  17.5 48.6 all-gather.1

commit v3 on v2

--- a/solution.py
+++ b/solution.py
@@ -22,7 +22,7 @@
 HALF = COLS // 2
 PIECE3 = COLS + HALF
 VMEM_LIMIT = 16 * 1024 * 1024
-CROSS_LIMIT = 52 * 1024 * 1024
+CROSS_LIMIT = 48 * 1024 * 1024
 
 
 GRID = ("prow", "side", "core")
@@ -38,7 +38,8 @@
     return high, low
 
 
-def spread_kernel(ancestor, pattern, out):
+def spread_kernel(ancestor, pattern, lower, out, kept):
+    kept[...] = lower[...]
     row = pattern[...].astype(jnp.float32)
     for leaf in range(N_LEAF):
         for block in range(OWN_BLOCKS):
@@ -49,23 +50,38 @@
         out[leaf, PAT_ROW:PAT_ROW + 1, 0:NP] = row
 
 
+def pair_kernel(own, received, out, semaphores):
+    first = pltpu.make_async_copy(own, out.at[0:LROWS, :], semaphores.at[0])
+    second = pltpu.make_async_copy(received, out.at[LROWS:2 * LROWS, :], semaphores.at[1])
+    first.start()
+    second.start()
+    first.wait()
+    second.wait()
+
+
 def select_kernel(pieces, out, patterns, semaphore):
     copy = pltpu.make_async_copy(pieces.at[:, PAT_ROW:PAT_ROW + 1, :], patterns, semaphore)
     copy.start()
     copy.wait()
 
-    def one_leaf(leaf, carry):
+    for leaf in range(N_LEAF):
         for block in range(NP):
             number = patterns[leaf, 0, block].astype(jnp.int32)
             owner = number // OWN_BLOCKS
             first = (number - owner * OWN_BLOCKS) * CHUNK
             out[leaf, block * CHUNK:(block + 1) * CHUNK, :] = pieces[owner, pl.ds(first, CHUNK), :]
-        return carry
-
-    lax.fori_loop(0, N_LEAF, one_leaf, 0)
-
-
-def cross_kernel(pieces, lower, cross, out, lower_high, lower_low, panel, product, held, semaphores):
+
+
+def panel_kernel(pieces, high, low, panel):
+    for leaf in range(N_LEAF):
+        for block in range(NP):
+            panel[leaf * CHUNK:(leaf + 1) * CHUNK, block * BLK:(block + 1) * BLK] = pieces[
+                leaf, block * CHUNK:(block + 1) * CHUNK, :
+            ]
+    high[...], low[...] = split(panel[...])
+
+
+def cross_kernel(panel_high, panel_low, lower, cross, out, lower_high, lower_low, product, held, semaphores):
     core = lax.axis_index("core")
     side = lax.axis_index("side")
     copies = [
@@ -74,12 +90,6 @@
     ]
     for copy in copies:
         copy.start()
-    for leaf in range(N_LEAF):
-        for block in range(NP):
-            panel[leaf * CHUNK:(leaf + 1) * CHUNK, block * BLK:(block + 1) * BLK] = pieces[
-                leaf, block * CHUNK:(block + 1) * CHUNK, :
-            ]
-    panel_high, panel_low = split(panel[...])
     for block in range(NP):
         copies[block].wait()
         for at_core in range(2):
@@ -93,8 +103,8 @@
     def dot(a, b):
         return jnp.dot(a, b, preferred_element_type=jnp.float32)
 
-    value = dot(panel_high, lower_high[...]) + (
-        dot(panel_low, lower_high[...]) + dot(panel_high, lower_low[...])
+    value = dot(panel_high[...], lower_high[...]) + (
+        dot(panel_low[...], lower_high[...]) + dot(panel_high[...], lower_low[...])
     )
     product[...] = value
     cross[0, :, :] = -value
@@ -138,16 +148,26 @@
 def shards(ancestor_inverse, pattern, child_lower, child_diag_inv):
     params = pltpu.CompilerParams(vmem_limit_bytes=VMEM_LIMIT)
     own_rows = child_lower[0]
-    pair = jnp.concatenate(
-        [own_rows, lax.ppermute(own_rows, "side", [(0, 1), (1, 0)])], axis=0
-    )
-    spread = pl.pallas_call(
+    received = lax.ppermute(own_rows, "side", [(0, 1), (1, 0)])
+    spread, kept = pl.pallas_call(
         spread_kernel,
-        out_shape=jax.ShapeDtypeStruct((N_LEAF, PIECE1, BLK), jnp.float32),
-        in_specs=in_vmem(2),
-        out_specs=in_vmem(1)[0],
-        compiler_params=params,
-    )(ancestor_inverse, pattern)
+        out_shape=(
+            jax.ShapeDtypeStruct((N_LEAF, PIECE1, BLK), jnp.float32),
+            jax.ShapeDtypeStruct((LROWS, S1), jnp.float32),
+        ),
+        in_specs=in_vmem(3),
+        out_specs=tuple(in_vmem(2)),
+        compiler_params=params,
+    )(ancestor_inverse, pattern, own_rows)
+    spread, received = lax.optimization_barrier((spread, received))
+    pair = pl.pallas_call(
+        pair_kernel,
+        out_shape=jax.ShapeDtypeStruct((2 * LROWS, S1), jnp.float32),
+        in_specs=[pl.BlockSpec(memory_space=pl.ANY)] * 2,
+        out_specs=pl.BlockSpec(memory_space=pltpu.HBM),
+        scratch_shapes=[pltpu.SemaphoreType.DMA((2,))],
+        compiler_params=params,
+    )(kept, received)
     pair, spread = lax.optimization_barrier((pair, spread))
     lower = lax.all_gather(pair, ("prow", "core"), axis=0, tiled=True)
     spread = lax.all_to_all(spread, "leaf", 0, 0, tiled=True)
@@ -160,6 +180,14 @@
         compiler_params=params,
     )(spread)
     chosen = lax.all_to_all(chosen, "leaf", 0, 0, tiled=True)
+    panel_high, panel_low = pl.pallas_call(
+        panel_kernel,
+        out_shape=(jax.ShapeDtypeStruct((ROWS, NP * BLK), jnp.bfloat16),) * 2,
+        in_specs=in_vmem(1),
+        out_specs=tuple(in_vmem(2)),
+        scratch_shapes=[pltpu.VMEM((ROWS, NP * BLK), jnp.float32)],
+        compiler_params=params,
+    )(chosen)
     cross, pieces, lower_high, lower_low = pl.pallas_call(
         cross_kernel,
         out_shape=(
@@ -168,16 +196,15 @@
             jax.ShapeDtypeStruct((NP * BLK, S1), jnp.bfloat16),
             jax.ShapeDtypeStruct((NP * BLK, S1), jnp.bfloat16),
         ),
-        in_specs=in_vmem(1) + [pl.BlockSpec(memory_space=pltpu.HBM)],
+        in_specs=in_vmem(2) + [pl.BlockSpec(memory_space=pltpu.HBM)],
         out_specs=tuple(in_vmem(4)),
         scratch_shapes=[
-            pltpu.VMEM((ROWS, NP * BLK), jnp.float32),
             pltpu.VMEM((ROWS, S1), jnp.float32),
             pltpu.VMEM((NP, BLK, S1), jnp.float32),
             pltpu.SemaphoreType.DMA((NP,)),
         ],
         compiler_params=pltpu.CompilerParams(vmem_limit_bytes=CROSS_LIMIT),
-    )(chosen, lower.reshape(NP, BLK, S1))
+    )(panel_high, panel_low, lower.reshape(NP, BLK, S1))
     pieces = lax.all_to_all(
         pieces.reshape(N_GRID, PIECE3, 1, BLK), GRID, 0, 0, tiled=True
     ).reshape(N_GRID * PIECE3, BLK)

time: 115 us -> 110 us (0.957)
  local copies, waits for them, and re-layouts: 4.62 us -> 2.51 us
  other arithmetic: 1.6 us -> 0 us
    unnamed x12 -> x10, local copies, waits for them, and re-layouts: 4.62 us -> 2.51 us
    concatenate x1 -> x0, other arithmetic: 1.6 us -> none  [shards(): jnp.concatenate([own_rows, lax.ppermute(own_rows, 'side', [(0, 1), (1, 0)...]
where the time goes in v3:
time: 110 us
  blocking collectives  77.3 us (70%)
  between operations  14.1 us (13%)
  Pallas kernels  9.33 us (8%)
  starting transfers between devices  3.35 us (3%)
  waiting for transfers between devices  3.04 us (3%)
  local copies, waits for them, and re-layouts  2.51 us (2%)
    all_to_all x1, blocking collectives, shards(): lax.all_to_all(pieces.reshape(N_GRID, PIECE3, 1, BLK), GRID, 0, 0, tiled=...  30.9 us
    all_to_all x1, blocking collectives, shards(): chosen = lax.all_to_all(chosen, 'leaf', 0, 0, tiled=True)  25.2 us
    all_to_all x1, blocking collectives, shards(): spread = lax.all_to_all(spread, 'leaf', 0, 0, tiled=True)  21.2 us
    pallas_call x1, Pallas kernels, shards(): pl.pallas_call(cross_kernel, out_shape=(jax.ShapeDtypeStruct((1, ROWS, S1...  4.45 us
    ppermute x1, starting transfers between devices, shards(): received = lax.ppermute(own_rows, 'side', [(0, 1), (1, 0)])  3.31 us
    ppermute x1, waiting for transfers between devices, shards(): received = lax.ppermute(own_rows, 'side', [(0, 1), (1, 0)])  2.61 us
    unnamed x10, local copies, waits for them, and re-layouts  2.51 us
  transfers between devices with their start and end apart: 2, of which 2 were waited for; matrix products, arithmetic and copies ran while one was open for 0% of the time, Pallas kernels for 2%

profile of v3, /device:TPU:6, one launch (start us, length us, event | category | flops | bytes accessed | tf_op | source)
XLA Modules:
  0.0 109.6 jit_solution(2192188087332104325)
XLA Ops:
  7.2 0.0 all-gather.2.cloned.1.call-start
  7.2 3.3 %collective-permute-start = (f32[32,896]{1,0:T(8,128)}, f32[32,896]{1,0:T(8,128)S(1)}, u32[]{:S(2)}, u32[]{:S(2)}) collective-permute-start(f32[32,896]{1,0:T(8,128)} %bitcast.8), channel_id=1, source_target_pairs={{0,2},{2,0},{1,3},{3,1},{4,6},{6,4},{5,7},{7,5},{8,10},{10,8},{9,1... | collective-permute-start | bytes 344072 | tf_op jit(solution)/shard_map/ppermute | solution.py:151
  10.5 0.0 copy-start
  10.5 1.0 copy-done
  11.5 0.0 copy-start.1
  11.5 0.9 copy-done.1
  12.4 0.0 copy-start.3
  12.4 0.7 copy-done.3
  13.1 2.6 %collective-permute-done.received = f32[32,896]{1,0:T(8,128)S(1)} collective-permute-done((f32[32,896]{1,0:T(8,128)}, f32[32,896]{1,0:T(8,128)S(1)}, u32[]{:S(2)}, u32[]{:S(2)}) %collective-permute-start) | collective-permute-done | bytes 114720 | tf_op jit(solution)/shard_map/ppermute | solution.py:151
  15.7 0.7 shard_map.60
  16.4 0.0 all-gather.2.cloned.1.call-update
  16.4 21.2 %all_to_all.15.pieces = f32[16,40,128]{2,1,0:T(8,128)S(1)} all-to-all(f32[16,40,128]{2,1,0:T(8,128)S(1)} %get-tuple-element.18), channel_id=1, replica_groups=mesh['leaf'=16,'prow'=8,'side'=2,'core'=2] {'leaf'}, dimensions={0} | all-to-all | bytes 655360 | tf_op jit(solution)/shard_map/all_to_all | solution.py:173
  37.6 1.7 %shard_map.61 = f32[16,96,128]{2,1,0:T(8,128)S(1)} custom-call(f32[16,40,128]{2,1,0:T(8,128)S(1)} %all_to_all.15.pieces), custom_call_target="tpu_custom_call" | custom-call | tf_op jit(solution)/shard_map/pallas_call | solution.py:174
  39.3 25.2 %all_to_all.16.pieces = f32[16,96,128]{2,1,0:T(8,128)S(1)} all-to-all(f32[16,96,128]{2,1,0:T(8,128)S(1)} %shard_map.61), channel_id=1, replica_groups=mesh['leaf'=16,'prow'=8,'side'=2,'core'=2] {'leaf'}, dimensions={0} | all-to-all | bytes 1572864 | tf_op jit(solution)/shard_map/all_to_all | solution.py:182
  64.6 0.3 shard_map.62
  64.9 0.4 all-gather.2.cloned.1.call-done
  65.3 0.0 copy-start.2
  65.3 0.0 copy-start.4
  65.3 4.4 %shard_map.63 = (f32[1,192,896]{2,1,0:T(8,128)}, f32[1344,128]{1,0:T(8,128)S(1)}, bf16[1024,896]{1,0:T(8,128)(2,1)S(1)}, bf16[1024,896]{1,0:T(8,128)(2,1)S(1)}) custom-call(bf16[192,1024]{1,0:T(8,128)(2,1)S(1)} %get-tuple-element.19.panel_high, bf16[192,1024]{1,0:T(8,128)(2,1)S(1)} %get-tuple-element.20.panel_low, f32[8,128,896]{2,1,0:T(8,128)} %bitcast.11), custom_call_target="tpu_custom_call" | custom-call | tf_op jit(solution)/shard_map/pallas_call | solution.py:191
  69.7 30.9 %all_to_all.17 = f32[32,42,1,128]{3,2,1,0:T(1,128)S(1)} all-to-all(f32[32,42,1,128]{3,2,1,0:T(1,128)S(1)} %bitcast.7), channel_id=1, replica_groups=mesh['leaf'=16,'prow'=8,'side'=2,'core'=2] {'prow','side','core'}, dimensions={0} | all-to-all | bytes 1376256 | tf_op jit(solution)/shard_map/all_to_all | solution.py:208
  100.6 0.0 copy-done.2
  100.6 0.0 copy-done.4
  100.6 2.2 %shard_map.64 = f32[28,1,896]{2,1,0:T(1,128)} custom-call(s32[1,8]{1,0:T(1,128)S(1)} %copy-done.4, f32[1344,128]{1,0:T(8,128)S(1)} %bitcast.6, bf16[1024,896]{1,0:T(8,128)(2,1)S(1)} %get-tuple-element.24.lower_high, bf16[1024,896]{1,0:T(8,128)(2,1)S(1)} %get-tuple-element.25.lower_low, f32[28,1,896]{2,1,0:T(1,128)S(1)} %bitcast.10), custom_call_target="tpu_custom_call" | custom-call | tf_op jit(solution)/shard_map/pallas_call | solution.py:211
  (1 shorter events, 0.0 us)
Async XLA Ops:
  7.2 58.1 %all-gather.2.cloned.1.call-start = ((), (), s32[]{:S(2)}) async-start(), calls=%async_computation.3 | async-start | bytes 3899392 | tf_op jit(solution)/shard_map/all_gather | solution.py:172
  7.2 8.5 %collective-permute-start = (f32[32,896]{1,0:T(8,128)}, f32[32,896]{1,0:T(8,128)S(1)}, u32[]{:S(2)}, u32[]{:S(2)}) collective-permute-start(f32[32,896]{1,0:T(8,128)} %bitcast.8), channel_id=1, source_target_pairs={{0,2},{2,0},{1,3},{3,1},{4,6},{6,4},{5,7},{7,5},{8,10},{10,8},{9,1... | collective-permute-start | bytes 344072 | tf_op jit(solution)/shard_map/ppermute | solution.py:151
  10.5 1.0 copy-start
  11.5 0.9 copy-start.1
  12.4 0.7 copy-start.3
  65.3 35.3 %copy-start.2 = (f32[1,28,896]{2,0,1:T(1,128)S(1)}, f32[1,28,896]{2,0,1:T(1,128)}, u32[]{:S(2)}) copy-start(f32[1,28,896]{2,0,1:T(1,128)} %param.7) | copy-start | bytes 301060
  65.3 35.3 %copy-start.4 = (s32[1,8]{1,0:T(1,128)S(1)}, s32[1,8]{1,0:T(1,128)}, u32[]{:S(2)}) copy-start(s32[1,8]{1,0:T(1,128)} %pattern.3) | copy-start | bytes 100
Sparse Core Ops, SparseCore 0:
  16.6 48.6 all-gather.1

commit v4 on v2

--- a/solution.py
+++ b/solution.py
@@ -16,16 +16,32 @@
 S1 = 896
 COLS = S1 // N_GRID
 LROWS = 32
+SELECT_PARTS = 4
 PAT_ROW = OWN_BLOCKS * CHUNK
 PIECE1 = 40
 PIECE2 = NP * CHUNK
 HALF = COLS // 2
 PIECE3 = COLS + HALF
 VMEM_LIMIT = 16 * 1024 * 1024
-CROSS_LIMIT = 52 * 1024 * 1024
+CROSS_LIMIT = 16 * 1024 * 1024
 
 
 GRID = ("prow", "side", "core")
+
+
+STEPS = ((0, 2), (1, 3), (-1, -3), (-2, 4))
+
+
+def from_row(value, distance):
+    return lax.ppermute(value, "prow", [(at, (at - distance) % NP) for at in range(NP)])
+
+
+def swap_side(value):
+    return lax.ppermute(value, "side", [(0, 1), (1, 0)])
+
+
+def hint(microseconds):
+    return pl.CostEstimate(flops=int(microseconds * 1.1e9), bytes_accessed=int(microseconds * 3.7e6), transcendentals=0)
 
 
 def in_vmem(count):
@@ -49,43 +65,79 @@
         out[leaf, PAT_ROW:PAT_ROW + 1, 0:NP] = row
 
 
-def select_kernel(pieces, out, patterns, semaphore):
-    copy = pltpu.make_async_copy(pieces.at[:, PAT_ROW:PAT_ROW + 1, :], patterns, semaphore)
-    copy.start()
-    copy.wait()
-
-    def one_leaf(leaf, carry):
-        for block in range(NP):
-            number = patterns[leaf, 0, block].astype(jnp.int32)
-            owner = number // OWN_BLOCKS
-            first = (number - owner * OWN_BLOCKS) * CHUNK
-            out[leaf, block * CHUNK:(block + 1) * CHUNK, :] = pieces[owner, pl.ds(first, CHUNK), :]
-        return carry
-
-    lax.fori_loop(0, N_LEAF, one_leaf, 0)
-
-
-def cross_kernel(pieces, lower, cross, out, lower_high, lower_low, panel, product, held, semaphores):
-    core = lax.axis_index("core")
-    side = lax.axis_index("side")
+def pair_kernel(own, across, out):
+    out[0:LROWS, :] = own[...]
+    out[LROWS:2 * LROWS, :] = across[...]
+
+
+def stack(out, *parts):
+    first = 0
+    for part in parts:
+        rows = part.shape[0]
+        out[first:first + rows, :] = part[...]
+        first += rows
+
+
+def near_kernel(pair, ahead, behind, up, down, up_half, down_half):
+    stack(up, pair, ahead)
+    stack(down, pair, behind)
+    up_half[...] = ahead[0:LROWS, :]
+    down_half[...] = behind[LROWS:2 * LROWS, :]
+
+
+def far_kernel(*refs):
+    stack(refs[-1], *refs[:-1])
+
+
+def select_kernel(pieces, out, held, chosen, patterns, semaphores):
     copies = [
-        pltpu.make_async_copy(lower.at[block], held.at[block], semaphores.at[block])
-        for block in range(NP)
+        pltpu.make_async_copy(pieces, held, semaphores.at[0]),
+        pltpu.make_async_copy(pieces.at[:, PAT_ROW:PAT_ROW + 1, :], patterns, semaphores.at[1]),
     ]
     for copy in copies:
         copy.start()
+    for copy in copies:
+        copy.wait()
+    sent = []
+    for part in range(SELECT_PARTS):
+        count = N_LEAF // SELECT_PARTS
+        for leaf in range(part * count, (part + 1) * count):
+            for block in range(NP):
+                number = patterns[leaf, 0, block].astype(jnp.int32)
+                owner = number // OWN_BLOCKS
+                first = (number - owner * OWN_BLOCKS) * CHUNK
+                chosen[leaf, block * CHUNK:(block + 1) * CHUNK, :] = held[
+                    owner, pl.ds(first, CHUNK), :
+                ]
+        here = pl.ds(part * count, count)
+        sent.append(pltpu.make_async_copy(chosen.at[here], out.at[here], semaphores.at[2 + part]))
+        sent[-1].start()
+    for copy in sent:
+        copy.wait()
+
+
+def panel_kernel(pieces, high, low, panel):
     for leaf in range(N_LEAF):
         for block in range(NP):
             panel[leaf * CHUNK:(leaf + 1) * CHUNK, block * BLK:(block + 1) * BLK] = pieces[
                 leaf, block * CHUNK:(block + 1) * CHUNK, :
             ]
-    panel_high, panel_low = split(panel[...])
-    for block in range(NP):
-        copies[block].wait()
-        for at_core in range(2):
+    high[...], low[...] = split(panel[...])
+
+
+def cross_kernel(panel_high, panel_low, *refs):
+    sources = refs[:2 * len(STEPS)]
+    cross, out, lower_high, lower_low, product = refs[2 * len(STEPS):]
+    core = lax.axis_index("core")
+    side = lax.axis_index("side")
+    place = lax.axis_index("prow")
+    for at, source in enumerate(sources):
+        at_core = core if at < len(STEPS) else 1 - core
+        for group, step in enumerate(STEPS[at % len(STEPS)]):
+            block = lax.rem(place + step + NP, NP)
             for part, at_side in ((0, side), (1, 1 - side)):
-                row = at_core * 64 + part * LROWS
-                high, low = split(held[block, row:row + LROWS, :])
+                row = group * 64 + part * LROWS
+                high, low = split(source[row:row + LROWS, :])
                 first = pl.multiple_of(block * BLK + at_side * 64 + at_core * LROWS, LROWS)
                 lower_high[pl.ds(first, LROWS), :] = high
                 lower_low[pl.ds(first, LROWS), :] = low
@@ -93,8 +145,8 @@
     def dot(a, b):
         return jnp.dot(a, b, preferred_element_type=jnp.float32)
 
-    value = dot(panel_high, lower_high[...]) + (
-        dot(panel_low, lower_high[...]) + dot(panel_high, lower_low[...])
+    value = dot(panel_high[...], lower_high[...]) + (
+        dot(panel_low[...], lower_high[...]) + dot(panel_high[...], lower_low[...])
     )
     product[...] = value
     cross[0, :, :] = -value
@@ -135,12 +187,20 @@
         out[row, 0:1, :] = child[row, 0:1, :] + update[row:row + 1, :]
 
 
+def call(kernel, rows, microseconds, *parts):
+    return pl.pallas_call(
+        kernel,
+        out_shape=tuple(jax.ShapeDtypeStruct((count, S1), jnp.float32) for count in rows),
+        in_specs=in_vmem(len(parts)),
+        out_specs=tuple(in_vmem(len(rows))),
+        cost_estimate=hint(microseconds),
+        compiler_params=pltpu.CompilerParams(vmem_limit_bytes=VMEM_LIMIT),
+    )(*parts)
+
+
 def shards(ancestor_inverse, pattern, child_lower, child_diag_inv):
     params = pltpu.CompilerParams(vmem_limit_bytes=VMEM_LIMIT)
-    own_rows = child_lower[0]
-    pair = jnp.concatenate(
-        [own_rows, lax.ppermute(own_rows, "side", [(0, 1), (1, 0)])], axis=0
-    )
+    own = child_lower[0]
     spread = pl.pallas_call(
         spread_kernel,
         out_shape=jax.ShapeDtypeStruct((N_LEAF, PIECE1, BLK), jnp.float32),
@@ -148,18 +208,43 @@
         out_specs=in_vmem(1)[0],
         compiler_params=params,
     )(ancestor_inverse, pattern)
-    pair, spread = lax.optimization_barrier((pair, spread))
-    lower = lax.all_gather(pair, ("prow", "core"), axis=0, tiled=True)
+    across = swap_side(own)
+    pair = pl.pallas_call(
+        pair_kernel,
+        out_shape=jax.ShapeDtypeStruct((64, S1), jnp.float32),
+        in_specs=in_vmem(2),
+        out_specs=in_vmem(1)[0],
+        cost_estimate=hint(2000),
+        compiler_params=params,
+    )(own, across)
+    ahead, behind = from_row(pair, 2), from_row(pair, -2)
     spread = lax.all_to_all(spread, "leaf", 0, 0, tiled=True)
     chosen = pl.pallas_call(
         select_kernel,
         out_shape=jax.ShapeDtypeStruct((N_LEAF, PIECE2, BLK), jnp.float32),
-        in_specs=in_vmem(1),
-        out_specs=in_vmem(1)[0],
-        scratch_shapes=[pltpu.SMEM((N_LEAF, 1, BLK), jnp.float32), pltpu.SemaphoreType.DMA(())],
+        in_specs=[pl.BlockSpec(memory_space=pl.ANY)],
+        out_specs=pl.BlockSpec(memory_space=pl.ANY),
+        scratch_shapes=[
+            pltpu.VMEM((N_LEAF, PIECE1, BLK), jnp.float32),
+            pltpu.VMEM((N_LEAF, PIECE2, BLK), jnp.float32),
+            pltpu.SMEM((N_LEAF, 1, BLK), jnp.float32),
+            pltpu.SemaphoreType.DMA((2 + SELECT_PARTS,)),
+        ],
         compiler_params=params,
     )(spread)
     chosen = lax.all_to_all(chosen, "leaf", 0, 0, tiled=True)
+    up, down, up_half, down_half = call(near_kernel, (128, 128, 32, 32), 2000, pair, ahead, behind)
+    (far,) = call(far_kernel, (128,), 0, behind, from_row(up_half, 2), from_row(down_half, -2))
+    mine = [up, from_row(up, 1), from_row(down, -1), far]
+    other = [lax.ppermute(value, "core", [(0, 1), (1, 0)]) for value in mine]
+    panel_high, panel_low = pl.pallas_call(
+        panel_kernel,
+        out_shape=(jax.ShapeDtypeStruct((ROWS, NP * BLK), jnp.bfloat16),) * 2,
+        in_specs=in_vmem(1),
+        out_specs=tuple(in_vmem(2)),
+        scratch_shapes=[pltpu.VMEM((ROWS, NP * BLK), jnp.float32)],
+        compiler_params=params,
+    )(chosen)
     cross, pieces, lower_high, lower_low = pl.pallas_call(
         cross_kernel,
         out_shape=(
@@ -168,16 +253,13 @@
             jax.ShapeDtypeStruct((NP * BLK, S1), jnp.bfloat16),
             jax.ShapeDtypeStruct((NP * BLK, S1), jnp.bfloat16),
         ),
-        in_specs=in_vmem(1) + [pl.BlockSpec(memory_space=pltpu.HBM)],
+        in_specs=in_vmem(10),
         out_specs=tuple(in_vmem(4)),
         scratch_shapes=[
-            pltpu.VMEM((ROWS, NP * BLK), jnp.float32),
             pltpu.VMEM((ROWS, S1), jnp.float32),
-            pltpu.VMEM((NP, BLK, S1), jnp.float32),
-            pltpu.SemaphoreType.DMA((NP,)),
         ],
         compiler_params=pltpu.CompilerParams(vmem_limit_bytes=CROSS_LIMIT),
-    )(chosen, lower.reshape(NP, BLK, S1))
+    )(panel_high, panel_low, *mine, *other)
     pieces = lax.all_to_all(
         pieces.reshape(N_GRID, PIECE3, 1, BLK), GRID, 0, 0, tiled=True
     ).reshape(N_GRID * PIECE3, BLK)

time: 115 us -> 105 us (0.913)
  blocking collectives: 77.2 us -> 28.4 us
  starting transfers between devices: 3.35 us -> 52 us
  between operations: 14.1 us -> 0.82 us
  waiting for transfers between devices: 4.07 us -> 9.82 us
  local copies, waits for them, and re-layouts: 4.62 us -> 2.51 us
  Pallas kernels: 9.21 us -> 11.1 us
  other arithmetic: 1.6 us -> 0 us
    all_to_all x2 -> x0, blocking collectives: 46.4 us -> none  [the longest x1 25.2 us: shards(): chosen = lax.all_to_all(chosen, 'leaf', 0, 0, tiled=True)]
    ppermute x1 -> x11, starting transfers between devices: 3.32 us -> 33.4 us  [the longest x6 21.9 us: from_row(): lax.ppermute(value, 'prow', [(at, (at - distance) % NP) for at in range(N...]
    all_to_all x0 -> x2, starting transfers between devices: none -> 18.6 us  [the longest x1 11.8 us: shards(): spread = lax.all_to_all(spread, 'leaf', 0, 0, tiled=True)]
    ppermute x1 -> x11, waiting for transfers between devices: 3.52 us -> 8.48 us  [the longest x6 8 us: from_row(): lax.ppermute(value, 'prow', [(at, (at - distance) % NP) for at in range(N...]
    all_to_all x1, blocking collectives: 30.7 us -> 28.4 us  [shards(): lax.all_to_all(pieces.reshape(N_GRID, PIECE3, 1, BLK), GRID, 0, 0, tiled=...]
    unnamed x12 -> x10, local copies, waits for them, and re-layouts: 4.62 us -> 2.51 us
    concatenate x1 -> x0, other arithmetic: 1.6 us -> none  [shards(): jnp.concatenate([own_rows, lax.ppermute(own_rows, 'side', [(0, 1), (1, 0)...]
    pallas_call x0 -> x4, Pallas kernels: none -> 1.52 us  [the longest x1 1.4 us: shards(): pl.pallas_call(panel_kernel, out_shape=(jax.ShapeDtypeStruct((ROWS, NP *...]
  transfers between devices with their start and end apart: 2 -> 13, of which waited for: 2 -> 4; matrix products, arithmetic and copies ran while one was open for 0% -> 0% of each run, Pallas kernels for 2% -> 5%
where the time goes in v4:
time: 105 us
  starting transfers between devices  52 us (50%)
  blocking collectives  28.4 us (27%)
  Pallas kernels  11.1 us (11%)
  waiting for transfers between devices  9.82 us (9%)
  local copies, waits for them, and re-layouts  2.51 us (2%)
    all_to_all x1, blocking collectives, shards(): lax.all_to_all(pieces.reshape(N_GRID, PIECE3, 1, BLK), GRID, 0, 0, tiled=...  28.4 us
    ppermute x6, starting transfers between devices, from_row(): lax.ppermute(value, 'prow', [(at, (at - distance) % NP) for at in range(N...  21.9 us
    all_to_all x1, starting transfers between devices, shards(): spread = lax.all_to_all(spread, 'leaf', 0, 0, tiled=True)  11.8 us
    ppermute x4, starting transfers between devices, shards(): other = [lax.ppermute(value, 'core', [(0, 1), (1, 0)]) for value in mine]  8.17 us
    ppermute x6, waiting for transfers between devices, from_row(): lax.ppermute(value, 'prow', [(at, (at - distance) % NP) for at in range(N...  8 us
    all_to_all x1, starting transfers between devices, shards(): chosen = lax.all_to_all(chosen, 'leaf', 0, 0, tiled=True)  6.81 us
    pallas_call x1, Pallas kernels, shards(): pl.pallas_call(cross_kernel, out_shape=(jax.ShapeDtypeStruct((1, ROWS, S1...  3.85 us
    ppermute x1, starting transfers between devices, swap_side(): return lax.ppermute(value, 'side', [(0, 1), (1, 0)])  3.32 us
  transfers between devices with their start and end apart: 13, of which 4 were waited for; matrix products, arithmetic and copies ran while one was open for 0% of the time, Pallas kernels for 5%

profile of v4, /device:TPU:6, one launch (start us, length us, event | category | flops | bytes accessed | tf_op | source)
XLA Modules:
  0.0 104.5 jit_solution(6276311332396263247)
XLA Ops:
  0.6 3.3 %collective-permute-start = (f32[32,896]{1,0:T(8,128)}, f32[32,896]{1,0:T(8,128)S(1)}, u32[]{:S(2)}, u32[]{:S(2)}) collective-permute-start(f32[32,896]{1,0:T(8,128)} %bitcast.8), channel_id=1, source_target_pairs={{0,2},{2,0},{1,3},{3,1},{4,6},{6,4},{5,7},{7,5},{8,10},{10,8},{9,1... | collective-permute-start | bytes 344072 | tf_op jit(solution)/shard_map/ppermute | solution.py:40
  4.0 1.0 copy-done
  4.9 0.7 copy-done.2
  5.6 0.8 shard_map.59
  6.3 11.8 %all-to-all-start = ((f32[16,40,128]{2,1,0:T(8,128)}), f32[16,40,128]{2,1,0:T(8,128)}, u32[]{:S(2)}, u32[]{:S(2)}) async-start(f32[16,40,128]{2,1,0:T(8,128)} %shard_map.59), calls=%async_computation | async-start | bytes 655360 | tf_op jit(solution)/shard_map/all_to_all | solution.py:221
  18.1 0.0 collective-permute-done.across
  18.1 0.0 copy-start.4
  18.1 0.9 copy-done.4
  19.1 4.5 %collective-permute-start.2 = (f32[64,896]{1,0:T(8,128)S(1)}, f32[64,896]{1,0:T(8,128)S(1)}, u32[]{:S(2)}, u32[]{:S(2)}) collective-permute-start(f32[64,896]{1,0:T(8,128)S(1)} %shard_map.62.pair), channel_id=1, source_target_pairs={{0,8},{4,12},{8,16},{12,20},{16,24},{20,28},{24,0},{28,4},{1,9},{5... | collective-permute-start | bytes 688136 | tf_op jit(solution)/shard_map/ppermute | solution.py:36
  23.6 3.6 %collective-permute-start.1 = (f32[64,896]{1,0:T(8,128)S(1)}, f32[64,896]{1,0:T(8,128)S(1)}, u32[]{:S(2)}, u32[]{:S(2)}) collective-permute-start(f32[64,896]{1,0:T(8,128)S(1)} %shard_map.62.pair), channel_id=1, source_target_pairs={{0,24},{4,28},{8,0},{12,4},{16,8},{20,12},{24,16},{28,20},{1,25},{... | collective-permute-start | bytes 688136 | tf_op jit(solution)/shard_map/ppermute | solution.py:36
  27.1 1.3 %all-to-all-done.pieces = f32[16,40,128]{2,1,0:T(8,128)} async-done(((f32[16,40,128]{2,1,0:T(8,128)}), f32[16,40,128]{2,1,0:T(8,128)}, u32[]{:S(2)}, u32[]{:S(2)}) %all-to-all-start) | async-done | bytes 327712 | tf_op jit(solution)/shard_map/all_to_all | solution.py:221
  28.5 2.7 %shard_map.60 = f32[16,96,128]{2,1,0:T(8,128)} custom-call(f32[16,40,128]{2,1,0:T(8,128)} %all-to-all-done.pieces), custom_call_target="tpu_custom_call" | custom-call | tf_op jit(solution)/shard_map/pallas_call | solution.py:222
  31.2 6.8 %all-to-all-start.1 = ((f32[16,96,128]{2,1,0:T(8,128)}), f32[16,96,128]{2,1,0:T(8,128)}, u32[]{:S(2)}, u32[]{:S(2)}) async-start(f32[16,96,128]{2,1,0:T(8,128)} %shard_map.60), calls=%async_computation.1 | async-start | bytes 1572864 | tf_op jit(solution)/shard_map/all_to_all | solution.py:235
  38.0 0.0 collective-permute-done.2.behind.refs_0_
  38.1 0.6 collective-permute-done.1.ahead
  38.7 0.1 shard_map.63
  38.7 2.8 %collective-permute-start.4 = (f32[128,896]{1,0:T(8,128)S(1)}, f32[128,896]{1,0:T(8,128)S(1)}, u32[]{:S(2)}, u32[]{:S(2)}) collective-permute-start(f32[128,896]{1,0:T(8,128)S(1)} %get-tuple-element.15), channel_id=1, source_target_pairs={{0,4},{4,8},{8,12},{12,16},{16,20},{20,24},{24,28},{28,0},{1,5},{5... | collective-permute-start | bytes 1376264 | tf_op jit(solution)/shard_map/ppermute | solution.py:36
  41.5 4.3 %collective-permute-start.3 = (f32[128,896]{1,0:T(8,128)S(1)}, f32[128,896]{1,0:T(8,128)S(1)}, u32[]{:S(2)}, u32[]{:S(2)}) collective-permute-start(f32[128,896]{1,0:T(8,128)S(1)} %get-tuple-element.14.refs_0_), channel_id=1, source_target_pairs={{0,28},{4,0},{8,4},{12,8},{16,12},{20,16},{24,20},{28,24},{1,29},{... | collective-permute-start | bytes 1376264 | tf_op jit(solution)/shard_map/ppermute | solution.py:36
  45.8 3.6 %collective-permute-start.5 = (f32[32,896]{1,0:T(8,128)S(1)}, f32[32,896]{1,0:T(8,128)S(1)}, u32[]{:S(2)}, u32[]{:S(2)}) collective-permute-start(f32[32,896]{1,0:T(8,128)S(1)} %get-tuple-element.16), channel_id=1, source_target_pairs={{0,24},{4,28},{8,0},{12,4},{16,8},{20,12},{24,16},{28,20},{1,25},{... | collective-permute-start | bytes 344072 | tf_op jit(solution)/shard_map/ppermute | solution.py:36
  49.4 3.2 %collective-permute-start.6 = (f32[32,896]{1,0:T(8,128)S(1)}, f32[32,896]{1,0:T(8,128)S(1)}, u32[]{:S(2)}, u32[]{:S(2)}) collective-permute-start(f32[32,896]{1,0:T(8,128)S(1)} %get-tuple-element.17), channel_id=1, source_target_pairs={{0,8},{4,12},{8,16},{12,20},{16,24},{20,28},{24,0},{28,4},{1,9},{5... | collective-permute-start | bytes 344072 | tf_op jit(solution)/shard_map/ppermute | solution.py:36
  52.6 1.9 %collective-permute-start.7 = (f32[128,896]{1,0:T(8,128)S(1)}, f32[128,896]{1,0:T(8,128)S(1)}, u32[]{:S(2)}, u32[]{:S(2)}) collective-permute-start(f32[128,896]{1,0:T(8,128)S(1)} %get-tuple-element.14.refs_0_), channel_id=1, source_target_pairs={{0,1},{1,0},{2,3},{3,2},{4,5},{5,4},{6,7},{7,6},{8,9},{9,8},{10,11... | collective-permute-start | bytes 1376264 | tf_op jit(solution)/shard_map/ppermute | solution.py:239
  54.5 7.4 %collective-permute-done.5.refs_1_ = f32[32,896]{1,0:T(8,128)S(1)} collective-permute-done((f32[32,896]{1,0:T(8,128)S(1)}, f32[32,896]{1,0:T(8,128)S(1)}, u32[]{:S(2)}, u32[]{:S(2)}) %collective-permute-start.5) | collective-permute-done | bytes 114720 | tf_op jit(solution)/shard_map/ppermute | solution.py:36
  61.9 1.9 %collective-permute-start.10 = (f32[128,896]{1,0:T(8,128)S(1)}, f32[128,896]{1,0:T(8,128)S(1)}, u32[]{:S(2)}, u32[]{:S(2)}) collective-permute-start(f32[128,896]{1,0:T(8,128)S(1)} %shard_map.64.refs_3_), channel_id=1, source_target_pairs={{0,1},{1,0},{2,3},{3,2},{4,5},{5,4},{6,7},{7,6},{8,9},{9,8},{10,11... | collective-permute-start | bytes 1376264 | tf_op jit(solution)/shard_map/ppermute | solution.py:239
  63.9 2.4 %collective-permute-start.9 = (f32[128,896]{1,0:T(8,128)S(1)}, f32[128,896]{1,0:T(8,128)S(1)}, u32[]{:S(2)}, u32[]{:S(2)}) collective-permute-start(f32[128,896]{1,0:T(8,128)S(1)} %collective-permute-done.4.refs_2_), channel_id=1, source_target_pairs={{0,1},{1,0},{2,3},{3,2},{4,5},{5,4},{6,7},{7,6},{8,9},{9,8},{10,11... | collective-permute-start | bytes 1376264 | tf_op jit(solution)/shard_map/ppermute | solution.py:239
  66.3 1.9 %collective-permute-start.8 = (f32[128,896]{1,0:T(8,128)S(1)}, f32[128,896]{1,0:T(8,128)}, u32[]{:S(2)}, u32[]{:S(2)}) collective-permute-start(f32[128,896]{1,0:T(8,128)S(1)} %collective-permute-done.3.refs_1_), channel_id=1, source_target_pairs={{0,1},{1,0},{2,3},{3,2},{4,5},{5,4},{6,7},{7,6},{8,9},{9,8},{10,11... | collective-permute-start | bytes 1376264 | tf_op jit(solution)/shard_map/ppermute | solution.py:239
  68.2 1.4 %shard_map.61 = (bf16[192,1024]{1,0:T(8,128)(2,1)S(1)}, bf16[192,1024]{1,0:T(8,128)(2,1)S(1)}) custom-call(f32[16,96,128]{2,1,0:T(8,128)} %all-to-all-done.1.pieces), custom_call_target="tpu_custom_call" | custom-call | tf_op jit(solution)/shard_map/pallas_call | solution.py:240
  69.6 0.0 collective-permute-done.10.refs_7_
  69.6 0.0 collective-permute-done.9.refs_6_
  69.7 0.5 collective-permute-done.8.refs_5_
  70.1 3.9 %shard_map.65 = (f32[1,192,896]{2,1,0:T(8,128)}, f32[1344,128]{1,0:T(8,128)S(1)}, bf16[1024,896]{1,0:T(8,128)(2,1)S(1)}, bf16[1024,896]{1,0:T(8,128)(2,1)S(1)}) custom-call(bf16[192,1024]{1,0:T(8,128)(2,1)S(1)} %get-tuple-element.12.panel_high, bf16[192,1024]{1,0:T(8,128)(2,1)S(1)} %get-tuple-element.13.panel_low, f32[128,896]{1,0:T(8,128)S(1)} %get-tuple-element.14.refs_0_, ...), custom_call_target="tpu_custom_call" | custom-call | tf_op jit(solution)/shard_map/pallas_call | solution.py:248
  74.0 28.4 %all_to_all.15 = f32[32,42,1,128]{3,2,1,0:T(1,128)S(1)} all-to-all(f32[32,42,1,128]{3,2,1,0:T(1,128)S(1)} %bitcast.6), channel_id=1, replica_groups=mesh['leaf'=16,'prow'=8,'side'=2,'core'=2] {'prow','side','core'}, dimensions={0} | all-to-all | bytes 1376256 | tf_op jit(solution)/shard_map/all_to_all | solution.py:263
  102.4 2.2 %shard_map.66 = f32[28,1,896]{2,1,0:T(1,128)} custom-call(s32[1,8]{1,0:T(1,128)S(1)} %copy-done.3, f32[1344,128]{1,0:T(8,128)S(1)} %bitcast.5, bf16[1024,896]{1,0:T(8,128)(2,1)S(1)} %get-tuple-element.20.lower_high, bf16[1024,896]{1,0:T(8,128)(2,1)S(1)} %get-tuple-element.21.lower_low, f32[28,1,896]{2,1,0:T(1,128)S(1)} %bitcast.7), custom_call_target="tpu_custom_call" | custom-call | tf_op jit(solution)/shard_map/pallas_call | solution.py:266
  (13 shorter events, 0.1 us)
Async XLA Ops:
  0.6 17.5 %collective-permute-start = (f32[32,896]{1,0:T(8,128)}, f32[32,896]{1,0:T(8,128)S(1)}, u32[]{:S(2)}, u32[]{:S(2)}) collective-permute-start(f32[32,896]{1,0:T(8,128)} %bitcast.8), channel_id=1, source_target_pairs={{0,2},{2,0},{1,3},{3,1},{4,6},{6,4},{5,7},{7,5},{8,10},{10,8},{9,1... | collective-permute-start | bytes 344072 | tf_op jit(solution)/shard_map/ppermute | solution.py:40
  4.0 1.0 copy-start
  4.9 0.7 copy-start.2
  6.3 22.2 %all-to-all-start = ((f32[16,40,128]{2,1,0:T(8,128)}), f32[16,40,128]{2,1,0:T(8,128)}, u32[]{:S(2)}, u32[]{:S(2)}) async-start(f32[16,40,128]{2,1,0:T(8,128)} %shard_map.59), calls=%async_computation | async-start | bytes 655360 | tf_op jit(solution)/shard_map/all_to_all | solution.py:221
  18.1 0.9 copy-start.4
  19.1 19.0 %collective-permute-start.2 = (f32[64,896]{1,0:T(8,128)S(1)}, f32[64,896]{1,0:T(8,128)S(1)}, u32[]{:S(2)}, u32[]{:S(2)}) collective-permute-start(f32[64,896]{1,0:T(8,128)S(1)} %shard_map.62.pair), channel_id=1, source_target_pairs={{0,8},{4,12},{8,16},{12,20},{16,24},{20,28},{24,0},{28,4},{1,9},{5... | collective-permute-start | bytes 688136 | tf_op jit(solution)/shard_map/ppermute | solution.py:36
  23.6 15.1 %collective-permute-start.1 = (f32[64,896]{1,0:T(8,128)S(1)}, f32[64,896]{1,0:T(8,128)S(1)}, u32[]{:S(2)}, u32[]{:S(2)}) collective-permute-start(f32[64,896]{1,0:T(8,128)S(1)} %shard_map.62.pair), channel_id=1, source_target_pairs={{0,24},{4,28},{8,0},{12,4},{16,8},{20,12},{24,16},{28,20},{1,25},{... | collective-permute-start | bytes 688136 | tf_op jit(solution)/shard_map/ppermute | solution.py:36
  31.2 37.0 %all-to-all-start.1 = ((f32[16,96,128]{2,1,0:T(8,128)}), f32[16,96,128]{2,1,0:T(8,128)}, u32[]{:S(2)}, u32[]{:S(2)}) async-start(f32[16,96,128]{2,1,0:T(8,128)} %shard_map.60), calls=%async_computation.1 | async-start | bytes 1572864 | tf_op jit(solution)/shard_map/all_to_all | solution.py:235
  38.7 25.1 %collective-permute-start.4 = (f32[128,896]{1,0:T(8,128)S(1)}, f32[128,896]{1,0:T(8,128)S(1)}, u32[]{:S(2)}, u32[]{:S(2)}) collective-permute-start(f32[128,896]{1,0:T(8,128)S(1)} %get-tuple-element.15), channel_id=1, source_target_pairs={{0,4},{4,8},{8,12},{12,16},{16,20},{20,24},{24,28},{28,0},{1,5},{5... | collective-permute-start | bytes 1376264 | tf_op jit(solution)/shard_map/ppermute | solution.py:36
  41.5 24.8 %collective-permute-start.3 = (f32[128,896]{1,0:T(8,128)S(1)}, f32[128,896]{1,0:T(8,128)S(1)}, u32[]{:S(2)}, u32[]{:S(2)}) collective-permute-start(f32[128,896]{1,0:T(8,128)S(1)} %get-tuple-element.14.refs_0_), channel_id=1, source_target_pairs={{0,28},{4,0},{8,4},{12,8},{16,12},{20,16},{24,20},{28,24},{1,29},{... | collective-permute-start | bytes 1376264 | tf_op jit(solution)/shard_map/ppermute | solution.py:36
  45.8 16.1 %collective-permute-start.5 = (f32[32,896]{1,0:T(8,128)S(1)}, f32[32,896]{1,0:T(8,128)S(1)}, u32[]{:S(2)}, u32[]{:S(2)}) collective-permute-start(f32[32,896]{1,0:T(8,128)S(1)} %get-tuple-element.16), channel_id=1, source_target_pairs={{0,24},{4,28},{8,0},{12,4},{16,8},{20,12},{24,16},{28,20},{1,25},{... | collective-permute-start | bytes 344072 | tf_op jit(solution)/shard_map/ppermute | solution.py:36
  49.4 12.5 %collective-permute-start.6 = (f32[32,896]{1,0:T(8,128)S(1)}, f32[32,896]{1,0:T(8,128)S(1)}, u32[]{:S(2)}, u32[]{:S(2)}) collective-permute-start(f32[32,896]{1,0:T(8,128)S(1)} %get-tuple-element.17), channel_id=1, source_target_pairs={{0,8},{4,12},{8,16},{12,20},{16,24},{20,28},{24,0},{28,4},{1,9},{5... | collective-permute-start | bytes 344072 | tf_op jit(solution)/shard_map/ppermute | solution.py:36
  52.6 17.1 %collective-permute-start.7 = (f32[128,896]{1,0:T(8,128)S(1)}, f32[128,896]{1,0:T(8,128)S(1)}, u32[]{:S(2)}, u32[]{:S(2)}) collective-permute-start(f32[128,896]{1,0:T(8,128)S(1)} %get-tuple-element.14.refs_0_), channel_id=1, source_target_pairs={{0,1},{1,0},{2,3},{3,2},{4,5},{5,4},{6,7},{7,6},{8,9},{9,8},{10,11... | collective-permute-start | bytes 1376264 | tf_op jit(solution)/shard_map/ppermute | solution.py:239
  61.9 7.7 %collective-permute-start.10 = (f32[128,896]{1,0:T(8,128)S(1)}, f32[128,896]{1,0:T(8,128)S(1)}, u32[]{:S(2)}, u32[]{:S(2)}) collective-permute-start(f32[128,896]{1,0:T(8,128)S(1)} %shard_map.64.refs_3_), channel_id=1, source_target_pairs={{0,1},{1,0},{2,3},{3,2},{4,5},{5,4},{6,7},{7,6},{8,9},{9,8},{10,11... | collective-permute-start | bytes 1376264 | tf_op jit(solution)/shard_map/ppermute | solution.py:239
  63.9 5.8 %collective-permute-start.9 = (f32[128,896]{1,0:T(8,128)S(1)}, f32[128,896]{1,0:T(8,128)S(1)}, u32[]{:S(2)}, u32[]{:S(2)}) collective-permute-start(f32[128,896]{1,0:T(8,128)S(1)} %collective-permute-done.4.refs_2_), channel_id=1, source_target_pairs={{0,1},{1,0},{2,3},{3,2},{4,5},{5,4},{6,7},{7,6},{8,9},{9,8},{10,11... | collective-permute-start | bytes 1376264 | tf_op jit(solution)/shard_map/ppermute | solution.py:239
  66.3 3.8 %collective-permute-start.8 = (f32[128,896]{1,0:T(8,128)S(1)}, f32[128,896]{1,0:T(8,128)}, u32[]{:S(2)}, u32[]{:S(2)}) collective-permute-start(f32[128,896]{1,0:T(8,128)S(1)} %collective-permute-done.3.refs_1_), channel_id=1, source_target_pairs={{0,1},{1,0},{2,3},{3,2},{4,5},{5,4},{6,7},{7,6},{8,9},{9,8},{10,11... | collective-permute-start | bytes 1376264 | tf_op jit(solution)/shard_map/ppermute | solution.py:239
  70.1 32.2 %copy-start.1 = (f32[1,28,896]{2,0,1:T(1,128)S(1)}, f32[1,28,896]{2,0,1:T(1,128)}, u32[]{:S(2)}) copy-start(f32[1,28,896]{2,0,1:T(1,128)} %param.7) | copy-start | bytes 301060
  70.1 32.2 %copy-start.3 = (s32[1,8]{1,0:T(1,128)S(1)}, s32[1,8]{1,0:T(1,128)}, u32[]{:S(2)}) copy-start(s32[1,8]{1,0:T(1,128)} %pattern.3) | copy-start | bytes 100

commit v5 on v4

--- a/solution.py
+++ b/solution.py
@@ -23,13 +23,13 @@
 HALF = COLS // 2
 PIECE3 = COLS + HALF
 VMEM_LIMIT = 16 * 1024 * 1024
-CROSS_LIMIT = 16 * 1024 * 1024
+SPREAD_LIMIT = 63 * 1024 * 1024
 
 
 GRID = ("prow", "side", "core")
 
 
-STEPS = ((0, 2), (1, 3), (-1, -3), (-2, 4))
+STEPS = (0, 2, -2, 1, 3, -1, -3, 4)
 
 
 def from_row(value, distance):
@@ -54,11 +54,19 @@
     return high, low
 
 
-def spread_kernel(ancestor, pattern, out):
-    row = pattern[...].astype(jnp.float32)
+def spread_kernel(ancestor, pattern, out, panel, numbers, semaphores):
+    copies = [
+        pltpu.make_async_copy(ancestor, panel, semaphores.at[0]),
+        pltpu.make_async_copy(pattern, numbers, semaphores.at[1]),
+    ]
+    for copy in copies:
+        copy.start()
+    for copy in copies:
+        copy.wait()
+    row = numbers[...].astype(jnp.float32)
     for leaf in range(N_LEAF):
         for block in range(OWN_BLOCKS):
-            out[leaf, block * CHUNK:(block + 1) * CHUNK, :] = ancestor[
+            out[leaf, block * CHUNK:(block + 1) * CHUNK, :] = panel[
                 leaf * CHUNK:(leaf + 1) * CHUNK, block * BLK:(block + 1) * BLK
             ]
         out[leaf, PAT_ROW:PIECE1, :] = jnp.zeros((PIECE1 - PAT_ROW, BLK), jnp.float32)
@@ -78,14 +86,12 @@
         first += rows
 
 
-def near_kernel(pair, ahead, behind, up, down, up_half, down_half):
-    stack(up, pair, ahead)
-    stack(down, pair, behind)
-    up_half[...] = ahead[0:LROWS, :]
-    down_half[...] = behind[LROWS:2 * LROWS, :]
-
-
-def far_kernel(*refs):
+def near_kernel(pair, ahead, behind, near, rear):
+    stack(near, pair, ahead, behind)
+    rear[...] = behind[...]
+
+
+def join_kernel(*refs):
     stack(refs[-1], *refs[:-1])
 
 
@@ -116,38 +122,65 @@
         copy.wait()
 
 
-def panel_kernel(pieces, high, low, panel):
+def by_core(first, second):
+    lane = lax.broadcasted_iota(jnp.int32, first.shape, 1)
+
+    def even(value):
+        return jnp.where(lane < 32, value, pltpu.roll(value, 96, 1))
+
+    def odd(value):
+        return jnp.where(lane < 32, pltpu.roll(value, 96, 1), pltpu.roll(value, 64, 1))
+
+    cores = [
+        jnp.where(lane < 64, pick(first), pltpu.roll(pick(second), 64, 1)) for pick in (even, odd)
+    ]
+    swap = lax.axis_index("core") == 1
+    return jnp.where(swap, cores[1], cores[0]), jnp.where(swap, cores[0], cores[1])
+
+
+def order_rows(source, high_out, low_out):
+    side = lax.axis_index("side")
+    place = lax.axis_index("prow")
+    for group, step in enumerate(STEPS):
+        block = lax.rem(place + step + NP, NP)
+        for part, at_side in ((0, side), (1, 1 - side)):
+            row = group * 64 + part * LROWS
+            high, low = split(source[row:row + LROWS, :])
+            first = pl.multiple_of(block * 64 + at_side * LROWS, LROWS)
+            high_out[pl.ds(first, LROWS), :] = high
+            low_out[pl.ds(first, LROWS), :] = low
+
+
+def multiply(high, low, lower_high, lower_low):
+    def dot(a, b):
+        return jnp.dot(a[...], b[...], preferred_element_type=jnp.float32)
+
+    return dot(high, lower_high) + (dot(low, lower_high) + dot(high, lower_low))
+
+
+def own_kernel(
+    pieces, lower, partial, other_high, other_low, lower_high, lower_low, panel, own_high, own_low
+):
     for leaf in range(N_LEAF):
         for block in range(NP):
             panel[leaf * CHUNK:(leaf + 1) * CHUNK, block * BLK:(block + 1) * BLK] = pieces[
                 leaf, block * CHUNK:(block + 1) * CHUNK, :
             ]
-    high[...], low[...] = split(panel[...])
-
-
-def cross_kernel(panel_high, panel_low, *refs):
-    sources = refs[:2 * len(STEPS)]
-    cross, out, lower_high, lower_low, product = refs[2 * len(STEPS):]
+    for at in range(NP // 2):
+        here = slice(at * BLK, (at + 1) * BLK)
+        own, other = by_core(
+            panel[:, 2 * at * BLK:(2 * at + 1) * BLK], panel[:, (2 * at + 1) * BLK:(2 * at + 2) * BLK]
+        )
+        own_high[:, here], own_low[:, here] = split(own)
+        other_high[:, here], other_low[:, here] = split(other)
+    order_rows(lower, lower_high, lower_low)
+    partial[...] = multiply(own_high, own_low, lower_high, lower_low)
+
+
+def cross_kernel(partial, high, low, lower, cross, out, lower_high, lower_low, product):
     core = lax.axis_index("core")
-    side = lax.axis_index("side")
-    place = lax.axis_index("prow")
-    for at, source in enumerate(sources):
-        at_core = core if at < len(STEPS) else 1 - core
-        for group, step in enumerate(STEPS[at % len(STEPS)]):
-            block = lax.rem(place + step + NP, NP)
-            for part, at_side in ((0, side), (1, 1 - side)):
-                row = group * 64 + part * LROWS
-                high, low = split(source[row:row + LROWS, :])
-                first = pl.multiple_of(block * BLK + at_side * 64 + at_core * LROWS, LROWS)
-                lower_high[pl.ds(first, LROWS), :] = high
-                lower_low[pl.ds(first, LROWS), :] = low
-
-    def dot(a, b):
-        return jnp.dot(a, b, preferred_element_type=jnp.float32)
-
-    value = dot(panel_high[...], lower_high[...]) + (
-        dot(panel_low[...], lower_high[...]) + dot(panel_high[...], lower_low[...])
-    )
+    order_rows(lower, lower_high, lower_low)
+    value = partial[...] + multiply(high, low, lower_high, lower_low)
     product[...] = value
     cross[0, :, :] = -value
     whole = product[pl.ds(pl.multiple_of(core * 64, 64), BLK), :].T
@@ -160,8 +193,11 @@
         out[first + COLS:first + PIECE3, 64:128] = half[at + HALF:at + COLS, :]
 
 
-def diagonal_kernel(pattern, pieces, lower_high, lower_low, child, out, rows):
+def diagonal_kernel(
+    pattern, pieces, own_high, own_low, other_high, other_low, child, out, rows, *parts
+):
     lane = lax.broadcasted_iota(jnp.int32, (HALF, BLK), 1)
+    rows[:, COLS:, :] = jnp.zeros((NP, 32 - COLS, BLK), jnp.float32)
     for block in range(NP):
         number = pattern[0, block]
         group = number // 3
@@ -173,16 +209,16 @@
         second = pieces[pl.ds((upper + 1) * PIECE3 + COLS, HALF), :]
         top = jnp.where(lane < 64, first, pltpu.roll(second, 64, 1))
         bottom = jnp.where(lane < 64, pltpu.roll(first, 64, 1), second)
-        here = slice(block * BLK, (block + 1) * BLK)
-        rows[0:HALF, here] = jnp.where(middle, top, whole[0:HALF, :])
-        rows[HALF:COLS, here] = jnp.where(middle, bottom, whole[HALF:COLS, :])
-    rows[COLS:, :] = jnp.zeros((32 - COLS, NP * BLK), jnp.float32)
-    high, low = split(rows[...])
-
-    def dot(a, b):
-        return jnp.dot(a, b, preferred_element_type=jnp.float32)
-
-    update = dot(high, lower_high[...]) + (dot(low, lower_high[...]) + dot(high, lower_low[...]))
+        rows[block, 0:HALF, :] = jnp.where(middle, top, whole[0:HALF, :])
+        rows[block, HALF:COLS, :] = jnp.where(middle, bottom, whole[HALF:COLS, :])
+    for at in range(NP // 2):
+        here = slice(at * BLK, (at + 1) * BLK)
+        own, other = by_core(rows[2 * at], rows[2 * at + 1])
+        parts[0][:, here], parts[1][:, here] = split(own)
+        parts[2][:, here], parts[3][:, here] = split(other)
+    update = multiply(parts[0], parts[1], own_high, own_low) + multiply(
+        parts[2], parts[3], other_high, other_low
+    )
     for row in range(COLS):
         out[row, 0:1, :] = child[row, 0:1, :] + update[row:row + 1, :]
 
@@ -204,9 +240,14 @@
     spread = pl.pallas_call(
         spread_kernel,
         out_shape=jax.ShapeDtypeStruct((N_LEAF, PIECE1, BLK), jnp.float32),
-        in_specs=in_vmem(2),
+        in_specs=[pl.BlockSpec(memory_space=pl.ANY)] * 2,
         out_specs=in_vmem(1)[0],
-        compiler_params=params,
+        scratch_shapes=[
+            pltpu.VMEM((ROWS, OWN_BLOCKS * BLK), jnp.float32),
+            pltpu.VMEM((1, NP), jnp.int32),
+            pltpu.SemaphoreType.DMA((2,)),
+        ],
+        compiler_params=pltpu.CompilerParams(vmem_limit_bytes=SPREAD_LIMIT),
     )(ancestor_inverse, pattern)
     across = swap_side(own)
     pair = pl.pallas_call(
@@ -233,44 +274,71 @@
         compiler_params=params,
     )(spread)
     chosen = lax.all_to_all(chosen, "leaf", 0, 0, tiled=True)
-    up, down, up_half, down_half = call(near_kernel, (128, 128, 32, 32), 2000, pair, ahead, behind)
-    (far,) = call(far_kernel, (128,), 0, behind, from_row(up_half, 2), from_row(down_half, -2))
-    mine = [up, from_row(up, 1), from_row(down, -1), far]
-    other = [lax.ppermute(value, "core", [(0, 1), (1, 0)]) for value in mine]
-    panel_high, panel_low = pl.pallas_call(
-        panel_kernel,
-        out_shape=(jax.ShapeDtypeStruct((ROWS, NP * BLK), jnp.bfloat16),) * 2,
-        in_specs=in_vmem(1),
-        out_specs=tuple(in_vmem(2)),
-        scratch_shapes=[pltpu.VMEM((ROWS, NP * BLK), jnp.float32)],
-        compiler_params=params,
-    )(chosen)
-    cross, pieces, lower_high, lower_low = pl.pallas_call(
+    near, rear = call(near_kernel, (192, 64), 2000, pair, ahead, behind)
+    (lower,) = call(
+        join_kernel,
+        (NP * 64,),
+        0,
+        near,
+        from_row(near, 1),
+        from_row(rear, -1),
+        from_row(rear, -2),
+    )
+    lower, chosen = lax.optimization_barrier((lower, chosen))
+    lower_other = lax.ppermute(lower, "core", [(0, 1), (1, 0)])
+    lower_shape = jax.ShapeDtypeStruct((NP * 64, S1), jnp.bfloat16)
+    panel_shape = jax.ShapeDtypeStruct((ROWS, NP * 64), jnp.bfloat16)
+    partial, panel_high, panel_low, own_high, own_low = pl.pallas_call(
+        own_kernel,
+        out_shape=(
+            jax.ShapeDtypeStruct((ROWS, S1), jnp.float32),
+            panel_shape,
+            panel_shape,
+            lower_shape,
+            lower_shape,
+        ),
+        in_specs=in_vmem(2),
+        out_specs=tuple(in_vmem(5)),
+        scratch_shapes=[
+            pltpu.VMEM((ROWS, NP * BLK), jnp.float32),
+            pltpu.VMEM((ROWS, NP * 64), jnp.bfloat16),
+            pltpu.VMEM((ROWS, NP * 64), jnp.bfloat16),
+        ],
+        compiler_params=params,
+    )(chosen, lower)
+    cross, pieces, other_high, other_low = pl.pallas_call(
         cross_kernel,
         out_shape=(
             jax.ShapeDtypeStruct((1, ROWS, S1), jnp.float32),
             jax.ShapeDtypeStruct((N_GRID * PIECE3, BLK), jnp.float32),
-            jax.ShapeDtypeStruct((NP * BLK, S1), jnp.bfloat16),
-            jax.ShapeDtypeStruct((NP * BLK, S1), jnp.bfloat16),
+            lower_shape,
+            lower_shape,
         ),
-        in_specs=in_vmem(10),
+        in_specs=in_vmem(4),
         out_specs=tuple(in_vmem(4)),
-        scratch_shapes=[
-            pltpu.VMEM((ROWS, S1), jnp.float32),
-        ],
-        compiler_params=pltpu.CompilerParams(vmem_limit_bytes=CROSS_LIMIT),
-    )(panel_high, panel_low, *mine, *other)
+        scratch_shapes=[pltpu.VMEM((ROWS, S1), jnp.float32)],
+        compiler_params=params,
+    )(partial, panel_high, panel_low, lower_other)
     pieces = lax.all_to_all(
         pieces.reshape(N_GRID, PIECE3, 1, BLK), GRID, 0, 0, tiled=True
     ).reshape(N_GRID * PIECE3, BLK)
     diagonal = pl.pallas_call(
         diagonal_kernel,
         out_shape=jax.ShapeDtypeStruct((COLS, 1, S1), jnp.float32),
-        in_specs=[pl.BlockSpec(memory_space=pltpu.SMEM)] + in_vmem(4),
+        in_specs=[pl.BlockSpec(memory_space=pltpu.SMEM)] + in_vmem(6),
         out_specs=in_vmem(1)[0],
-        scratch_shapes=[pltpu.VMEM((32, NP * BLK), jnp.float32)],
-        compiler_params=params,
-    )(pattern, pieces, lower_high, lower_low, jnp.transpose(child_diag_inv, (1, 0, 2)))
+        scratch_shapes=[pltpu.VMEM((NP, 32, BLK), jnp.float32)]
+        + [pltpu.VMEM((32, NP * 64), jnp.bfloat16)] * 4,
+        compiler_params=params,
+    )(
+        pattern,
+        pieces,
+        own_high,
+        own_low,
+        other_high,
+        other_low,
+        jnp.transpose(child_diag_inv, (1, 0, 2)),
+    )
     return cross, jnp.transpose(diagonal, (1, 0, 2))
 
 

time: 105 us -> 100 us (0.952)
  starting transfers between devices: 52 us -> 42.8 us
  waiting for transfers between devices: 9.82 us -> 15.6 us
  local copies, waits for them, and re-layouts: 2.51 us -> 0.9 us
    ppermute x4 -> x1, starting transfers between devices: 8.17 us -> 1.92 us  [shards(): lower_other = lax.ppermute(lower, 'core', [(0, 1), (1, 0)])]
    ppermute x6 -> x5, waiting for transfers between devices: 8 us -> 13.2 us  [from_row(): lax.ppermute(value, 'prow', [(at, (at - distance) % NP) for at in range(N...]
    ppermute x6 -> x5, starting transfers between devices: 21.9 us -> 18.9 us  [from_row(): lax.ppermute(value, 'prow', [(at, (at - distance) % NP) for at in range(N...]
    pallas_call x1, Pallas kernels: 3.85 us -> 1.99 us  [shards(): pl.pallas_call(cross_kernel, out_shape=(jax.ShapeDtypeStruct((1, ROWS, S1...]
    unnamed x10 -> x6, local copies, waits for them, and re-layouts: 2.51 us -> 0.9 us
    pallas_call x1, Pallas kernels: 1.4 us -> 2.69 us  [shards(): pl.pallas_call(own_kernel, out_shape=(jax.ShapeDtypeStruct((ROWS, S1), jn...]
  transfers between devices with their start and end apart: 13 -> 9, of which waited for: 4 -> 5; matrix products, arithmetic and copies ran while one was open for 0% -> 0% of each run, Pallas kernels for 5% -> 7%
where the time goes in v5:
time: 100 us; the launch traced here: 99.9 us
  starting transfers between devices  42.8 us (43%)
  blocking collectives  28.2 us (28%)
  waiting for transfers between devices  15.6 us (16%)
  Pallas kernels  11.7 us (12%)
    all_to_all x1, blocking collectives, shards(): lax.all_to_all(pieces.reshape(N_GRID, PIECE3, 1, BLK), GRID, 0, 0, tiled=...  28.2 us
    ppermute x5, starting transfers between devices, from_row(): lax.ppermute(value, 'prow', [(at, (at - distance) % NP) for at in range(N...  18.9 us
    ppermute x5, waiting for transfers between devices, from_row(): lax.ppermute(value, 'prow', [(at, (at - distance) % NP) for at in range(N...  13.2 us
    all_to_all x1, starting transfers between devices, shards(): spread = lax.all_to_all(spread, 'leaf', 0, 0, tiled=True)  11.8 us
    all_to_all x1, starting transfers between devices, shards(): chosen = lax.all_to_all(chosen, 'leaf', 0, 0, tiled=True)  6.81 us
    ppermute x1, starting transfers between devices, swap_side(): return lax.ppermute(value, 'side', [(0, 1), (1, 0)])  3.32 us
    pallas_call x1, Pallas kernels, shards(): pl.pallas_call(select_kernel, out_shape=jax.ShapeDtypeStruct((N_LEAF, PIE...  2.74 us
    pallas_call x1, Pallas kernels, shards(): pl.pallas_call(own_kernel, out_shape=(jax.ShapeDtypeStruct((ROWS, S1), jn...  2.69 us
  transfers between devices with their start and end apart: 9, of which 5 were waited for; matrix products, arithmetic and copies ran while one was open for 0% of the time, Pallas kernels for 7%

profile of v5, /device:TPU:6, one launch (start us, length us, event | category | flops | bytes accessed | tf_op | source)
XLA Modules:
  0.0 99.9 jit_solution(5132219341282951742)
XLA Ops:
  0.6 3.3 %collective-permute-start = (f32[32,896]{1,0:T(8,128)}, f32[32,896]{1,0:T(8,128)S(1)}, u32[]{:S(2)}, u32[]{:S(2)}) collective-permute-start(f32[32,896]{1,0:T(8,128)} %bitcast.8), channel_id=1, source_target_pairs={{0,2},{2,0},{1,3},{3,1},{4,6},{6,4},{5,7},{7,5},{8,10},{10,8},{9,1... | collective-permute-start | bytes 344072 | tf_op jit(solution)/shard_map/ppermute | solution.py:40
  4.0 1.7 %shard_map.62 = f32[16,40,128]{2,1,0:T(8,128)} custom-call(f32[192,384]{1,0:T(8,128)} %ancestor.1, s32[1,8]{1,0:T(1,128)} %pattern.3), custom_call_target="tpu_custom_call" | custom-call | tf_op jit(solution)/shard_map/pallas_call | solution.py:240
  5.7 11.8 %all-to-all-start = ((f32[16,40,128]{2,1,0:T(8,128)}), f32[16,40,128]{2,1,0:T(8,128)}, u32[]{:S(2)}, u32[]{:S(2)}) async-start(f32[16,40,128]{2,1,0:T(8,128)} %shard_map.62), calls=%async_computation | async-start | bytes 655360 | tf_op jit(solution)/shard_map/all_to_all | solution.py:262
  17.5 0.0 collective-permute-done.across
  17.5 0.0 copy-start.2
  17.5 0.9 copy-done.2
  18.4 4.5 %collective-permute-start.2 = (f32[64,896]{1,0:T(8,128)S(1)}, f32[64,896]{1,0:T(8,128)S(1)}, u32[]{:S(2)}, u32[]{:S(2)}) collective-permute-start(f32[64,896]{1,0:T(8,128)S(1)} %shard_map.59.pair), channel_id=1, source_target_pairs={{0,8},{4,12},{8,16},{12,20},{16,24},{20,28},{24,0},{28,4},{1,9},{5... | collective-permute-start | bytes 688136 | tf_op jit(solution)/shard_map/ppermute | solution.py:36
  22.9 3.6 %collective-permute-start.1 = (f32[64,896]{1,0:T(8,128)S(1)}, f32[64,896]{1,0:T(8,128)S(1)}, u32[]{:S(2)}, u32[]{:S(2)}) collective-permute-start(f32[64,896]{1,0:T(8,128)S(1)} %shard_map.59.pair), channel_id=1, source_target_pairs={{0,24},{4,28},{8,0},{12,4},{16,8},{20,12},{24,16},{28,20},{1,25},{... | collective-permute-start | bytes 688136 | tf_op jit(solution)/shard_map/ppermute | solution.py:36
  26.5 1.3 %all-to-all-done.pieces = f32[16,40,128]{2,1,0:T(8,128)} async-done(((f32[16,40,128]{2,1,0:T(8,128)}), f32[16,40,128]{2,1,0:T(8,128)}, u32[]{:S(2)}, u32[]{:S(2)}) %all-to-all-start) | async-done | bytes 327712 | tf_op jit(solution)/shard_map/all_to_all | solution.py:262
  27.9 2.7 %shard_map.63 = f32[16,96,128]{2,1,0:T(8,128)} custom-call(f32[16,40,128]{2,1,0:T(8,128)} %all-to-all-done.pieces), custom_call_target="tpu_custom_call" | custom-call | tf_op jit(solution)/shard_map/pallas_call | solution.py:263
  30.6 6.8 %all-to-all-start.1 = ((f32[16,96,128]{2,1,0:T(8,128)}), f32[16,96,128]{2,1,0:T(8,128)}, u32[]{:S(2)}, u32[]{:S(2)}) async-start(f32[16,96,128]{2,1,0:T(8,128)} %shard_map.63), calls=%async_computation.1 | async-start | bytes 1572864 | tf_op jit(solution)/shard_map/all_to_all | solution.py:276
  37.4 0.0 collective-permute-done.2.behind
  37.4 0.6 collective-permute-done.1.ahead
  38.0 0.1 shard_map.60
  38.1 3.5 %collective-permute-start.3 = (f32[192,896]{1,0:T(8,128)S(1)}, f32[192,896]{1,0:T(8,128)S(1)}, u32[]{:S(2)}, u32[]{:S(2)}) collective-permute-start(f32[192,896]{1,0:T(8,128)S(1)} %get-tuple-element.15.refs_0_), channel_id=1, source_target_pairs={{0,28},{4,0},{8,4},{12,8},{16,12},{20,16},{24,20},{28,24},{1,29},{... | collective-permute-start | bytes 2064392 | tf_op jit(solution)/shard_map/ppermute | solution.py:36
  41.6 3.4 %collective-permute-start.5 = (f32[64,896]{1,0:T(8,128)S(1)}, f32[64,896]{1,0:T(8,128)S(1)}, u32[]{:S(2)}, u32[]{:S(2)}) collective-permute-start(f32[64,896]{1,0:T(8,128)S(1)} %get-tuple-element.16), channel_id=1, source_target_pairs={{0,8},{4,12},{8,16},{12,20},{16,24},{20,28},{24,0},{28,4},{1,9},{5... | collective-permute-start | bytes 688136 | tf_op jit(solution)/shard_map/ppermute | solution.py:36
  45.0 3.9 %collective-permute-start.4 = (f32[64,896]{1,0:T(8,128)S(1)}, f32[64,896]{1,0:T(8,128)S(1)}, u32[]{:S(2)}, u32[]{:S(2)}) collective-permute-start(f32[64,896]{1,0:T(8,128)S(1)} %get-tuple-element.16), channel_id=1, source_target_pairs={{0,4},{4,8},{8,12},{12,16},{16,20},{20,24},{24,28},{28,0},{1,5},{5... | collective-permute-start | bytes 688136 | tf_op jit(solution)/shard_map/ppermute | solution.py:36
  48.9 9.0 %collective-permute-done.5.refs_3_ = f32[64,896]{1,0:T(8,128)S(1)} collective-permute-done((f32[64,896]{1,0:T(8,128)S(1)}, f32[64,896]{1,0:T(8,128)S(1)}, u32[]{:S(2)}, u32[]{:S(2)}) %collective-permute-start.5) | collective-permute-done | bytes 229408 | tf_op jit(solution)/shard_map/ppermute | solution.py:36
  58.0 3.5 %collective-permute-done.4.refs_2_ = f32[64,896]{1,0:T(8,128)S(1)} collective-permute-done((f32[64,896]{1,0:T(8,128)S(1)}, f32[64,896]{1,0:T(8,128)S(1)}, u32[]{:S(2)}, u32[]{:S(2)}) %collective-permute-start.4) | collective-permute-done | bytes 229408 | tf_op jit(solution)/shard_map/ppermute | solution.py:36
  61.5 0.0 collective-permute-done.3.refs_1_
  61.5 0.1 shard_map.61.lower
  61.6 0.0 all-to-all-done.1.pieces
  61.7 1.9 %collective-permute-start.6 = (f32[512,896]{1,0:T(8,128)S(1)}, f32[512,896]{1,0:T(8,128)S(1)}, u32[]{:S(2)}, u32[]{:S(2)}) collective-permute-start(f32[512,896]{1,0:T(8,128)S(1)} %shard_map.61.lower), channel_id=1, source_target_pairs={{0,1},{1,0},{2,3},{3,2},{4,5},{5,4},{6,7},{7,6},{8,9},{9,8},{10,11... | collective-permute-start | bytes 5505032 | tf_op jit(solution)/shard_map/ppermute | solution.py:288
  63.6 2.7 %shard_map.64 = (f32[192,896]{1,0:T(8,128)S(1)}, bf16[192,512]{1,0:T(8,128)(2,1)S(1)}, bf16[192,512]{1,0:T(8,128)(2,1)S(1)}, bf16[512,896]{1,0:T(8,128)(2,1)S(1)}, bf16[512,896]{1,0:T(8,128)(2,1)S(1)}) custom-call(f32[16,96,128]{2,1,0:T(8,128)} %all-to-all-done.1.pieces, f32[512,896]{1,0:T(8,128)S(1)} %shard_map.61.lower), custom_call_target="tpu_custom_call" | custom-call | tf_op jit(solution)/shard_map/pallas_call | solution.py:291
  66.3 1.1 %collective-permute-done.6.lower = f32[512,896]{1,0:T(8,128)S(1)} collective-permute-done((f32[512,896]{1,0:T(8,128)S(1)}, f32[512,896]{1,0:T(8,128)S(1)}, u32[]{:S(2)}, u32[]{:S(2)}) %collective-permute-start.6) | collective-permute-done | bytes 1835040 | tf_op jit(solution)/shard_map/ppermute | solution.py:288
  67.3 0.0 copy-start
  67.3 0.0 copy-start.1
  67.3 2.0 %shard_map.65 = (f32[1,192,896]{2,1,0:T(8,128)}, f32[1344,128]{1,0:T(8,128)S(1)}, bf16[512,896]{1,0:T(8,128)(2,1)S(1)}, bf16[512,896]{1,0:T(8,128)(2,1)S(1)}) custom-call(f32[192,896]{1,0:T(8,128)S(1)} %get-tuple-element.19.partial, bf16[192,512]{1,0:T(8,128)(2,1)S(1)} %get-tuple-element.20.high, bf16[192,512]{1,0:T(8,128)(2,1)S(1)} %get-tuple-element.21.low, ...), custom_call_target="tpu_custom_call" | custom-call | tf_op jit(solution)/shard_map/pallas_call | solution.py:309
  69.3 28.2 %all_to_all.15 = f32[32,42,1,128]{3,2,1,0:T(1,128)S(1)} all-to-all(f32[32,42,1,128]{3,2,1,0:T(1,128)S(1)} %bitcast.6), channel_id=1, replica_groups=mesh['leaf'=16,'prow'=8,'side'=2,'core'=2] {'prow','side','core'}, dimensions={0} | all-to-all | bytes 1376256 | tf_op jit(solution)/shard_map/all_to_all | solution.py:322
  97.6 0.0 copy-done
  97.6 0.0 copy-done.1
  97.6 2.3 %shard_map.66 = f32[28,1,896]{2,1,0:T(1,128)} custom-call(s32[1,8]{1,0:T(1,128)S(1)} %copy-done.1, f32[1344,128]{1,0:T(8,128)S(1)} %bitcast.5, bf16[512,896]{1,0:T(8,128)(2,1)S(1)} %get-tuple-element.24.own_high, bf16[512,896]{1,0:T(8,128)(2,1)S(1)} %get-tuple-element.25.own_low, bf16[512,896]{1,0:T(8,128)(2,1)S(1)} %get-tuple-element.26.other_high, ...), custom_call_target="tpu_custom_call" | custom-call | tf_op jit(solution)/shard_map/pallas_call | solution.py:325
  (1 shorter events, 0.0 us)
Async XLA Ops:
  0.6 16.9 %collective-permute-start = (f32[32,896]{1,0:T(8,128)}, f32[32,896]{1,0:T(8,128)S(1)}, u32[]{:S(2)}, u32[]{:S(2)}) collective-permute-start(f32[32,896]{1,0:T(8,128)} %bitcast.8), channel_id=1, source_target_pairs={{0,2},{2,0},{1,3},{3,1},{4,6},{6,4},{5,7},{7,5},{8,10},{10,8},{9,1... | collective-permute-start | bytes 344072 | tf_op jit(solution)/shard_map/ppermute | solution.py:40
  5.7 22.2 %all-to-all-start = ((f32[16,40,128]{2,1,0:T(8,128)}), f32[16,40,128]{2,1,0:T(8,128)}, u32[]{:S(2)}, u32[]{:S(2)}) async-start(f32[16,40,128]{2,1,0:T(8,128)} %shard_map.62), calls=%async_computation | async-start | bytes 655360 | tf_op jit(solution)/shard_map/all_to_all | solution.py:262
  17.5 0.9 copy-start.2
  18.4 19.0 %collective-permute-start.2 = (f32[64,896]{1,0:T(8,128)S(1)}, f32[64,896]{1,0:T(8,128)S(1)}, u32[]{:S(2)}, u32[]{:S(2)}) collective-permute-start(f32[64,896]{1,0:T(8,128)S(1)} %shard_map.59.pair), channel_id=1, source_target_pairs={{0,8},{4,12},{8,16},{12,20},{16,24},{20,28},{24,0},{28,4},{1,9},{5... | collective-permute-start | bytes 688136 | tf_op jit(solution)/shard_map/ppermute | solution.py:36
  22.9 15.1 %collective-permute-start.1 = (f32[64,896]{1,0:T(8,128)S(1)}, f32[64,896]{1,0:T(8,128)S(1)}, u32[]{:S(2)}, u32[]{:S(2)}) collective-permute-start(f32[64,896]{1,0:T(8,128)S(1)} %shard_map.59.pair), channel_id=1, source_target_pairs={{0,24},{4,28},{8,0},{12,4},{16,8},{20,12},{24,16},{28,20},{1,25},{... | collective-permute-start | bytes 688136 | tf_op jit(solution)/shard_map/ppermute | solution.py:36
  30.6 31.0 %all-to-all-start.1 = ((f32[16,96,128]{2,1,0:T(8,128)}), f32[16,96,128]{2,1,0:T(8,128)}, u32[]{:S(2)}, u32[]{:S(2)}) async-start(f32[16,96,128]{2,1,0:T(8,128)} %shard_map.63), calls=%async_computation.1 | async-start | bytes 1572864 | tf_op jit(solution)/shard_map/all_to_all | solution.py:276
  38.1 23.4 %collective-permute-start.3 = (f32[192,896]{1,0:T(8,128)S(1)}, f32[192,896]{1,0:T(8,128)S(1)}, u32[]{:S(2)}, u32[]{:S(2)}) collective-permute-start(f32[192,896]{1,0:T(8,128)S(1)} %get-tuple-element.15.refs_0_), channel_id=1, source_target_pairs={{0,28},{4,0},{8,4},{12,8},{16,12},{20,16},{24,20},{28,24},{1,29},{... | collective-permute-start | bytes 2064392 | tf_op jit(solution)/shard_map/ppermute | solution.py:36
  41.6 16.4 %collective-permute-start.5 = (f32[64,896]{1,0:T(8,128)S(1)}, f32[64,896]{1,0:T(8,128)S(1)}, u32[]{:S(2)}, u32[]{:S(2)}) collective-permute-start(f32[64,896]{1,0:T(8,128)S(1)} %get-tuple-element.16), channel_id=1, source_target_pairs={{0,8},{4,12},{8,16},{12,20},{16,24},{20,28},{24,0},{28,4},{1,9},{5... | collective-permute-start | bytes 688136 | tf_op jit(solution)/shard_map/ppermute | solution.py:36
  45.0 16.5 %collective-permute-start.4 = (f32[64,896]{1,0:T(8,128)S(1)}, f32[64,896]{1,0:T(8,128)S(1)}, u32[]{:S(2)}, u32[]{:S(2)}) collective-permute-start(f32[64,896]{1,0:T(8,128)S(1)} %get-tuple-element.16), channel_id=1, source_target_pairs={{0,4},{4,8},{8,12},{12,16},{16,20},{20,24},{24,28},{28,0},{1,5},{5... | collective-permute-start | bytes 688136 | tf_op jit(solution)/shard_map/ppermute | solution.py:36
  61.7 5.7 %collective-permute-start.6 = (f32[512,896]{1,0:T(8,128)S(1)}, f32[512,896]{1,0:T(8,128)S(1)}, u32[]{:S(2)}, u32[]{:S(2)}) collective-permute-start(f32[512,896]{1,0:T(8,128)S(1)} %shard_map.61.lower), channel_id=1, source_target_pairs={{0,1},{1,0},{2,3},{3,2},{4,5},{5,4},{6,7},{7,6},{8,9},{9,8},{10,11... | collective-permute-start | bytes 5505032 | tf_op jit(solution)/shard_map/ppermute | solution.py:288
  67.3 30.2 %copy-start = (f32[1,28,896]{2,0,1:T(1,128)S(1)}, f32[1,28,896]{2,0,1:T(1,128)}, u32[]{:S(2)}) copy-start(f32[1,28,896]{2,0,1:T(1,128)} %param.7) | copy-start | bytes 301060
  67.3 30.2 %copy-start.1 = (s32[1,8]{1,0:T(1,128)S(1)}, s32[1,8]{1,0:T(1,128)}, u32[]{:S(2)}) copy-start(s32[1,8]{1,0:T(1,128)} %pattern.3) | copy-start | bytes 100

commit v6 on v5

--- a/solution.py
+++ b/solution.py
@@ -151,16 +151,19 @@
             low_out[pl.ds(first, LROWS), :] = low
 
 
-def multiply(high, low, lower_high, lower_low):
-    def dot(a, b):
-        return jnp.dot(a[...], b[...], preferred_element_type=jnp.float32)
-
-    return dot(high, lower_high) + (dot(low, lower_high) + dot(high, lower_low))
-
-
-def own_kernel(
-    pieces, lower, partial, other_high, other_low, lower_high, lower_low, panel, own_high, own_low
-):
+def multiply(both, lower_high, lower_low):
+    count = both.shape[0] // 2
+    first = jnp.dot(both[...], lower_high[...], preferred_element_type=jnp.float32)
+    second = jnp.dot(both[0:count, :], lower_low[...], preferred_element_type=jnp.float32)
+    return first[0:count, :] + (first[count:, :] + second)
+
+
+def put_both(out, lanes, value):
+    count = value.shape[0]
+    out[0:count, lanes], out[count:, lanes] = split(value)
+
+
+def own_kernel(pieces, lower, partial, other_both, lower_high, lower_low, panel, own_both):
     for leaf in range(N_LEAF):
         for block in range(NP):
             panel[leaf * CHUNK:(leaf + 1) * CHUNK, block * BLK:(block + 1) * BLK] = pieces[
@@ -171,16 +174,16 @@
         own, other = by_core(
             panel[:, 2 * at * BLK:(2 * at + 1) * BLK], panel[:, (2 * at + 1) * BLK:(2 * at + 2) * BLK]
         )
-        own_high[:, here], own_low[:, here] = split(own)
-        other_high[:, here], other_low[:, here] = split(other)
+        put_both(own_both, here, own)
+        put_both(other_both, here, other)
     order_rows(lower, lower_high, lower_low)
-    partial[...] = multiply(own_high, own_low, lower_high, lower_low)
-
-
-def cross_kernel(partial, high, low, lower, cross, out, lower_high, lower_low, product):
+    partial[...] = multiply(own_both, lower_high, lower_low)
+
+
+def cross_kernel(partial, both, lower, cross, out, lower_high, lower_low, product):
     core = lax.axis_index("core")
     order_rows(lower, lower_high, lower_low)
-    value = partial[...] + multiply(high, low, lower_high, lower_low)
+    value = partial[...] + multiply(both, lower_high, lower_low)
     product[...] = value
     cross[0, :, :] = -value
     whole = product[pl.ds(pl.multiple_of(core * 64, 64), BLK), :].T
@@ -194,7 +197,7 @@
 
 
 def diagonal_kernel(
-    pattern, pieces, own_high, own_low, other_high, other_low, child, out, rows, *parts
+    pattern, pieces, own_high, own_low, other_high, other_low, child, out, rows, own_both, other_both
 ):
     lane = lax.broadcasted_iota(jnp.int32, (HALF, BLK), 1)
     rows[:, COLS:, :] = jnp.zeros((NP, 32 - COLS, BLK), jnp.float32)
@@ -205,8 +208,8 @@
         upper = 2 * group
         middle = place == 1
         whole = pieces[pl.ds((upper + place // 2) * PIECE3, COLS), :]
-        first = pieces[pl.ds(upper * PIECE3 + COLS, HALF), :]
-        second = pieces[pl.ds((upper + 1) * PIECE3 + COLS, HALF), :]
+        first = pieces[pl.ds(upper * PIECE3 + COLS - 2, HALF + 2), :][2:, :]
+        second = pieces[pl.ds((upper + 1) * PIECE3 + COLS - 2, HALF + 2), :][2:, :]
         top = jnp.where(lane < 64, first, pltpu.roll(second, 64, 1))
         bottom = jnp.where(lane < 64, pltpu.roll(first, 64, 1), second)
         rows[block, 0:HALF, :] = jnp.where(middle, top, whole[0:HALF, :])
@@ -214,11 +217,9 @@
     for at in range(NP // 2):
         here = slice(at * BLK, (at + 1) * BLK)
         own, other = by_core(rows[2 * at], rows[2 * at + 1])
-        parts[0][:, here], parts[1][:, here] = split(own)
-        parts[2][:, here], parts[3][:, here] = split(other)
-    update = multiply(parts[0], parts[1], own_high, own_low) + multiply(
-        parts[2], parts[3], other_high, other_low
-    )
+        put_both(own_both, here, own)
+        put_both(other_both, here, other)
+    update = multiply(own_both, own_high, own_low) + multiply(other_both, other_high, other_low)
     for row in range(COLS):
         out[row, 0:1, :] = child[row, 0:1, :] + update[row:row + 1, :]
 
@@ -287,22 +288,20 @@
     lower, chosen = lax.optimization_barrier((lower, chosen))
     lower_other = lax.ppermute(lower, "core", [(0, 1), (1, 0)])
     lower_shape = jax.ShapeDtypeStruct((NP * 64, S1), jnp.bfloat16)
-    panel_shape = jax.ShapeDtypeStruct((ROWS, NP * 64), jnp.bfloat16)
-    partial, panel_high, panel_low, own_high, own_low = pl.pallas_call(
+    panel_shape = jax.ShapeDtypeStruct((2 * ROWS, NP * 64), jnp.bfloat16)
+    partial, panel_both, own_high, own_low = pl.pallas_call(
         own_kernel,
         out_shape=(
             jax.ShapeDtypeStruct((ROWS, S1), jnp.float32),
-            panel_shape,
             panel_shape,
             lower_shape,
             lower_shape,
         ),
         in_specs=in_vmem(2),
-        out_specs=tuple(in_vmem(5)),
+        out_specs=tuple(in_vmem(4)),
         scratch_shapes=[
             pltpu.VMEM((ROWS, NP * BLK), jnp.float32),
-            pltpu.VMEM((ROWS, NP * 64), jnp.bfloat16),
-            pltpu.VMEM((ROWS, NP * 64), jnp.bfloat16),
+            pltpu.VMEM((2 * ROWS, NP * 64), jnp.bfloat16),
         ],
         compiler_params=params,
     )(chosen, lower)
@@ -314,11 +313,11 @@
             lower_shape,
             lower_shape,
         ),
-        in_specs=in_vmem(4),
+        in_specs=in_vmem(3),
         out_specs=tuple(in_vmem(4)),
         scratch_shapes=[pltpu.VMEM((ROWS, S1), jnp.float32)],
         compiler_params=params,
-    )(partial, panel_high, panel_low, lower_other)
+    )(partial, panel_both, lower_other)
     pieces = lax.all_to_all(
         pieces.reshape(N_GRID, PIECE3, 1, BLK), GRID, 0, 0, tiled=True
     ).reshape(N_GRID * PIECE3, BLK)
@@ -328,7 +327,7 @@
         in_specs=[pl.BlockSpec(memory_space=pltpu.SMEM)] + in_vmem(6),
         out_specs=in_vmem(1)[0],
         scratch_shapes=[pltpu.VMEM((NP, 32, BLK), jnp.float32)]
-        + [pltpu.VMEM((32, NP * 64), jnp.bfloat16)] * 4,
+        + [pltpu.VMEM((64, NP * 64), jnp.bfloat16)] * 2,
         compiler_params=params,
     )(
         pattern,

time: 100 us -> 100 us (level)
  no operation moved by 1% of the time
where the time goes in v6:
time: 100 us; the launch traced here: 99.7 us
  starting transfers between devices  42.8 us (43%)
  blocking collectives  28.2 us (28%)
  waiting for transfers between devices  15.6 us (16%)
  Pallas kernels  11.5 us (12%)
    all_to_all x1, blocking collectives, shards(): lax.all_to_all(pieces.reshape(N_GRID, PIECE3, 1, BLK), GRID, 0, 0, tiled=...  28.2 us
    ppermute x5, starting transfers between devices, from_row(): lax.ppermute(value, 'prow', [(at, (at - distance) % NP) for at in range(N...  18.9 us
    ppermute x5, waiting for transfers between devices, from_row(): lax.ppermute(value, 'prow', [(at, (at - distance) % NP) for at in range(N...  13.2 us
    all_to_all x1, starting transfers between devices, shards(): spread = lax.all_to_all(spread, 'leaf', 0, 0, tiled=True)  11.8 us
    all_to_all x1, starting transfers between devices, shards(): chosen = lax.all_to_all(chosen, 'leaf', 0, 0, tiled=True)  6.81 us
    ppermute x1, starting transfers between devices, swap_side(): return lax.ppermute(value, 'side', [(0, 1), (1, 0)])  3.32 us
    pallas_call x1, Pallas kernels, shards(): pl.pallas_call(select_kernel, out_shape=jax.ShapeDtypeStruct((N_LEAF, PIE...  2.74 us
    pallas_call x1, Pallas kernels, shards(): pl.pallas_call(own_kernel, out_shape=(jax.ShapeDtypeStruct((ROWS, S1), jn...  2.7 us
  transfers between devices with their start and end apart: 9, of which 5 were waited for; matrix products, arithmetic and copies ran while one was open for 0% of the time, Pallas kernels for 7%

profile of v6, /device:TPU:6, one launch (start us, length us, event | category | flops | bytes accessed | tf_op | source)
XLA Modules:
  0.0 99.7 jit_solution(11992834124636939395)
XLA Ops:
  0.6 3.3 %collective-permute-start = (f32[32,896]{1,0:T(8,128)}, f32[32,896]{1,0:T(8,128)S(1)}, u32[]{:S(2)}, u32[]{:S(2)}) collective-permute-start(f32[32,896]{1,0:T(8,128)} %bitcast.8), channel_id=1, source_target_pairs={{0,2},{2,0},{1,3},{3,1},{4,6},{6,4},{5,7},{7,5},{8,10},{10,8},{9,1... | collective-permute-start | bytes 344072 | tf_op jit(solution)/shard_map/ppermute | solution.py:40
  4.0 1.7 %shard_map.62 = f32[16,40,128]{2,1,0:T(8,128)} custom-call(f32[192,384]{1,0:T(8,128)} %ancestor.1, s32[1,8]{1,0:T(1,128)} %pattern.3), custom_call_target="tpu_custom_call" | custom-call | tf_op jit(solution)/shard_map/pallas_call | solution.py:241
  5.7 11.8 %all-to-all-start = ((f32[16,40,128]{2,1,0:T(8,128)}), f32[16,40,128]{2,1,0:T(8,128)}, u32[]{:S(2)}, u32[]{:S(2)}) async-start(f32[16,40,128]{2,1,0:T(8,128)} %shard_map.62), calls=%async_computation | async-start | bytes 655360 | tf_op jit(solution)/shard_map/all_to_all | solution.py:263
  17.5 0.0 collective-permute-done.across
  17.5 0.0 copy-start.2
  17.5 0.9 copy-done.2
  18.4 4.5 %collective-permute-start.2 = (f32[64,896]{1,0:T(8,128)S(1)}, f32[64,896]{1,0:T(8,128)S(1)}, u32[]{:S(2)}, u32[]{:S(2)}) collective-permute-start(f32[64,896]{1,0:T(8,128)S(1)} %shard_map.59.pair), channel_id=1, source_target_pairs={{0,8},{4,12},{8,16},{12,20},{16,24},{20,28},{24,0},{28,4},{1,9},{5... | collective-permute-start | bytes 688136 | tf_op jit(solution)/shard_map/ppermute | solution.py:36
  22.9 3.6 %collective-permute-start.1 = (f32[64,896]{1,0:T(8,128)S(1)}, f32[64,896]{1,0:T(8,128)S(1)}, u32[]{:S(2)}, u32[]{:S(2)}) collective-permute-start(f32[64,896]{1,0:T(8,128)S(1)} %shard_map.59.pair), channel_id=1, source_target_pairs={{0,24},{4,28},{8,0},{12,4},{16,8},{20,12},{24,16},{28,20},{1,25},{... | collective-permute-start | bytes 688136 | tf_op jit(solution)/shard_map/ppermute | solution.py:36
  26.5 1.3 %all-to-all-done.pieces = f32[16,40,128]{2,1,0:T(8,128)} async-done(((f32[16,40,128]{2,1,0:T(8,128)}), f32[16,40,128]{2,1,0:T(8,128)}, u32[]{:S(2)}, u32[]{:S(2)}) %all-to-all-start) | async-done | bytes 327712 | tf_op jit(solution)/shard_map/all_to_all | solution.py:263
  27.9 2.7 %shard_map.63 = f32[16,96,128]{2,1,0:T(8,128)} custom-call(f32[16,40,128]{2,1,0:T(8,128)} %all-to-all-done.pieces), custom_call_target="tpu_custom_call" | custom-call | tf_op jit(solution)/shard_map/pallas_call | solution.py:264
  30.6 6.8 %all-to-all-start.1 = ((f32[16,96,128]{2,1,0:T(8,128)}), f32[16,96,128]{2,1,0:T(8,128)}, u32[]{:S(2)}, u32[]{:S(2)}) async-start(f32[16,96,128]{2,1,0:T(8,128)} %shard_map.63), calls=%async_computation.1 | async-start | bytes 1572864 | tf_op jit(solution)/shard_map/all_to_all | solution.py:277
  37.4 0.0 collective-permute-done.2.behind
  37.4 0.6 collective-permute-done.1.ahead
  38.0 0.1 shard_map.60
  38.1 3.5 %collective-permute-start.3 = (f32[192,896]{1,0:T(8,128)S(1)}, f32[192,896]{1,0:T(8,128)S(1)}, u32[]{:S(2)}, u32[]{:S(2)}) collective-permute-start(f32[192,896]{1,0:T(8,128)S(1)} %get-tuple-element.14.refs_0_), channel_id=1, source_target_pairs={{0,28},{4,0},{8,4},{12,8},{16,12},{20,16},{24,20},{28,24},{1,29},{... | collective-permute-start | bytes 2064392 | tf_op jit(solution)/shard_map/ppermute | solution.py:36
  41.6 3.4 %collective-permute-start.5 = (f32[64,896]{1,0:T(8,128)S(1)}, f32[64,896]{1,0:T(8,128)S(1)}, u32[]{:S(2)}, u32[]{:S(2)}) collective-permute-start(f32[64,896]{1,0:T(8,128)S(1)} %get-tuple-element.15), channel_id=1, source_target_pairs={{0,8},{4,12},{8,16},{12,20},{16,24},{20,28},{24,0},{28,4},{1,9},{5... | collective-permute-start | bytes 688136 | tf_op jit(solution)/shard_map/ppermute | solution.py:36
  45.0 3.9 %collective-permute-start.4 = (f32[64,896]{1,0:T(8,128)S(1)}, f32[64,896]{1,0:T(8,128)S(1)}, u32[]{:S(2)}, u32[]{:S(2)}) collective-permute-start(f32[64,896]{1,0:T(8,128)S(1)} %get-tuple-element.15), channel_id=1, source_target_pairs={{0,4},{4,8},{8,12},{12,16},{16,20},{20,24},{24,28},{28,0},{1,5},{5... | collective-permute-start | bytes 688136 | tf_op jit(solution)/shard_map/ppermute | solution.py:36
  48.9 9.0 %collective-permute-done.5.refs_3_ = f32[64,896]{1,0:T(8,128)S(1)} collective-permute-done((f32[64,896]{1,0:T(8,128)S(1)}, f32[64,896]{1,0:T(8,128)S(1)}, u32[]{:S(2)}, u32[]{:S(2)}) %collective-permute-start.5) | collective-permute-done | bytes 229408 | tf_op jit(solution)/shard_map/ppermute | solution.py:36
  58.0 3.5 %collective-permute-done.4.refs_2_ = f32[64,896]{1,0:T(8,128)S(1)} collective-permute-done((f32[64,896]{1,0:T(8,128)S(1)}, f32[64,896]{1,0:T(8,128)S(1)}, u32[]{:S(2)}, u32[]{:S(2)}) %collective-permute-start.4) | collective-permute-done | bytes 229408 | tf_op jit(solution)/shard_map/ppermute | solution.py:36
  61.5 0.0 collective-permute-done.3.refs_1_
  61.5 0.1 shard_map.61.lower
  61.6 0.0 all-to-all-done.1.pieces
  61.7 1.9 %collective-permute-start.6 = (f32[512,896]{1,0:T(8,128)S(1)}, f32[512,896]{1,0:T(8,128)S(1)}, u32[]{:S(2)}, u32[]{:S(2)}) collective-permute-start(f32[512,896]{1,0:T(8,128)S(1)} %shard_map.61.lower), channel_id=1, source_target_pairs={{0,1},{1,0},{2,3},{3,2},{4,5},{5,4},{6,7},{7,6},{8,9},{9,8},{10,11... | collective-permute-start | bytes 5505032 | tf_op jit(solution)/shard_map/ppermute | solution.py:289
  63.6 2.7 %shard_map.64 = (f32[192,896]{1,0:T(8,128)S(1)}, bf16[384,512]{1,0:T(8,128)(2,1)S(1)}, bf16[512,896]{1,0:T(8,128)(2,1)S(1)}, bf16[512,896]{1,0:T(8,128)(2,1)S(1)}) custom-call(f32[16,96,128]{2,1,0:T(8,128)} %all-to-all-done.1.pieces, f32[512,896]{1,0:T(8,128)S(1)} %shard_map.61.lower), custom_call_target="tpu_custom_call" | custom-call | tf_op jit(solution)/shard_map/pallas_call | solution.py:292
  66.3 1.0 %collective-permute-done.6.lower = f32[512,896]{1,0:T(8,128)S(1)} collective-permute-done((f32[512,896]{1,0:T(8,128)S(1)}, f32[512,896]{1,0:T(8,128)S(1)}, u32[]{:S(2)}, u32[]{:S(2)}) %collective-permute-start.6) | collective-permute-done | bytes 1835040 | tf_op jit(solution)/shard_map/ppermute | solution.py:289
  67.3 0.0 copy-start
  67.3 0.0 copy-start.1
  67.3 2.0 %shard_map.65 = (f32[1,192,896]{2,1,0:T(8,128)}, f32[1344,128]{1,0:T(8,128)S(1)}, bf16[512,896]{1,0:T(8,128)(2,1)S(1)}, bf16[512,896]{1,0:T(8,128)(2,1)S(1)}) custom-call(f32[192,896]{1,0:T(8,128)S(1)} %get-tuple-element.18.partial, bf16[384,512]{1,0:T(8,128)(2,1)S(1)} %get-tuple-element.19.both, f32[512,896]{1,0:T(8,128)S(1)} %collective-permute-done.6.lower), custom_call_target="tpu_custom_call" | custom-call | tf_op jit(solution)/shard_map/pallas_call | solution.py:308
  69.3 28.2 %all_to_all.15 = f32[32,42,1,128]{3,2,1,0:T(1,128)S(1)} all-to-all(f32[32,42,1,128]{3,2,1,0:T(1,128)S(1)} %bitcast.6), channel_id=1, replica_groups=mesh['leaf'=16,'prow'=8,'side'=2,'core'=2] {'prow','side','core'}, dimensions={0} | all-to-all | bytes 1376256 | tf_op jit(solution)/shard_map/all_to_all | solution.py:321
  97.5 0.0 copy-done
  97.6 0.0 copy-done.1
  97.6 2.1 %shard_map.66 = f32[28,1,896]{2,1,0:T(1,128)} custom-call(s32[1,8]{1,0:T(1,128)S(1)} %copy-done.1, f32[1344,128]{1,0:T(8,128)S(1)} %bitcast.5, bf16[512,896]{1,0:T(8,128)(2,1)S(1)} %get-tuple-element.22.own_high, bf16[512,896]{1,0:T(8,128)(2,1)S(1)} %get-tuple-element.23.own_low, bf16[512,896]{1,0:T(8,128)(2,1)S(1)} %get-tuple-element.24.other_high, ...), custom_call_target="tpu_custom_call" | custom-call | tf_op jit(solution)/shard_map/pallas_call | solution.py:324
  (1 shorter events, 0.0 us)
Async XLA Ops:
  0.6 16.9 %collective-permute-start = (f32[32,896]{1,0:T(8,128)}, f32[32,896]{1,0:T(8,128)S(1)}, u32[]{:S(2)}, u32[]{:S(2)}) collective-permute-start(f32[32,896]{1,0:T(8,128)} %bitcast.8), channel_id=1, source_target_pairs={{0,2},{2,0},{1,3},{3,1},{4,6},{6,4},{5,7},{7,5},{8,10},{10,8},{9,1... | collective-permute-start | bytes 344072 | tf_op jit(solution)/shard_map/ppermute | solution.py:40
  5.7 22.2 %all-to-all-start = ((f32[16,40,128]{2,1,0:T(8,128)}), f32[16,40,128]{2,1,0:T(8,128)}, u32[]{:S(2)}, u32[]{:S(2)}) async-start(f32[16,40,128]{2,1,0:T(8,128)} %shard_map.62), calls=%async_computation | async-start | bytes 655360 | tf_op jit(solution)/shard_map/all_to_all | solution.py:263
  17.5 0.9 copy-start.2
  18.4 19.0 %collective-permute-start.2 = (f32[64,896]{1,0:T(8,128)S(1)}, f32[64,896]{1,0:T(8,128)S(1)}, u32[]{:S(2)}, u32[]{:S(2)}) collective-permute-start(f32[64,896]{1,0:T(8,128)S(1)} %shard_map.59.pair), channel_id=1, source_target_pairs={{0,8},{4,12},{8,16},{12,20},{16,24},{20,28},{24,0},{28,4},{1,9},{5... | collective-permute-start | bytes 688136 | tf_op jit(solution)/shard_map/ppermute | solution.py:36
  22.9 15.1 %collective-permute-start.1 = (f32[64,896]{1,0:T(8,128)S(1)}, f32[64,896]{1,0:T(8,128)S(1)}, u32[]{:S(2)}, u32[]{:S(2)}) collective-permute-start(f32[64,896]{1,0:T(8,128)S(1)} %shard_map.59.pair), channel_id=1, source_target_pairs={{0,24},{4,28},{8,0},{12,4},{16,8},{20,12},{24,16},{28,20},{1,25},{... | collective-permute-start | bytes 688136 | tf_op jit(solution)/shard_map/ppermute | solution.py:36
  30.6 31.0 %all-to-all-start.1 = ((f32[16,96,128]{2,1,0:T(8,128)}), f32[16,96,128]{2,1,0:T(8,128)}, u32[]{:S(2)}, u32[]{:S(2)}) async-start(f32[16,96,128]{2,1,0:T(8,128)} %shard_map.63), calls=%async_computation.1 | async-start | bytes 1572864 | tf_op jit(solution)/shard_map/all_to_all | solution.py:277
  38.1 23.4 %collective-permute-start.3 = (f32[192,896]{1,0:T(8,128)S(1)}, f32[192,896]{1,0:T(8,128)S(1)}, u32[]{:S(2)}, u32[]{:S(2)}) collective-permute-start(f32[192,896]{1,0:T(8,128)S(1)} %get-tuple-element.14.refs_0_), channel_id=1, source_target_pairs={{0,28},{4,0},{8,4},{12,8},{16,12},{20,16},{24,20},{28,24},{1,29},{... | collective-permute-start | bytes 2064392 | tf_op jit(solution)/shard_map/ppermute | solution.py:36
  41.6 16.4 %collective-permute-start.5 = (f32[64,896]{1,0:T(8,128)S(1)}, f32[64,896]{1,0:T(8,128)S(1)}, u32[]{:S(2)}, u32[]{:S(2)}) collective-permute-start(f32[64,896]{1,0:T(8,128)S(1)} %get-tuple-element.15), channel_id=1, source_target_pairs={{0,8},{4,12},{8,16},{12,20},{16,24},{20,28},{24,0},{28,4},{1,9},{5... | collective-permute-start | bytes 688136 | tf_op jit(solution)/shard_map/ppermute | solution.py:36
  45.0 16.5 %collective-permute-start.4 = (f32[64,896]{1,0:T(8,128)S(1)}, f32[64,896]{1,0:T(8,128)S(1)}, u32[]{:S(2)}, u32[]{:S(2)}) collective-permute-start(f32[64,896]{1,0:T(8,128)S(1)} %get-tuple-element.15), channel_id=1, source_target_pairs={{0,4},{4,8},{8,12},{12,16},{16,20},{20,24},{24,28},{28,0},{1,5},{5... | collective-permute-start | bytes 688136 | tf_op jit(solution)/shard_map/ppermute | solution.py:36
  61.7 5.7 %collective-permute-start.6 = (f32[512,896]{1,0:T(8,128)S(1)}, f32[512,896]{1,0:T(8,128)S(1)}, u32[]{:S(2)}, u32[]{:S(2)}) collective-permute-start(f32[512,896]{1,0:T(8,128)S(1)} %shard_map.61.lower), channel_id=1, source_target_pairs={{0,1},{1,0},{2,3},{3,2},{4,5},{5,4},{6,7},{7,6},{8,9},{9,8},{10,11... | collective-permute-start | bytes 5505032 | tf_op jit(solution)/shard_map/ppermute | solution.py:289
  67.3 30.2 %copy-start = (f32[1,28,896]{2,0,1:T(1,128)S(1)}, f32[1,28,896]{2,0,1:T(1,128)}, u32[]{:S(2)}) copy-start(f32[1,28,896]{2,0,1:T(1,128)} %param.7) | copy-start | bytes 301060
  67.3 30.2 %copy-start.1 = (s32[1,8]{1,0:T(1,128)S(1)}, s32[1,8]{1,0:T(1,128)}, u32[]{:S(2)}) copy-start(s32[1,8]{1,0:T(1,128)} %pattern.3) | copy-start | bytes 100

commit v7 on v6

--- a/solution.py
+++ b/solution.py
@@ -34,6 +34,10 @@
 
 def from_row(value, distance):
     return lax.ppermute(value, "prow", [(at, (at - distance) % NP) for at in range(NP)])
+
+
+def swap_core(value):
+    return lax.ppermute(value, "core", [(0, 1), (1, 0)])
 
 
 def swap_side(value):
@@ -138,10 +142,11 @@
     return jnp.where(swap, cores[1], cores[0]), jnp.where(swap, cores[0], cores[1])
 
 
-def order_rows(source, high_out, low_out):
+def order_rows(sources, high_out, low_out):
     side = lax.axis_index("side")
     place = lax.axis_index("prow")
-    for group, step in enumerate(STEPS):
+    for index, step in enumerate(STEPS):
+        source, group = (sources[index], 0) if index < 3 else (sources[3], index - 3)
         block = lax.rem(place + step + NP, NP)
         for part, at_side in ((0, side), (1, 1 - side)):
             row = group * 64 + part * LROWS
@@ -163,7 +168,9 @@
     out[0:count, lanes], out[count:, lanes] = split(value)
 
 
-def own_kernel(pieces, lower, partial, other_both, lower_high, lower_low, panel, own_both):
+def own_kernel(pieces, *refs):
+    sources = refs[:4]
+    partial, other_both, lower_high, lower_low, panel, own_both = refs[4:]
     for leaf in range(N_LEAF):
         for block in range(NP):
             panel[leaf * CHUNK:(leaf + 1) * CHUNK, block * BLK:(block + 1) * BLK] = pieces[
@@ -176,13 +183,15 @@
         )
         put_both(own_both, here, own)
         put_both(other_both, here, other)
-    order_rows(lower, lower_high, lower_low)
+    order_rows(sources, lower_high, lower_low)
     partial[...] = multiply(own_both, lower_high, lower_low)
 
 
-def cross_kernel(partial, both, lower, cross, out, lower_high, lower_low, product):
+def cross_kernel(partial, both, *refs):
+    sources = refs[:4]
+    cross, out, lower_high, lower_low, product = refs[4:]
     core = lax.axis_index("core")
-    order_rows(lower, lower_high, lower_low)
+    order_rows(sources, lower_high, lower_low)
     value = partial[...] + multiply(both, lower_high, lower_low)
     product[...] = value
     cross[0, :, :] = -value
@@ -276,17 +285,13 @@
     )(spread)
     chosen = lax.all_to_all(chosen, "leaf", 0, 0, tiled=True)
     near, rear = call(near_kernel, (192, 64), 2000, pair, ahead, behind)
-    (lower,) = call(
-        join_kernel,
-        (NP * 64,),
-        0,
-        near,
-        from_row(near, 1),
-        from_row(rear, -1),
-        from_row(rear, -2),
+    (far,) = call(
+        join_kernel, (320,), 0, from_row(near, 1), from_row(rear, -1), from_row(rear, -2)
     )
-    lower, chosen = lax.optimization_barrier((lower, chosen))
-    lower_other = lax.ppermute(lower, "core", [(0, 1), (1, 0)])
+    near_parts = [pair, ahead, rear]
+    near_other = [swap_core(part) for part in near_parts]
+    near_other, far, chosen = lax.optimization_barrier((near_other, far, chosen))
+    far_other = swap_core(far)
     lower_shape = jax.ShapeDtypeStruct((NP * 64, S1), jnp.bfloat16)
     panel_shape = jax.ShapeDtypeStruct((2 * ROWS, NP * 64), jnp.bfloat16)
     partial, panel_both, own_high, own_low = pl.pallas_call(
@@ -297,14 +302,14 @@
             lower_shape,
             lower_shape,
         ),
-        in_specs=in_vmem(2),
+        in_specs=in_vmem(5),
         out_specs=tuple(in_vmem(4)),
         scratch_shapes=[
             pltpu.VMEM((ROWS, NP * BLK), jnp.float32),
             pltpu.VMEM((2 * ROWS, NP * 64), jnp.bfloat16),
         ],
         compiler_params=params,
-    )(chosen, lower)
+    )(chosen, *near_parts, far)
     cross, pieces, other_high, other_low = pl.pallas_call(
         cross_kernel,
         out_shape=(
@@ -313,11 +318,11 @@
             lower_shape,
             lower_shape,
         ),
-        in_specs=in_vmem(3),
+        in_specs=in_vmem(6),
         out_specs=tuple(in_vmem(4)),
         scratch_shapes=[pltpu.VMEM((ROWS, S1), jnp.float32)],
         compiler_params=params,
-    )(partial, panel_both, lower_other)
+    )(partial, panel_both, *near_other, far_other)
     pieces = lax.all_to_all(
         pieces.reshape(N_GRID, PIECE3, 1, BLK), GRID, 0, 0, tiled=True
     ).reshape(N_GRID * PIECE3, BLK)

time: 100 us -> 100 us (level)
  waiting for transfers between devices: 15.6 us -> 9.96 us
  starting transfers between devices: 42.8 us -> 48.3 us
    ppermute x1 -> x4, starting transfers between devices: 1.92 us -> 8.27 us  [swap_core(): return lax.ppermute(value, 'core', [(0, 1), (1, 0)])]
    ppermute x5, waiting for transfers between devices: 13.2 us -> 6.94 us  [from_row(): lax.ppermute(value, 'prow', [(at, (at - distance) % NP) for at in range(N...]
  transfers between devices with their start and end apart: 9 -> 12, of which waited for: 5 -> 5; matrix products, arithmetic and copies ran while one was open for 0% -> 0% of each run, Pallas kernels for 7% -> 7%
where the time goes in v7:
time: 100 us; the launch traced here: 99.6 us
  starting transfers between devices  48.3 us (48%)
  blocking collectives  29.1 us (29%)
  Pallas kernels  11.4 us (11%)
  waiting for transfers between devices  9.96 us (10%)
    all_to_all x1, blocking collectives, shards(): lax.all_to_all(pieces.reshape(N_GRID, PIECE3, 1, BLK), GRID, 0, 0, tiled=...  29.1 us
    ppermute x5, starting transfers between devices, from_row(): lax.ppermute(value, 'prow', [(at, (at - distance) % NP) for at in range(N...  18.9 us
    all_to_all x1, starting transfers between devices, shards(): spread = lax.all_to_all(spread, 'leaf', 0, 0, tiled=True)  11.8 us
    ppermute x4, starting transfers between devices, swap_core(): return lax.ppermute(value, 'core', [(0, 1), (1, 0)])  8.27 us
    ppermute x5, waiting for transfers between devices, from_row(): lax.ppermute(value, 'prow', [(at, (at - distance) % NP) for at in range(N...  6.94 us
    all_to_all x1, starting transfers between devices, shards(): chosen = lax.all_to_all(chosen, 'leaf', 0, 0, tiled=True)  5.92 us
    ppermute x1, starting transfers between devices, swap_side(): return lax.ppermute(value, 'side', [(0, 1), (1, 0)])  3.44 us
    pallas_call x1, Pallas kernels, shards(): pl.pallas_call(select_kernel, out_shape=jax.ShapeDtypeStruct((N_LEAF, PIE...  2.73 us
  transfers between devices with their start and end apart: 12, of which 5 were waited for; matrix products, arithmetic and copies ran while one was open for 0% of the time, Pallas kernels for 7%

profile of v7, /device:TPU:6, one launch (start us, length us, event | category | flops | bytes accessed | tf_op | source)
XLA Modules:
  0.0 99.6 jit_solution(8139111518404172472)
XLA Ops:
  0.6 3.4 %collective-permute-start = (f32[32,896]{1,0:T(8,128)}, f32[32,896]{1,0:T(8,128)S(1)}, u32[]{:S(2)}, u32[]{:S(2)}) collective-permute-start(f32[32,896]{1,0:T(8,128)} %bitcast.8), channel_id=1, source_target_pairs={{0,2},{2,0},{1,3},{3,1},{4,6},{6,4},{5,7},{7,5},{8,10},{10,8},{9,1... | collective-permute-start | bytes 344072 | tf_op jit(solution)/shard_map/ppermute | solution.py:44
  4.1 1.7 %shard_map.62 = f32[16,40,128]{2,1,0:T(8,128)} custom-call(f32[192,384]{1,0:T(8,128)} %ancestor.1, s32[1,8]{1,0:T(1,128)} %pattern.3), custom_call_target="tpu_custom_call" | custom-call | tf_op jit(solution)/shard_map/pallas_call | solution.py:250
  5.8 11.8 %all-to-all-start = ((f32[16,40,128]{2,1,0:T(8,128)}), f32[16,40,128]{2,1,0:T(8,128)}, u32[]{:S(2)}, u32[]{:S(2)}) async-start(f32[16,40,128]{2,1,0:T(8,128)} %shard_map.62), calls=%async_computation | async-start | bytes 655360 | tf_op jit(solution)/shard_map/all_to_all | solution.py:272
  17.6 0.0 collective-permute-done.across
  17.7 4.5 %collective-permute-start.4 = (f32[64,896]{1,0:T(8,128)S(1)}, f32[64,896]{1,0:T(8,128)S(1)}, u32[]{:S(2)}, u32[]{:S(2)}) collective-permute-start(f32[64,896]{1,0:T(8,128)S(1)} %shard_map.59.pair.refs_0_), channel_id=1, source_target_pairs={{0,8},{4,12},{8,16},{12,20},{16,24},{20,28},{24,0},{28,4},{1,9},{5... | collective-permute-start | bytes 688136 | tf_op jit(solution)/shard_map/ppermute | solution.py:36
  22.2 3.6 %collective-permute-start.2 = (f32[64,896]{1,0:T(8,128)S(1)}, f32[64,896]{1,0:T(8,128)S(1)}, u32[]{:S(2)}, u32[]{:S(2)}) collective-permute-start(f32[64,896]{1,0:T(8,128)S(1)} %shard_map.59.pair.refs_0_), channel_id=1, source_target_pairs={{0,24},{4,28},{8,0},{12,4},{16,8},{20,12},{24,16},{28,20},{1,25},{... | collective-permute-start | bytes 688136 | tf_op jit(solution)/shard_map/ppermute | solution.py:36
  25.8 2.2 %all-to-all-done.pieces = f32[16,40,128]{2,1,0:T(8,128)} async-done(((f32[16,40,128]{2,1,0:T(8,128)}), f32[16,40,128]{2,1,0:T(8,128)}, u32[]{:S(2)}, u32[]{:S(2)}) %all-to-all-start) | async-done | bytes 327712 | tf_op jit(solution)/shard_map/all_to_all | solution.py:272
  28.0 2.7 %shard_map.63 = f32[16,96,128]{2,1,0:T(8,128)} custom-call(f32[16,40,128]{2,1,0:T(8,128)} %all-to-all-done.pieces), custom_call_target="tpu_custom_call" | custom-call | tf_op jit(solution)/shard_map/pallas_call | solution.py:273
  30.8 5.9 %all-to-all-start.1 = ((f32[16,96,128]{2,1,0:T(8,128)}), f32[16,96,128]{2,1,0:T(8,128)}, u32[]{:S(2)}, u32[]{:S(2)}) async-start(f32[16,96,128]{2,1,0:T(8,128)} %shard_map.63), calls=%async_computation.1 | async-start | bytes 1572864 | tf_op jit(solution)/shard_map/all_to_all | solution.py:286
  36.7 0.0 collective-permute-done.4.behind
  36.7 0.6 collective-permute-done.2.ahead.refs_1_
  37.3 0.1 shard_map.60
  37.4 4.4 %collective-permute-start.6 = (f32[192,896]{1,0:T(8,128)S(1)}, f32[192,896]{1,0:T(8,128)S(1)}, u32[]{:S(2)}, u32[]{:S(2)}) collective-permute-start(f32[192,896]{1,0:T(8,128)S(1)} %get-tuple-element.18), channel_id=1, source_target_pairs={{0,28},{4,0},{8,4},{12,8},{16,12},{20,16},{24,20},{28,24},{1,29},{... | collective-permute-start | bytes 2064392 | tf_op jit(solution)/shard_map/ppermute | solution.py:36
  41.7 2.5 %collective-permute-start.8 = (f32[64,896]{1,0:T(8,128)S(1)}, f32[64,896]{1,0:T(8,128)S(1)}, u32[]{:S(2)}, u32[]{:S(2)}) collective-permute-start(f32[64,896]{1,0:T(8,128)S(1)} %get-tuple-element.17.refs_2_), channel_id=1, source_target_pairs={{0,8},{4,12},{8,16},{12,20},{16,24},{20,28},{24,0},{28,4},{1,9},{5... | collective-permute-start | bytes 688136 | tf_op jit(solution)/shard_map/ppermute | solution.py:36
  44.3 3.9 %collective-permute-start.7 = (f32[64,896]{1,0:T(8,128)S(1)}, f32[64,896]{1,0:T(8,128)S(1)}, u32[]{:S(2)}, u32[]{:S(2)}) collective-permute-start(f32[64,896]{1,0:T(8,128)S(1)} %get-tuple-element.17.refs_2_), channel_id=1, source_target_pairs={{0,4},{4,8},{8,12},{12,16},{16,20},{20,24},{24,28},{28,0},{1,5},{5... | collective-permute-start | bytes 688136 | tf_op jit(solution)/shard_map/ppermute | solution.py:36
  48.2 1.9 %collective-permute-start.1 = (f32[64,896]{1,0:T(8,128)S(1)}, f32[64,896]{1,0:T(8,128)S(1)}, u32[]{:S(2)}, u32[]{:S(2)}) collective-permute-start(f32[64,896]{1,0:T(8,128)S(1)} %shard_map.59.pair.refs_0_), channel_id=1, source_target_pairs={{0,1},{1,0},{2,3},{3,2},{4,5},{5,4},{6,7},{7,6},{8,9},{9,8},{10,11... | collective-permute-start | bytes 688136 | tf_op jit(solution)/shard_map/ppermute | solution.py:40
  50.1 2.4 %collective-permute-start.3 = (f32[64,896]{1,0:T(8,128)S(1)}, f32[64,896]{1,0:T(8,128)S(1)}, u32[]{:S(2)}, u32[]{:S(2)}) collective-permute-start(f32[64,896]{1,0:T(8,128)S(1)} %collective-permute-done.2.ahead.refs_1_), channel_id=1, source_target_pairs={{0,1},{1,0},{2,3},{3,2},{4,5},{5,4},{6,7},{7,6},{8,9},{9,8},{10,11... | collective-permute-start | bytes 688136 | tf_op jit(solution)/shard_map/ppermute | solution.py:40
  52.5 5.8 %collective-permute-done.8.refs_2_ = f32[64,896]{1,0:T(8,128)S(1)} collective-permute-done((f32[64,896]{1,0:T(8,128)S(1)}, f32[64,896]{1,0:T(8,128)S(1)}, u32[]{:S(2)}, u32[]{:S(2)}) %collective-permute-start.8) | collective-permute-done | bytes 229408 | tf_op jit(solution)/shard_map/ppermute | solution.py:36
  58.3 1.9 %collective-permute-start.5 = (f32[64,896]{1,0:T(8,128)S(1)}, f32[64,896]{1,0:T(8,128)S(1)}, u32[]{:S(2)}, u32[]{:S(2)}) collective-permute-start(f32[64,896]{1,0:T(8,128)S(1)} %get-tuple-element.17.refs_2_), channel_id=1, source_target_pairs={{0,1},{1,0},{2,3},{3,2},{4,5},{5,4},{6,7},{7,6},{8,9},{9,8},{10,11... | collective-permute-start | bytes 688136 | tf_op jit(solution)/shard_map/ppermute | solution.py:40
  60.2 0.6 collective-permute-done.7.refs_1_
  60.8 0.0 collective-permute-done.6.refs_0_
  60.8 0.1 shard_map.61.refs_3_
  60.9 0.0 collective-permute-done.1.refs_0_
  60.9 0.0 collective-permute-done.3.refs_1_
  60.9 0.8 collective-permute-done.5.refs_2_
  61.7 0.0 all-to-all-done.1.pieces
  61.7 2.0 %collective-permute-start.9 = (f32[320,896]{1,0:T(8,128)S(1)}, f32[320,896]{1,0:T(8,128)S(1)}, u32[]{:S(2)}, u32[]{:S(2)}) collective-permute-start(f32[320,896]{1,0:T(8,128)S(1)} %shard_map.61.refs_3_), channel_id=1, source_target_pairs={{0,1},{1,0},{2,3},{3,2},{4,5},{5,4},{6,7},{7,6},{8,9},{9,8},{10,11... | collective-permute-start | bytes 3440648 | tf_op jit(solution)/shard_map/ppermute | solution.py:40
  63.7 2.7 %shard_map.64 = (f32[192,896]{1,0:T(8,128)S(1)}, bf16[384,512]{1,0:T(8,128)(2,1)S(1)}, bf16[512,896]{1,0:T(8,128)(2,1)S(1)}, bf16[512,896]{1,0:T(8,128)(2,1)S(1)}) custom-call(f32[16,96,128]{2,1,0:T(8,128)} %all-to-all-done.1.pieces, f32[64,896]{1,0:T(8,128)S(1)} %shard_map.59.pair.refs_0_, f32[64,896]{1,0:T(8,128)S(1)} %collective-permute-done.2.ahead.refs_1_, ...), custom_call_target="tpu_custom_call" | custom-call | tf_op jit(solution)/shard_map/pallas_call | solution.py:297
  66.4 0.0 collective-permute-done.9.refs_3_
  66.4 2.0 %shard_map.65 = (f32[1,192,896]{2,1,0:T(8,128)}, f32[1344,128]{1,0:T(8,128)S(1)}, bf16[512,896]{1,0:T(8,128)(2,1)S(1)}, bf16[512,896]{1,0:T(8,128)(2,1)S(1)}) custom-call(f32[192,896]{1,0:T(8,128)S(1)} %get-tuple-element.21.partial, bf16[384,512]{1,0:T(8,128)(2,1)S(1)} %get-tuple-element.22.both, f32[64,896]{1,0:T(8,128)S(1)} %collective-permute-done.1.refs_0_, ...), custom_call_target="tpu_custom_call" | custom-call | tf_op jit(solution)/shard_map/pallas_call | solution.py:313
  68.4 29.1 %all_to_all.15 = f32[32,42,1,128]{3,2,1,0:T(1,128)S(1)} all-to-all(f32[32,42,1,128]{3,2,1,0:T(1,128)S(1)} %bitcast.6), channel_id=1, replica_groups=mesh['leaf'=16,'prow'=8,'side'=2,'core'=2] {'prow','side','core'}, dimensions={0} | all-to-all | bytes 1376256 | tf_op jit(solution)/shard_map/all_to_all | solution.py:326
  97.5 2.1 %shard_map.66 = f32[28,1,896]{2,1,0:T(1,128)} custom-call(s32[1,8]{1,0:T(1,128)S(1)} %copy-done.1, f32[1344,128]{1,0:T(8,128)S(1)} %bitcast.5, bf16[512,896]{1,0:T(8,128)(2,1)S(1)} %get-tuple-element.28.own_high, bf16[512,896]{1,0:T(8,128)(2,1)S(1)} %get-tuple-element.29.own_low, bf16[512,896]{1,0:T(8,128)(2,1)S(1)} %get-tuple-element.30.other_high, ...), custom_call_target="tpu_custom_call" | custom-call | tf_op jit(solution)/shard_map/pallas_call | solution.py:329
  (7 shorter events, 0.0 us)
Async XLA Ops:
  0.6 17.0 %copy-start.2 = (f32[1,32,896]{2,1,0:T(8,128)S(1)}, f32[1,32,896]{2,1,0:T(8,128)}, u32[]{:S(2)}) copy-start(f32[1,32,896]{2,1,0:T(8,128)} %param.6) | copy-start | bytes 344068
  0.6 17.0 %collective-permute-start = (f32[32,896]{1,0:T(8,128)}, f32[32,896]{1,0:T(8,128)S(1)}, u32[]{:S(2)}, u32[]{:S(2)}) collective-permute-start(f32[32,896]{1,0:T(8,128)} %bitcast.8), channel_id=1, source_target_pairs={{0,2},{2,0},{1,3},{3,1},{4,6},{6,4},{5,7},{7,5},{8,10},{10,8},{9,1... | collective-permute-start | bytes 344072 | tf_op jit(solution)/shard_map/ppermute | solution.py:44
  5.8 22.2 %all-to-all-start = ((f32[16,40,128]{2,1,0:T(8,128)}), f32[16,40,128]{2,1,0:T(8,128)}, u32[]{:S(2)}, u32[]{:S(2)}) async-start(f32[16,40,128]{2,1,0:T(8,128)} %shard_map.62), calls=%async_computation | async-start | bytes 655360 | tf_op jit(solution)/shard_map/all_to_all | solution.py:272
  17.7 19.0 %collective-permute-start.4 = (f32[64,896]{1,0:T(8,128)S(1)}, f32[64,896]{1,0:T(8,128)S(1)}, u32[]{:S(2)}, u32[]{:S(2)}) collective-permute-start(f32[64,896]{1,0:T(8,128)S(1)} %shard_map.59.pair.refs_0_), channel_id=1, source_target_pairs={{0,8},{4,12},{8,16},{12,20},{16,24},{20,28},{24,0},{28,4},{1,9},{5... | collective-permute-start | bytes 688136 | tf_op jit(solution)/shard_map/ppermute | solution.py:36
  22.2 15.1 %collective-permute-start.2 = (f32[64,896]{1,0:T(8,128)S(1)}, f32[64,896]{1,0:T(8,128)S(1)}, u32[]{:S(2)}, u32[]{:S(2)}) collective-permute-start(f32[64,896]{1,0:T(8,128)S(1)} %shard_map.59.pair.refs_0_), channel_id=1, source_target_pairs={{0,24},{4,28},{8,0},{12,4},{16,8},{20,12},{24,16},{28,20},{1,25},{... | collective-permute-start | bytes 688136 | tf_op jit(solution)/shard_map/ppermute | solution.py:36
  30.8 30.9 %all-to-all-start.1 = ((f32[16,96,128]{2,1,0:T(8,128)}), f32[16,96,128]{2,1,0:T(8,128)}, u32[]{:S(2)}, u32[]{:S(2)}) async-start(f32[16,96,128]{2,1,0:T(8,128)} %shard_map.63), calls=%async_computation.1 | async-start | bytes 1572864 | tf_op jit(solution)/shard_map/all_to_all | solution.py:286
  37.4 23.4 %collective-permute-start.6 = (f32[192,896]{1,0:T(8,128)S(1)}, f32[192,896]{1,0:T(8,128)S(1)}, u32[]{:S(2)}, u32[]{:S(2)}) collective-permute-start(f32[192,896]{1,0:T(8,128)S(1)} %get-tuple-element.18), channel_id=1, source_target_pairs={{0,28},{4,0},{8,4},{12,8},{16,12},{20,16},{24,20},{28,24},{1,29},{... | collective-permute-start | bytes 2064392 | tf_op jit(solution)/shard_map/ppermute | solution.py:36
  41.7 16.6 %collective-permute-start.8 = (f32[64,896]{1,0:T(8,128)S(1)}, f32[64,896]{1,0:T(8,128)S(1)}, u32[]{:S(2)}, u32[]{:S(2)}) collective-permute-start(f32[64,896]{1,0:T(8,128)S(1)} %get-tuple-element.17.refs_2_), channel_id=1, source_target_pairs={{0,8},{4,12},{8,16},{12,20},{16,24},{20,28},{24,0},{28,4},{1,9},{5... | collective-permute-start | bytes 688136 | tf_op jit(solution)/shard_map/ppermute | solution.py:36
  44.3 16.5 %collective-permute-start.7 = (f32[64,896]{1,0:T(8,128)S(1)}, f32[64,896]{1,0:T(8,128)S(1)}, u32[]{:S(2)}, u32[]{:S(2)}) collective-permute-start(f32[64,896]{1,0:T(8,128)S(1)} %get-tuple-element.17.refs_2_), channel_id=1, source_target_pairs={{0,4},{4,8},{8,12},{12,16},{16,20},{20,24},{24,28},{28,0},{1,5},{5... | collective-permute-start | bytes 688136 | tf_op jit(solution)/shard_map/ppermute | solution.py:36
  48.2 12.7 %collective-permute-start.1 = (f32[64,896]{1,0:T(8,128)S(1)}, f32[64,896]{1,0:T(8,128)S(1)}, u32[]{:S(2)}, u32[]{:S(2)}) collective-permute-start(f32[64,896]{1,0:T(8,128)S(1)} %shard_map.59.pair.refs_0_), channel_id=1, source_target_pairs={{0,1},{1,0},{2,3},{3,2},{4,5},{5,4},{6,7},{7,6},{8,9},{9,8},{10,11... | collective-permute-start | bytes 688136 | tf_op jit(solution)/shard_map/ppermute | solution.py:40
  50.1 10.8 %collective-permute-start.3 = (f32[64,896]{1,0:T(8,128)S(1)}, f32[64,896]{1,0:T(8,128)S(1)}, u32[]{:S(2)}, u32[]{:S(2)}) collective-permute-start(f32[64,896]{1,0:T(8,128)S(1)} %collective-permute-done.2.ahead.refs_1_), channel_id=1, source_target_pairs={{0,1},{1,0},{2,3},{3,2},{4,5},{5,4},{6,7},{7,6},{8,9},{9,8},{10,11... | collective-permute-start | bytes 688136 | tf_op jit(solution)/shard_map/ppermute | solution.py:40
  58.3 3.4 %collective-permute-start.5 = (f32[64,896]{1,0:T(8,128)S(1)}, f32[64,896]{1,0:T(8,128)S(1)}, u32[]{:S(2)}, u32[]{:S(2)}) collective-permute-start(f32[64,896]{1,0:T(8,128)S(1)} %get-tuple-element.17.refs_2_), channel_id=1, source_target_pairs={{0,1},{1,0},{2,3},{3,2},{4,5},{5,4},{6,7},{7,6},{8,9},{9,8},{10,11... | collective-permute-start | bytes 688136 | tf_op jit(solution)/shard_map/ppermute | solution.py:40
  61.7 4.7 %collective-permute-start.9 = (f32[320,896]{1,0:T(8,128)S(1)}, f32[320,896]{1,0:T(8,128)S(1)}, u32[]{:S(2)}, u32[]{:S(2)}) collective-permute-start(f32[320,896]{1,0:T(8,128)S(1)} %shard_map.61.refs_3_), channel_id=1, source_target_pairs={{0,1},{1,0},{2,3},{3,2},{4,5},{5,4},{6,7},{7,6},{8,9},{9,8},{10,11... | collective-permute-start | bytes 3440648 | tf_op jit(solution)/shard_map/ppermute | solution.py:40
  68.4 29.1 %copy-start = (f32[1,28,896]{2,0,1:T(1,128)S(1)}, f32[1,28,896]{2,0,1:T(1,128)}, u32[]{:S(2)}) copy-start(f32[1,28,896]{2,0,1:T(1,128)} %param.7) | copy-start | bytes 301060
  68.4 29.1 %copy-start.1 = (s32[1,8]{1,0:T(1,128)S(1)}, s32[1,8]{1,0:T(1,128)}, u32[]{:S(2)}) copy-start(s32[1,8]{1,0:T(1,128)} %pattern.3) | copy-start | bytes 100

commit v8 on v7

--- a/solution.py
+++ b/solution.py
@@ -146,7 +146,7 @@
     side = lax.axis_index("side")
     place = lax.axis_index("prow")
     for index, step in enumerate(STEPS):
-        source, group = (sources[index], 0) if index < 3 else (sources[3], index - 3)
+        source, group = (sources[index], 0) if index < 2 else (sources[2], index - 2)
         block = lax.rem(place + step + NP, NP)
         for part, at_side in ((0, side), (1, 1 - side)):
             row = group * 64 + part * LROWS
@@ -169,8 +169,8 @@
 
 
 def own_kernel(pieces, *refs):
-    sources = refs[:4]
-    partial, other_both, lower_high, lower_low, panel, own_both = refs[4:]
+    sources = refs[:3]
+    partial, other_both, lower_high, lower_low, panel, own_both = refs[3:]
     for leaf in range(N_LEAF):
         for block in range(NP):
             panel[leaf * CHUNK:(leaf + 1) * CHUNK, block * BLK:(block + 1) * BLK] = pieces[
@@ -188,8 +188,8 @@
 
 
 def cross_kernel(partial, both, *refs):
-    sources = refs[:4]
-    cross, out, lower_high, lower_low, product = refs[4:]
+    sources = refs[:3]
+    cross, out, lower_high, lower_low, product = refs[3:]
     core = lax.axis_index("core")
     order_rows(sources, lower_high, lower_low)
     value = partial[...] + multiply(both, lower_high, lower_low)
@@ -286,9 +286,9 @@
     chosen = lax.all_to_all(chosen, "leaf", 0, 0, tiled=True)
     near, rear = call(near_kernel, (192, 64), 2000, pair, ahead, behind)
     (far,) = call(
-        join_kernel, (320,), 0, from_row(near, 1), from_row(rear, -1), from_row(rear, -2)
+        join_kernel, (384,), 0, rear, from_row(near, 1), from_row(rear, -1), from_row(rear, -2)
     )
-    near_parts = [pair, ahead, rear]
+    near_parts = [pair, ahead]
     near_other = [swap_core(part) for part in near_parts]
     near_other, far, chosen = lax.optimization_barrier((near_other, far, chosen))
     far_other = swap_core(far)
@@ -302,7 +302,7 @@
             lower_shape,
             lower_shape,
         ),
-        in_specs=in_vmem(5),
+        in_specs=in_vmem(4),
         out_specs=tuple(in_vmem(4)),
         scratch_shapes=[
             pltpu.VMEM((ROWS, NP * BLK), jnp.float32),
@@ -318,7 +318,7 @@
             lower_shape,
             lower_shape,
         ),
-        in_specs=in_vmem(6),
+        in_specs=in_vmem(5),
         out_specs=tuple(in_vmem(4)),
         scratch_shapes=[pltpu.VMEM((ROWS, S1), jnp.float32)],
         compiler_params=params,

time: 100 us -> 99.8 us (level)
  starting transfers between devices: 48.3 us -> 47.1 us
    ppermute x4 -> x3, starting transfers between devices: 8.27 us -> 6.25 us  [swap_core(): return lax.ppermute(value, 'core', [(0, 1), (1, 0)])]
    ppermute x5, waiting for transfers between devices: 6.94 us -> 8.83 us  [from_row(): lax.ppermute(value, 'prow', [(at, (at - distance) % NP) for at in range(N...]
  transfers between devices with their start and end apart: 12 -> 11, of which waited for: 5 -> 5; matrix products, arithmetic and copies ran while one was open for 0% -> 0% of each run, Pallas kernels for 7% -> 7%
where the time goes in v8:
time: 99.8 us; the launch traced here: 99.1 us
  starting transfers between devices  47.1 us (47%)
  blocking collectives  28.4 us (28%)
  Pallas kernels  11.4 us (11%)
  waiting for transfers between devices  10.6 us (11%)
    all_to_all x1, blocking collectives, shards(): lax.all_to_all(pieces.reshape(N_GRID, PIECE3, 1, BLK), GRID, 0, 0, tiled=...  28.4 us
    ppermute x5, starting transfers between devices, from_row(): lax.ppermute(value, 'prow', [(at, (at - distance) % NP) for at in range(N...  18.9 us
    all_to_all x1, starting transfers between devices, shards(): spread = lax.all_to_all(spread, 'leaf', 0, 0, tiled=True)  11.8 us
    ppermute x5, waiting for transfers between devices, from_row(): lax.ppermute(value, 'prow', [(at, (at - distance) % NP) for at in range(N...  8.83 us
    all_to_all x1, starting transfers between devices, shards(): chosen = lax.all_to_all(chosen, 'leaf', 0, 0, tiled=True)  6.81 us
    ppermute x3, starting transfers between devices, swap_core(): return lax.ppermute(value, 'core', [(0, 1), (1, 0)])  6.25 us
    ppermute x1, starting transfers between devices, swap_side(): return lax.ppermute(value, 'side', [(0, 1), (1, 0)])  3.32 us
    pallas_call x1, Pallas kernels, shards(): pl.pallas_call(select_kernel, out_shape=jax.ShapeDtypeStruct((N_LEAF, PIE...  2.74 us
  transfers between devices with their start and end apart: 11, of which 5 were waited for; matrix products, arithmetic and copies ran while one was open for 0% of the time, Pallas kernels for 7%

profile of v8, /device:TPU:6, one launch (start us, length us, event | category | flops | bytes accessed | tf_op | source)
XLA Modules:
  0.0 99.1 jit_solution(5025877232565159725)
XLA Ops:
  0.6 3.3 %collective-permute-start = (f32[32,896]{1,0:T(8,128)}, f32[32,896]{1,0:T(8,128)S(1)}, u32[]{:S(2)}, u32[]{:S(2)}) collective-permute-start(f32[32,896]{1,0:T(8,128)} %bitcast.8), channel_id=1, source_target_pairs={{0,2},{2,0},{1,3},{3,1},{4,6},{6,4},{5,7},{7,5},{8,10},{10,8},{9,1... | collective-permute-start | bytes 344072 | tf_op jit(solution)/shard_map/ppermute | solution.py:44
  4.0 1.7 %shard_map.62 = f32[16,40,128]{2,1,0:T(8,128)} custom-call(f32[192,384]{1,0:T(8,128)} %ancestor.1, s32[1,8]{1,0:T(1,128)} %pattern.3), custom_call_target="tpu_custom_call" | custom-call | tf_op jit(solution)/shard_map/pallas_call | solution.py:250
  5.7 11.8 %all-to-all-start = ((f32[16,40,128]{2,1,0:T(8,128)}), f32[16,40,128]{2,1,0:T(8,128)}, u32[]{:S(2)}, u32[]{:S(2)}) async-start(f32[16,40,128]{2,1,0:T(8,128)} %shard_map.62), calls=%async_computation | async-start | bytes 655360 | tf_op jit(solution)/shard_map/all_to_all | solution.py:272
  17.5 0.0 collective-permute-done.across
  17.5 0.0 copy-start.2
  17.5 0.9 copy-done.2
  18.4 4.5 %collective-permute-start.4 = (f32[64,896]{1,0:T(8,128)S(1)}, f32[64,896]{1,0:T(8,128)S(1)}, u32[]{:S(2)}, u32[]{:S(2)}) collective-permute-start(f32[64,896]{1,0:T(8,128)S(1)} %shard_map.59.pair.refs_0_), channel_id=1, source_target_pairs={{0,8},{4,12},{8,16},{12,20},{16,24},{20,28},{24,0},{28,4},{1,9},{5... | collective-permute-start | bytes 688136 | tf_op jit(solution)/shard_map/ppermute | solution.py:36
  22.9 3.6 %collective-permute-start.2 = (f32[64,896]{1,0:T(8,128)S(1)}, f32[64,896]{1,0:T(8,128)S(1)}, u32[]{:S(2)}, u32[]{:S(2)}) collective-permute-start(f32[64,896]{1,0:T(8,128)S(1)} %shard_map.59.pair.refs_0_), channel_id=1, source_target_pairs={{0,24},{4,28},{8,0},{12,4},{16,8},{20,12},{24,16},{28,20},{1,25},{... | collective-permute-start | bytes 688136 | tf_op jit(solution)/shard_map/ppermute | solution.py:36
  26.5 1.3 %all-to-all-done.pieces = f32[16,40,128]{2,1,0:T(8,128)} async-done(((f32[16,40,128]{2,1,0:T(8,128)}), f32[16,40,128]{2,1,0:T(8,128)}, u32[]{:S(2)}, u32[]{:S(2)}) %all-to-all-start) | async-done | bytes 327712 | tf_op jit(solution)/shard_map/all_to_all | solution.py:272
  27.9 2.7 %shard_map.63 = f32[16,96,128]{2,1,0:T(8,128)} custom-call(f32[16,40,128]{2,1,0:T(8,128)} %all-to-all-done.pieces), custom_call_target="tpu_custom_call" | custom-call | tf_op jit(solution)/shard_map/pallas_call | solution.py:273
  30.6 6.8 %all-to-all-start.1 = ((f32[16,96,128]{2,1,0:T(8,128)}), f32[16,96,128]{2,1,0:T(8,128)}, u32[]{:S(2)}, u32[]{:S(2)}) async-start(f32[16,96,128]{2,1,0:T(8,128)} %shard_map.63), calls=%async_computation.1 | async-start | bytes 1572864 | tf_op jit(solution)/shard_map/all_to_all | solution.py:286
  37.4 0.0 collective-permute-done.4.behind
  37.4 0.6 collective-permute-done.2.ahead.refs_1_
  38.0 0.1 shard_map.60
  38.1 3.5 %collective-permute-start.5 = (f32[192,896]{1,0:T(8,128)S(1)}, f32[192,896]{1,0:T(8,128)S(1)}, u32[]{:S(2)}, u32[]{:S(2)}) collective-permute-start(f32[192,896]{1,0:T(8,128)S(1)} %get-tuple-element.17), channel_id=1, source_target_pairs={{0,28},{4,0},{8,4},{12,8},{16,12},{20,16},{24,20},{28,24},{1,29},{... | collective-permute-start | bytes 2064392 | tf_op jit(solution)/shard_map/ppermute | solution.py:36
  41.6 3.4 %collective-permute-start.7 = (f32[64,896]{1,0:T(8,128)S(1)}, f32[64,896]{1,0:T(8,128)S(1)}, u32[]{:S(2)}, u32[]{:S(2)}) collective-permute-start(f32[64,896]{1,0:T(8,128)S(1)} %get-tuple-element.16.refs_0_), channel_id=1, source_target_pairs={{0,8},{4,12},{8,16},{12,20},{16,24},{20,28},{24,0},{28,4},{1,9},{5... | collective-permute-start | bytes 688136 | tf_op jit(solution)/shard_map/ppermute | solution.py:36
  45.0 3.9 %collective-permute-start.6 = (f32[64,896]{1,0:T(8,128)S(1)}, f32[64,896]{1,0:T(8,128)S(1)}, u32[]{:S(2)}, u32[]{:S(2)}) collective-permute-start(f32[64,896]{1,0:T(8,128)S(1)} %get-tuple-element.16.refs_0_), channel_id=1, source_target_pairs={{0,4},{4,8},{8,12},{12,16},{16,20},{20,24},{24,28},{28,0},{1,5},{5... | collective-permute-start | bytes 688136 | tf_op jit(solution)/shard_map/ppermute | solution.py:36
  48.9 1.9 %collective-permute-start.1 = (f32[64,896]{1,0:T(8,128)S(1)}, f32[64,896]{1,0:T(8,128)S(1)}, u32[]{:S(2)}, u32[]{:S(2)}) collective-permute-start(f32[64,896]{1,0:T(8,128)S(1)} %shard_map.59.pair.refs_0_), channel_id=1, source_target_pairs={{0,1},{1,0},{2,3},{3,2},{4,5},{5,4},{6,7},{7,6},{8,9},{9,8},{10,11... | collective-permute-start | bytes 688136 | tf_op jit(solution)/shard_map/ppermute | solution.py:40
  50.9 2.4 %collective-permute-start.3 = (f32[64,896]{1,0:T(8,128)S(1)}, f32[64,896]{1,0:T(8,128)S(1)}, u32[]{:S(2)}, u32[]{:S(2)}) collective-permute-start(f32[64,896]{1,0:T(8,128)S(1)} %collective-permute-done.2.ahead.refs_1_), channel_id=1, source_target_pairs={{0,1},{1,0},{2,3},{3,2},{4,5},{5,4},{6,7},{7,6},{8,9},{9,8},{10,11... | collective-permute-start | bytes 688136 | tf_op jit(solution)/shard_map/ppermute | solution.py:40
  53.3 4.7 %collective-permute-done.7.refs_3_ = f32[64,896]{1,0:T(8,128)S(1)} collective-permute-done((f32[64,896]{1,0:T(8,128)S(1)}, f32[64,896]{1,0:T(8,128)S(1)}, u32[]{:S(2)}, u32[]{:S(2)}) %collective-permute-start.7) | collective-permute-done | bytes 229408 | tf_op jit(solution)/shard_map/ppermute | solution.py:36
  58.0 3.5 %collective-permute-done.6.refs_2_ = f32[64,896]{1,0:T(8,128)S(1)} collective-permute-done((f32[64,896]{1,0:T(8,128)S(1)}, f32[64,896]{1,0:T(8,128)S(1)}, u32[]{:S(2)}, u32[]{:S(2)}) %collective-permute-start.6) | collective-permute-done | bytes 229408 | tf_op jit(solution)/shard_map/ppermute | solution.py:36
  61.5 0.0 collective-permute-done.5.refs_1_
  61.5 0.1 shard_map.61.refs_2_
  61.6 0.0 collective-permute-done.1.refs_0_
  61.6 0.0 collective-permute-done.3.refs_1_
  61.6 0.0 all-to-all-done.1.pieces
  61.7 1.9 %collective-permute-start.8 = (f32[384,896]{1,0:T(8,128)S(1)}, f32[384,896]{1,0:T(8,128)S(1)}, u32[]{:S(2)}, u32[]{:S(2)}) collective-permute-start(f32[384,896]{1,0:T(8,128)S(1)} %shard_map.61.refs_2_), channel_id=1, source_target_pairs={{0,1},{1,0},{2,3},{3,2},{4,5},{5,4},{6,7},{7,6},{8,9},{9,8},{10,11... | collective-permute-start | bytes 4128776 | tf_op jit(solution)/shard_map/ppermute | solution.py:40
  63.6 2.7 %shard_map.64 = (f32[192,896]{1,0:T(8,128)S(1)}, bf16[384,512]{1,0:T(8,128)(2,1)S(1)}, bf16[512,896]{1,0:T(8,128)(2,1)S(1)}, bf16[512,896]{1,0:T(8,128)(2,1)S(1)}) custom-call(f32[16,96,128]{2,1,0:T(8,128)} %all-to-all-done.1.pieces, f32[64,896]{1,0:T(8,128)S(1)} %shard_map.59.pair.refs_0_, f32[64,896]{1,0:T(8,128)S(1)} %collective-permute-done.2.ahead.refs_1_, ...), custom_call_target="tpu_custom_call" | custom-call | tf_op jit(solution)/shard_map/pallas_call | solution.py:297
  66.3 0.4 collective-permute-done.8.refs_2_
  66.7 2.0 %shard_map.65 = (f32[1,192,896]{2,1,0:T(8,128)}, f32[1344,128]{1,0:T(8,128)S(1)}, bf16[512,896]{1,0:T(8,128)(2,1)S(1)}, bf16[512,896]{1,0:T(8,128)(2,1)S(1)}) custom-call(f32[192,896]{1,0:T(8,128)S(1)} %get-tuple-element.20.partial, bf16[384,512]{1,0:T(8,128)(2,1)S(1)} %get-tuple-element.21.both, f32[64,896]{1,0:T(8,128)S(1)} %collective-permute-done.1.refs_0_, ...), custom_call_target="tpu_custom_call" | custom-call | tf_op jit(solution)/shard_map/pallas_call | solution.py:313
  68.6 28.4 %all_to_all.15 = f32[32,42,1,128]{3,2,1,0:T(1,128)S(1)} all-to-all(f32[32,42,1,128]{3,2,1,0:T(1,128)S(1)} %bitcast.6), channel_id=1, replica_groups=mesh['leaf'=16,'prow'=8,'side'=2,'core'=2] {'prow','side','core'}, dimensions={0} | all-to-all | bytes 1376256 | tf_op jit(solution)/shard_map/all_to_all | solution.py:326
  97.0 2.1 %shard_map.66 = f32[28,1,896]{2,1,0:T(1,128)} custom-call(s32[1,8]{1,0:T(1,128)S(1)} %copy-done.1, f32[1344,128]{1,0:T(8,128)S(1)} %bitcast.5, bf16[512,896]{1,0:T(8,128)(2,1)S(1)} %get-tuple-element.26.own_high, bf16[512,896]{1,0:T(8,128)(2,1)S(1)} %get-tuple-element.27.own_low, bf16[512,896]{1,0:T(8,128)(2,1)S(1)} %get-tuple-element.28.other_high, ...), custom_call_target="tpu_custom_call" | custom-call | tf_op jit(solution)/shard_map/pallas_call | solution.py:329
  (5 shorter events, 0.0 us)
Async XLA Ops:
  0.6 16.9 %collective-permute-start = (f32[32,896]{1,0:T(8,128)}, f32[32,896]{1,0:T(8,128)S(1)}, u32[]{:S(2)}, u32[]{:S(2)}) collective-permute-start(f32[32,896]{1,0:T(8,128)} %bitcast.8), channel_id=1, source_target_pairs={{0,2},{2,0},{1,3},{3,1},{4,6},{6,4},{5,7},{7,5},{8,10},{10,8},{9,1... | collective-permute-start | bytes 344072 | tf_op jit(solution)/shard_map/ppermute | solution.py:44
  5.7 22.2 %all-to-all-start = ((f32[16,40,128]{2,1,0:T(8,128)}), f32[16,40,128]{2,1,0:T(8,128)}, u32[]{:S(2)}, u32[]{:S(2)}) async-start(f32[16,40,128]{2,1,0:T(8,128)} %shard_map.62), calls=%async_computation | async-start | bytes 655360 | tf_op jit(solution)/shard_map/all_to_all | solution.py:272
  17.5 0.9 copy-start.2
  18.4 19.0 %collective-permute-start.4 = (f32[64,896]{1,0:T(8,128)S(1)}, f32[64,896]{1,0:T(8,128)S(1)}, u32[]{:S(2)}, u32[]{:S(2)}) collective-permute-start(f32[64,896]{1,0:T(8,128)S(1)} %shard_map.59.pair.refs_0_), channel_id=1, source_target_pairs={{0,8},{4,12},{8,16},{12,20},{16,24},{20,28},{24,0},{28,4},{1,9},{5... | collective-permute-start | bytes 688136 | tf_op jit(solution)/shard_map/ppermute | solution.py:36
  22.9 15.1 %collective-permute-start.2 = (f32[64,896]{1,0:T(8,128)S(1)}, f32[64,896]{1,0:T(8,128)S(1)}, u32[]{:S(2)}, u32[]{:S(2)}) collective-permute-start(f32[64,896]{1,0:T(8,128)S(1)} %shard_map.59.pair.refs_0_), channel_id=1, source_target_pairs={{0,24},{4,28},{8,0},{12,4},{16,8},{20,12},{24,16},{28,20},{1,25},{... | collective-permute-start | bytes 688136 | tf_op jit(solution)/shard_map/ppermute | solution.py:36
  30.6 31.0 %all-to-all-start.1 = ((f32[16,96,128]{2,1,0:T(8,128)}), f32[16,96,128]{2,1,0:T(8,128)}, u32[]{:S(2)}, u32[]{:S(2)}) async-start(f32[16,96,128]{2,1,0:T(8,128)} %shard_map.63), calls=%async_computation.1 | async-start | bytes 1572864 | tf_op jit(solution)/shard_map/all_to_all | solution.py:286
  38.1 23.4 %collective-permute-start.5 = (f32[192,896]{1,0:T(8,128)S(1)}, f32[192,896]{1,0:T(8,128)S(1)}, u32[]{:S(2)}, u32[]{:S(2)}) collective-permute-start(f32[192,896]{1,0:T(8,128)S(1)} %get-tuple-element.17), channel_id=1, source_target_pairs={{0,28},{4,0},{8,4},{12,8},{16,12},{20,16},{24,20},{28,24},{1,29},{... | collective-permute-start | bytes 2064392 | tf_op jit(solution)/shard_map/ppermute | solution.py:36
  41.6 16.4 %collective-permute-start.7 = (f32[64,896]{1,0:T(8,128)S(1)}, f32[64,896]{1,0:T(8,128)S(1)}, u32[]{:S(2)}, u32[]{:S(2)}) collective-permute-start(f32[64,896]{1,0:T(8,128)S(1)} %get-tuple-element.16.refs_0_), channel_id=1, source_target_pairs={{0,8},{4,12},{8,16},{12,20},{16,24},{20,28},{24,0},{28,4},{1,9},{5... | collective-permute-start | bytes 688136 | tf_op jit(solution)/shard_map/ppermute | solution.py:36
  45.0 16.5 %collective-permute-start.6 = (f32[64,896]{1,0:T(8,128)S(1)}, f32[64,896]{1,0:T(8,128)S(1)}, u32[]{:S(2)}, u32[]{:S(2)}) collective-permute-start(f32[64,896]{1,0:T(8,128)S(1)} %get-tuple-element.16.refs_0_), channel_id=1, source_target_pairs={{0,4},{4,8},{8,12},{12,16},{16,20},{20,24},{24,28},{28,0},{1,5},{5... | collective-permute-start | bytes 688136 | tf_op jit(solution)/shard_map/ppermute | solution.py:36
  48.9 12.7 %collective-permute-start.1 = (f32[64,896]{1,0:T(8,128)S(1)}, f32[64,896]{1,0:T(8,128)S(1)}, u32[]{:S(2)}, u32[]{:S(2)}) collective-permute-start(f32[64,896]{1,0:T(8,128)S(1)} %shard_map.59.pair.refs_0_), channel_id=1, source_target_pairs={{0,1},{1,0},{2,3},{3,2},{4,5},{5,4},{6,7},{7,6},{8,9},{9,8},{10,11... | collective-permute-start | bytes 688136 | tf_op jit(solution)/shard_map/ppermute | solution.py:40
  50.9 10.8 %collective-permute-start.3 = (f32[64,896]{1,0:T(8,128)S(1)}, f32[64,896]{1,0:T(8,128)S(1)}, u32[]{:S(2)}, u32[]{:S(2)}) collective-permute-start(f32[64,896]{1,0:T(8,128)S(1)} %collective-permute-done.2.ahead.refs_1_), channel_id=1, source_target_pairs={{0,1},{1,0},{2,3},{3,2},{4,5},{5,4},{6,7},{7,6},{8,9},{9,8},{10,11... | collective-permute-start | bytes 688136 | tf_op jit(solution)/shard_map/ppermute | solution.py:40
  61.7 5.0 %collective-permute-start.8 = (f32[384,896]{1,0:T(8,128)S(1)}, f32[384,896]{1,0:T(8,128)S(1)}, u32[]{:S(2)}, u32[]{:S(2)}) collective-permute-start(f32[384,896]{1,0:T(8,128)S(1)} %shard_map.61.refs_2_), channel_id=1, source_target_pairs={{0,1},{1,0},{2,3},{3,2},{4,5},{5,4},{6,7},{7,6},{8,9},{9,8},{10,11... | collective-permute-start | bytes 4128776 | tf_op jit(solution)/shard_map/ppermute | solution.py:40
  68.6 28.4 %copy-start = (f32[1,28,896]{2,0,1:T(1,128)S(1)}, f32[1,28,896]{2,0,1:T(1,128)}, u32[]{:S(2)}) copy-start(f32[1,28,896]{2,0,1:T(1,128)} %param.7) | copy-start | bytes 301060
  68.6 28.4 %copy-start.1 = (s32[1,8]{1,0:T(1,128)S(1)}, s32[1,8]{1,0:T(1,128)}, u32[]{:S(2)}) copy-start(s32[1,8]{1,0:T(1,128)} %pattern.3) | copy-start | bytes 100
